TPU v7x, 512 devices: a whole 4x8x8 slice. The times are simulated.
512 devices in a mesh: doc: 32 (over y, z_lo, core), cent: 16 (over z_hi, x).
Axes of the slice: x: 4, y: 8, z: 8 (z_hi: 4, z_lo: 2; z = z_hi * 2 + z_lo), core: 2. Of those that a mesh axis runs over, the one named last changes fastest.
Arguments:
- docs: bfloat16 [32768, 256], P('doc'), may hold values from -24 to 24
- centroids: bfloat16 [32768, 256], P('cent'), may hold values from -7 to 7
- shard_ids: int32 [32768], P('doc'), may hold values from 0 to 63
- shard_mass: int32 [64], replicated, may hold values from 1 to 8
Outputs:
- new_centroids: bfloat16 [32768, 256], P('cent')
- row_potential: float32 [32768], P('doc')
All inputs are finite; a program needn't handle non-finite values.
Results may differ from a plain program's by a relative error of at most 0.0033.
Values may be sent and summed in bfloat16 or wider, within the bound.
No kernel may reach another device: no remote copies, remote signals or barrier semaphores. Data moves between devices by JAX's collectives and lax.ppermute only.
A program may use at most 64 MiB of HBM per device.

v0:
```python
import jax
import jax.numpy as jnp
from jax import lax
from jax.sharding import PartitionSpec as P

D = 256
K = 32768
PASSES = 3


def row_lse(tile):
    top = lax.pmax(jnp.max(tile, axis=1), "cent")
    total = lax.psum(jnp.sum(jnp.exp(tile - top[:, None]), axis=1), "cent")
    return top + jnp.log(total)


def col_lse(tile):
    top = lax.pmax(jnp.max(tile, axis=0), "doc")
    total = lax.psum(jnp.sum(jnp.exp(tile - top[None, :]), axis=0), "doc")
    return top + jnp.log(total)


def per_device(docs, centroids, shard_ids, shard_mass):
    rows = docs.shape[0]
    logits = lax.dot_general(
        docs, centroids, (((1,), (1,)), ((), ())), preferred_element_type=jnp.float32
    ) * (4.0 * D ** (-0.5))
    table = (shard_ids[:, None] == jnp.arange(shard_mass.shape[0])[None, :]).astype(jnp.float32)
    weights = jnp.sum(table * shard_mass.astype(jnp.float32)[None, :], axis=1) / 8.0
    log_mass = jnp.log(weights)
    log_target = jnp.log(jnp.float32(0.5 * rows * lax.axis_size("doc") / K))
    col_pot = jnp.zeros((centroids.shape[0],), jnp.float32)
    row_pot = log_mass - row_lse(logits)
    for turn in range(PASSES):
        col_pot = log_target - col_lse(logits + row_pot[:, None])
        row_pot = log_mass - row_lse(logits + col_pot[None, :])
    plan = jnp.exp(logits + row_pot[:, None] + col_pot[None, :])
    mass = jnp.sum(plan, axis=0)
    sums = lax.dot_general(
        plan.astype(jnp.bfloat16),
        docs,
        (((0,), (0,)), ((), ())),
        preferred_element_type=jnp.float32,
    )
    all_sums, all_mass = lax.psum((sums, mass), "doc")
    new_centroids = (all_sums / all_mass[:, None]).astype(jnp.bfloat16)
    return (new_centroids, row_pot)


def solution(mesh):
    placed = (P("doc", None), P("cent", None), P("doc"), P())
    return jax.shard_map(
        per_device,
        mesh=mesh,
        in_specs=placed,
        out_specs=(P("cent", None), P("doc")),
        check_vma=False,
    )
```

profile of v0, /device:TPU:1, one launch (start us, length us, event | category | flops | bytes accessed | tf_op | source)
XLA Modules:
  0.0 970.7 jit_solution(9862815443429184480)
XLA Ops:
  7.2 0.0 copy-start
  7.2 0.0 all-reduce.2.cloned.1.call-start
  7.2 0.7 convert_element_type.10
  8.0 0.4 copy-done
  8.4 0.0 copy-start.3
  8.4 5.6 fusion.6
  14.0 43.8 %pmax.49 = f32[1024]{0:T(1024)S(1)} all-reduce(f32[1024]{0:T(1024)S(1)} %get-tuple-element.2), channel_id=1, replica_groups=mesh['doc'=32,'cent'=16] {'cent'}, use_global_device_ids=true, to_apply=%region_2.0 | all-reduce | flops 1024 | bytes 8192 | tf_op jit(solution)/shard_map/pmax | solution.py:12
  57.8 4.6 exponential_reduce_fusion.6
  62.4 32.1 %psum.63 = f32[1024]{0:T(1024)S(1)} all-reduce(f32[1024]{0:T(1024)S(1)} %exponential_reduce_fusion.6), channel_id=1, replica_groups=mesh['doc'=32,'cent'=16] {'cent'}, use_global_device_ids=true, to_apply=%region_4.0 | all-reduce | flops 1024 | bytes 8192 | tf_op jit(solution)/shard_map/psum | solution.py:13
  94.6 0.0 copy-done.3
  94.6 0.1 select_reduce_fusion
  94.7 4.0 add_reduce_fusion.5
  98.7 68.9 %pmax.50 = f32[2048]{0:T(1024)S(1)} all-reduce(f32[2048]{0:T(1024)S(1)} %add_reduce_fusion.5), channel_id=1, replica_groups=mesh['doc'=32,'cent'=16] {'doc'}, use_global_device_ids=true, to_apply=%region_6.0 | all-reduce | flops 2048 | bytes 16384 | tf_op jit(solution)/shard_map/pmax | solution.py:18
  167.6 4.3 exponential_reduce_fusion.5
  171.9 53.5 %psum.64 = f32[2048]{0:T(1024)S(1)} all-reduce(f32[2048]{0:T(1024)S(1)} %exponential_reduce_fusion.5), channel_id=1, replica_groups=mesh['doc'=32,'cent'=16] {'doc'}, use_global_device_ids=true, to_apply=%region_8.0 | all-reduce | flops 2048 | bytes 16384 | tf_op jit(solution)/shard_map/psum | solution.py:19
  225.4 4.0 add_reduce_fusion.4
  229.4 33.9 %pmax.51 = f32[1024]{0:T(1024)S(1)} all-reduce(f32[1024]{0:T(1024)S(1)} %add_reduce_fusion.4), channel_id=1, replica_groups=mesh['doc'=32,'cent'=16] {'cent'}, use_global_device_ids=true, to_apply=%region_10.0 | all-reduce | flops 1024 | bytes 8192 | tf_op jit(solution)/shard_map/pmax | solution.py:12
  263.3 4.4 exponential_reduce_fusion.4
  267.6 32.4 %psum.65 = f32[1024]{0:T(1024)S(1)} all-reduce(f32[1024]{0:T(1024)S(1)} %exponential_reduce_fusion.4), channel_id=1, replica_groups=mesh['doc'=32,'cent'=16] {'cent'}, use_global_device_ids=true, to_apply=%region_12.0 | all-reduce | flops 1024 | bytes 8192 | tf_op jit(solution)/shard_map/psum | solution.py:13
  300.1 4.0 add_reduce_fusion.3
  304.1 68.2 %pmax.52 = f32[2048]{0:T(1024)S(1)} all-reduce(f32[2048]{0:T(1024)S(1)} %add_reduce_fusion.3), channel_id=1, replica_groups=mesh['doc'=32,'cent'=16] {'doc'}, use_global_device_ids=true, to_apply=%region_14.0 | all-reduce | flops 2048 | bytes 16384 | tf_op jit(solution)/shard_map/pmax | solution.py:18
  372.3 4.3 exponential_reduce_fusion.3
  376.6 54.0 %psum.66 = f32[2048]{0:T(1024)S(1)} all-reduce(f32[2048]{0:T(1024)S(1)} %exponential_reduce_fusion.3), channel_id=1, replica_groups=mesh['doc'=32,'cent'=16] {'doc'}, use_global_device_ids=true, to_apply=%region_16.0 | all-reduce | flops 2048 | bytes 16384 | tf_op jit(solution)/shard_map/psum | solution.py:19
  430.6 4.0 add_reduce_fusion.2
  434.6 33.8 %pmax.53 = f32[1024]{0:T(1024)S(1)} all-reduce(f32[1024]{0:T(1024)S(1)} %add_reduce_fusion.2), channel_id=1, replica_groups=mesh['doc'=32,'cent'=16] {'cent'}, use_global_device_ids=true, to_apply=%region_18.0 | all-reduce | flops 1024 | bytes 8192 | tf_op jit(solution)/shard_map/pmax | solution.py:12
  468.5 4.4 exponential_reduce_fusion.2
  472.8 32.1 %psum.67 = f32[1024]{0:T(1024)S(1)} all-reduce(f32[1024]{0:T(1024)S(1)} %exponential_reduce_fusion.2), channel_id=1, replica_groups=mesh['doc'=32,'cent'=16] {'cent'}, use_global_device_ids=true, to_apply=%region_20.0 | all-reduce | flops 1024 | bytes 8192 | tf_op jit(solution)/shard_map/psum | solution.py:13
  505.0 4.0 add_reduce_fusion.1
  509.0 68.2 %pmax.54 = f32[2048]{0:T(1024)S(1)} all-reduce(f32[2048]{0:T(1024)S(1)} %add_reduce_fusion.1), channel_id=1, replica_groups=mesh['doc'=32,'cent'=16] {'doc'}, use_global_device_ids=true, to_apply=%region_22.0 | all-reduce | flops 2048 | bytes 16384 | tf_op jit(solution)/shard_map/pmax | solution.py:18
  577.2 4.3 exponential_reduce_fusion.1
  581.5 54.2 %psum.68 = f32[2048]{0:T(1024)S(1)} all-reduce(f32[2048]{0:T(1024)S(1)} %exponential_reduce_fusion.1), channel_id=1, replica_groups=mesh['doc'=32,'cent'=16] {'doc'}, use_global_device_ids=true, to_apply=%region_24.0 | all-reduce | flops 2048 | bytes 16384 | tf_op jit(solution)/shard_map/psum | solution.py:19
  635.7 0.0 copy-start.1
  635.7 4.1 add_reduce_fusion
  639.8 33.8 %pmax.55 = f32[1024]{0:T(1024)S(1)} all-reduce(f32[1024]{0:T(1024)S(1)} %add_reduce_fusion), channel_id=1, replica_groups=mesh['doc'=32,'cent'=16] {'cent'}, use_global_device_ids=true, to_apply=%region_26.0 | all-reduce | flops 1024 | bytes 8192 | tf_op jit(solution)/shard_map/pmax | solution.py:12
  673.6 4.4 exponential_reduce_fusion
  677.9 32.1 %psum.69 = f32[1024]{0:T(1024)S(1)} all-reduce(f32[1024]{0:T(1024)S(1)} %exponential_reduce_fusion), channel_id=1, replica_groups=mesh['doc'=32,'cent'=16] {'cent'}, use_global_device_ids=true, to_apply=%region_28.0 | all-reduce | flops 1024 | bytes 8192 | tf_op jit(solution)/shard_map/psum | solution.py:13
  710.1 0.0 copy-done.1
  710.1 0.0 copy-start.2
  710.1 6.5 fusion.2
  716.6 0.0 all-reduce.2.cloned.1.call-update
  716.6 0.0 copy-done.2
  716.6 4.3 fusion
  720.9 68.3 %psum.71 = f32[2048]{0:T(1024)S(1)} all-reduce(f32[2048]{0:T(1024)S(1)} %fusion), channel_id=1, replica_groups=mesh['doc'=32,'cent'=16] {'doc'}, use_global_device_ids=true, to_apply=%region_31.0 | all-reduce | flops 2048 | bytes 16384 | tf_op jit(solution)/shard_map/psum | solution.py:45
  789.2 171.7 %all-reduce.2.cloned.1.call-done = f32[2048,256]{1,0:T(8,128)} async-done(((f32[2048,256]{1,0:T(8,128)}), f32[2048,256]{1,0:T(8,128)}) %all-reduce.2.cloned.1.call-update) | async-done | bytes 2097168 | tf_op jit(solution)/shard_map/psum | solution.py:45
  960.9 2.9 divide_convert_fusion
  (7 shorter events, 0.1 us)
Async XLA Ops:
  7.2 1.2 copy-start
  7.2 953.8 %all-reduce.2.cloned.1.call-start = ((), (), s32[]{:S(2)}) async-start(), calls=%async_computation | async-start | bytes 4194304 | tf_op jit(solution)/shard_map/psum | solution.py:45
  8.4 86.1 %copy-start.3 = (s32[1024]{0:T(1024)S(1)}, s32[1024]{0:T(1024)}, u32[]{:S(2)}) copy-start(s32[1024]{0:T(1024)} %param.6) | copy-start | bytes 12292
  635.7 74.4 %copy-start.1 = (bf16[1024,256]{1,0:T(8,128)(2,1)S(1)}, bf16[1024,256]{1,0:T(8,128)(2,1)}, u32[]{:S(2)}) copy-start(bf16[1024,256]{1,0:T(8,128)(2,1)} %param.4) | copy-start | bytes 1572868
  710.1 6.5 copy-start.2
Sparse Core Ops, SparseCore 0:
  716.7 244.1 all-reduce.1
where the time goes:
time: 971 us
  blocking collectives  709 us (73%)
  waiting for transfers between devices  172 us (18%)
  other arithmetic  62.8 us (6%)
  between operations  14.2 us (1%)
  matrix products  12 us (1%)
    pmax x3, blocking collectives, col_lse(): top = lax.pmax(jnp.max(tile, axis=0), 'doc')  205 us
    psum x1, waiting for transfers between devices, per_device(): all_sums, all_mass = lax.psum((sums, mass), 'doc')  172 us
    psum x3, blocking collectives, col_lse(): total = lax.psum(jnp.sum(jnp.exp(tile - top[None, :]), axis=0), 'doc')  162 us
    pmax x4, blocking collectives, row_lse(): top = lax.pmax(jnp.max(tile, axis=1), 'cent')  145 us
    psum x4, blocking collectives, row_lse(): total = lax.psum(jnp.sum(jnp.exp(tile - top[:, None]), axis=1), 'cent')  129 us
    psum x1, blocking collectives, per_device(): all_sums, all_mass = lax.psum((sums, mass), 'doc')  68.3 us
  transfers between devices with their start and end apart: 1, of which 1 were waited for; matrix products, arithmetic and copies ran while one was open for 0% of the time, Pallas kernels for 0%

commit v1 on v0

v1 whole, which is shorter than its diff:
```python
import functools
import math

import jax
import jax.numpy as jnp
from jax import lax
from jax.experimental import pallas as pl
from jax.experimental.pallas import tpu as pltpu
from jax.sharding import Mesh
from jax.sharding import PartitionSpec as P

LOG2E = 1.4426950408889634
LN2 = 0.6931471805599453
LANES = 128
VMEM_LIMIT = 32 * 1024 * 1024
ROWS = ("zl", "zh", "x")
COLS = ("y", "core")
F32 = jnp.float32
BF16 = jnp.bfloat16


def call(kernel, out_shape, n_in, smem=(), scratch=(), flops=0, out_specs=None, in_specs=None):
    vmem = pl.BlockSpec(memory_space=pltpu.VMEM)
    if in_specs is None:
        in_specs = [pl.BlockSpec(memory_space=pltpu.SMEM) if i in smem else vmem for i in range(n_in)]
    if out_specs is None:
        out_specs = jax.tree.map(lambda _: vmem, out_shape)
    return pl.pallas_call(
        kernel,
        out_shape=out_shape,
        in_specs=in_specs,
        out_specs=out_specs,
        scratch_shapes=list(scratch),
        compiler_params=pltpu.CompilerParams(vmem_limit_bytes=VMEM_LIMIT),
        cost_estimate=pl.CostEstimate(flops=flops, bytes_accessed=1 << 20, transcendentals=0),
    )


def lane_iota():
    return lax.broadcasted_iota(jnp.int32, (LANES, LANES), 1)


def to_columns(dense):
    return jnp.concatenate([dense] * (LANES // dense.shape[0]), axis=0).T


def nt_dot(a, b):
    return lax.dot_general(a, b, (((1,), (1,)), ((), ())), preferred_element_type=F32)


def weights_of(ids, mass_ref):
    def step(s, total):
        return jnp.where(ids == s, mass_ref[s].astype(F32), total)

    return lax.fori_loop(0, mass_ref.shape[0], step, jnp.zeros(ids.shape, F32)) * 0.125


def first_rows(scale, peers, docs_ref, cents_ref, out_ref, s_ref):
    n_cent = cents_ref.shape[0]
    block = 64

    def group(g, _):
        docs = docs_ref[pl.ds(pl.multiple_of(g * 256, 256), 256), :]
        top = jnp.full((8, 256), -jnp.inf, F32)
        for q in range(n_cent // 256):
            s = nt_dot(cents_ref[q * 256 : (q + 1) * 256, :], docs)
            s_ref[q * 256 : (q + 1) * 256, :] = s
            top = jnp.maximum(top, jnp.max(s.reshape(32, 8, 256), axis=0))
        top = jnp.max(top, axis=0, keepdims=True) * scale

        def part(q, total):
            s = s_ref[pl.ds(pl.multiple_of(q * block, block), block), :]
            return total + jnp.sum(jnp.exp2(s * scale - top).reshape(block // 8, 8, 256), axis=0)

        total = lax.fori_loop(0, n_cent // block, part, jnp.zeros((8, 256), F32), unroll=8)
        lse = top + jnp.log2(jnp.sum(total, axis=0, keepdims=True))
        for h in range(2):
            row = lse[:, h * LANES : (h + 1) * LANES]
            out_ref[:, pl.ds(g * 2 + h, 1), :] = jnp.broadcast_to(row[None], (peers, 1, LANES))
        return 0

    lax.fori_loop(0, docs_ref.shape[0] // 256, group, 0)


def first_columns(
    scale, peers, zl_ref, mass_ref, parts_ref, ids_ref, other_ids_ref, docs_ref, other_ref, cents_ref,
    out_ref, tile_ref, top_ref, f_ref, w_ref, docs_all_ref,
):
    zl = zl_ref[0]
    n_doc, n_cent = docs_ref.shape[0], cents_ref.shape[0] // 2
    groups = 2 * n_doc // LANES
    docs_all_ref[pl.ds(pl.multiple_of(zl * n_doc, n_doc), n_doc), :] = docs_ref[...]
    docs_all_ref[pl.ds(pl.multiple_of((1 - zl) * n_doc, n_doc), n_doc), :] = other_ref[...]
    own = weights_of(ids_ref[...], mass_ref)
    other = weights_of(other_ids_ref[...], mass_ref)
    w_ref[0:8, :] = jnp.where(zl == 0, own, other)
    w_ref[8:16, :] = jnp.where(zl == 0, other, own)
    half = parts_ref.shape[0] // 2
    for z in range(2):
        parts = parts_ref[z * half : (z + 1) * half]
        top = jnp.max(parts, axis=0)
        lse = top + jnp.log2(jnp.sum(jnp.exp2(parts - top[None]), axis=0))
        f_ref[z * 8 : (z + 1) * 8, :] = jnp.log2(w_ref[z * 8 : (z + 1) * 8, :]) - lse
    base = pl.multiple_of(zl * n_cent, n_cent)

    for g in range(groups // 2):
        f = jnp.concatenate([f_ref[2 * g : 2 * g + 1, :], f_ref[2 * g + 1 : 2 * g + 2, :]], axis=1)
        docs = docs_all_ref[g * 256 : (g + 1) * 256, :]
        for q in range(n_cent // 256):
            cents = cents_ref[pl.ds(pl.multiple_of(base + q * 256, 256), 256), :]
            tile_ref[q * 256 : (q + 1) * 256, g * 256 : (g + 1) * 256] = nt_dot(cents, docs) * scale + f
    lane = lane_iota()
    tops = jnp.zeros((LANES, LANES), F32)
    lses = jnp.zeros((LANES, LANES), F32)
    for r in range(n_cent // LANES):
        rows = slice(r * LANES, (r + 1) * LANES)
        top = tile_ref[rows, 0:LANES]
        for g in range(1, groups):
            top = jnp.maximum(top, tile_ref[rows, g * LANES : (g + 1) * LANES])
        top = jnp.broadcast_to(jnp.max(top, axis=1, keepdims=True), (LANES, LANES))
        total = jnp.zeros((LANES, LANES), F32)
        for g in range(groups):
            e = jnp.exp2(tile_ref[rows, g * LANES : (g + 1) * LANES] - top)
            tile_ref[rows, g * LANES : (g + 1) * LANES] = e
            total = total + e
        tops = jnp.where(lane == r, top, tops)
        lses = jnp.where(lane == r, top + jnp.log2(jnp.sum(total, axis=1, keepdims=True)), lses)
    top_ref[...] = tops.T[0:8, :]
    out_ref[...] = jnp.broadcast_to(lses.T[0:8, :][None], (peers, 8, LANES))


def weigh_columns(c, tile_ref, out_ref):
    groups = tile_ref.shape[1] // LANES
    cols = to_columns(c)
    totals = [jnp.zeros((8, LANES), F32) for _ in range(groups)]
    for r in range(tile_ref.shape[0] // LANES):
        col = jnp.broadcast_to(cols[:, r : r + 1], (LANES, LANES))
        for g in range(groups):
            p = tile_ref[r * LANES : (r + 1) * LANES, g * LANES : (g + 1) * LANES] * col
            totals[g] = totals[g] + jnp.sum(p.reshape(LANES // 8, 8, LANES), axis=0)
    rows = jnp.concatenate([jnp.sum(t, axis=0, keepdims=True) for t in totals], axis=0)
    out_ref[...] = jnp.broadcast_to(rows[None], out_ref.shape).astype(out_ref.dtype)


def rows_after_first(log_target, parts_ref, top_ref, tile_ref, out_ref, c_ref):
    parts = parts_ref[...]
    top = jnp.max(parts, axis=0)
    lse = top + jnp.log2(jnp.sum(jnp.exp2(parts - top[None]), axis=0))
    c = jnp.exp2(top_ref[...] + (log_target - lse))
    c_ref[...] = c
    weigh_columns(c, tile_ref, out_ref)


def rows_after(target, parts_ref, last_ref, tile_ref, out_ref, c_ref):
    c = last_ref[...] * (target / jnp.sum(parts_ref[...].astype(F32), axis=0))
    c_ref[...] = c
    weigh_columns(c, tile_ref, out_ref)


def columns_after(parts_ref, w_ref, c_ref, tile_ref, out_ref):
    groups = tile_ref.shape[1] // LANES
    u = w_ref[...] / jnp.sum(parts_ref[...].astype(F32), axis=0)
    lane = lane_iota()
    sums = jnp.zeros((LANES, LANES), F32)
    for r in range(tile_ref.shape[0] // LANES):
        total = jnp.zeros((LANES, LANES), F32)
        for g in range(groups):
            total = total + tile_ref[r * LANES : (r + 1) * LANES, g * LANES : (g + 1) * LANES] * u[g : g + 1, :]
        sums = jnp.where(lane == r, jnp.sum(total, axis=1, keepdims=True), sums)
    out = sums.T[0:8, :] * c_ref[...]
    out_ref[...] = jnp.broadcast_to(out[None], out_ref.shape).astype(out_ref.dtype)


def final_sums(n_y, n_core, zl_ref, parts_ref, w_ref, f_ref, c_ref, tile_ref, docs_ref, out_ref, pot_ref, p_ref):
    n_cent, n_doc = tile_ref.shape
    groups = n_doc // LANES
    u = w_ref[...] / jnp.sum(parts_ref[...], axis=0)
    pot = (f_ref[...] + jnp.log2(u)) * LN2
    pot_ref[...] = jnp.where(zl_ref[0] == 0, pot[0:8, :], pot[8:16, :])
    cols = to_columns(c_ref[...])
    lane = lane_iota()
    masses = jnp.zeros((LANES, LANES), F32)
    for r in range(n_cent // LANES):
        rows = slice(r * LANES, (r + 1) * LANES)
        col = jnp.broadcast_to(cols[:, r : r + 1], (LANES, LANES))
        total = jnp.zeros((LANES, LANES), F32)
        for g in range(groups):
            lanes = slice(g * LANES, (g + 1) * LANES)
            p = tile_ref[rows, lanes] * u[g : g + 1, :] * col
            total = total + p
            p_ref[rows, lanes] = p.astype(BF16)
        masses = jnp.where(lane == r, jnp.sum(total, axis=1, keepdims=True), masses)
    mass = masses.T[0:8, :]
    high = mass.astype(BF16)
    low = (mass - high.astype(F32)).astype(BF16)
    chunk = n_cent // (n_y * n_core)
    for b in range(n_cent // 256):
        sums = jnp.dot(p_ref[b * 256 : (b + 1) * 256, :], docs_ref[...], preferred_element_type=F32).astype(BF16)
        for k in range(256 // chunk):
            q = b * (256 // chunk) + k
            peer = (q % n_y) * n_core + q // n_y
            out_ref[peer, 0:chunk, :] = sums[k * chunk : (k + 1) * chunk, :]
            r = q * chunk // LANES
            pair = jnp.concatenate([high[r : r + 1, :], low[r : r + 1, :]], axis=1)
            out_ref[peer, chunk : chunk + 16, :] = jnp.broadcast_to(pair.astype(F32), (16, 256)).astype(BF16)


def divide(half_ref, parts_ref, out_ref, mass_ref):
    chunk = parts_ref.shape[1] - 16
    total = jnp.zeros((chunk, 256), F32)
    mass = jnp.zeros((16, 256), F32)
    for p in range(parts_ref.shape[0]):
        total = total + parts_ref[p, 0:chunk, :].astype(F32)
        mass = mass + parts_ref[p, chunk : chunk + 16, :].astype(F32)
    mass = mass[0:8, 0:LANES] + mass[0:8, LANES:256]
    mass_ref[...] = to_columns(mass)
    col = mass_ref[pl.ds(pl.multiple_of(half_ref[0] * chunk, chunk), chunk), :]
    new = (total / jnp.concatenate([col, col], axis=1)).astype(BF16)
    out_ref[...] = jnp.broadcast_to(new[None], out_ref.shape)


def assemble(at_ref, own_ref, zl_ref, core_ref, both_ref, out_ref, sems):
    rows = own_ref.shape[0]
    zl, core = at_ref[0], at_ref[1]
    places = (zl * 2 + core, (1 - zl) * 2 + core, zl * 2 + 1 - core, (1 - zl) * 2 + 1 - core)
    copies = []
    for k, (place, ref) in enumerate(zip(places, (own_ref, zl_ref, core_ref, both_ref))):
        dst = out_ref.at[pl.ds(pl.multiple_of(place * rows, rows), rows), :]
        copies.append(pltpu.make_async_copy(ref, dst, sems.at[k]))
    for copy in copies:
        copy.start()
    for copy in copies:
        copy.wait()


def exchange(x, axes):
    return lax.all_to_all(x, axes, 0, 0)


def per_device(sizes, docs, cents, shard_ids, shard_mass):
    n_y, n_zl, n_core, n_zh, n_x = sizes
    row_peers, col_peers = n_zl * n_zh * n_x, n_y * n_core
    n_doc, n_cent = docs.shape[0] * 2, cents.shape[0] // 2
    doc_rows, cent_rows = n_doc // LANES, n_cent // LANES
    scale = 4.0 * docs.shape[1] ** -0.5 * LOG2E
    target = 0.5 * (docs.shape[0] * n_y * n_zl * n_core) / (cents.shape[0] * n_zh * n_x)
    zl = lax.axis_index("zl")
    core = lax.axis_index("core")
    at = jnp.stack([zl, core]).astype(jnp.int32)
    half = (lax.axis_index("y") % 2).astype(jnp.int32).reshape(1)
    swap = [(0, 1), (1, 0)]
    shape = jax.ShapeDtypeStruct
    tile_shape = pltpu.VMEM((n_cent, n_doc), F32)
    small = shape((cent_rows, LANES), F32)

    other_docs = lax.ppermute(docs, "zl", swap)
    ids = shard_ids.reshape(-1, LANES)
    other_ids = lax.ppermute(ids, "zl", swap)
    parts = call(
        functools.partial(first_rows, scale, row_peers),
        shape((row_peers, doc_rows // 2, LANES), F32),
        2,
        scratch=[pltpu.VMEM((cents.shape[0], 256), F32)],
        flops=2 * docs.shape[0] * cents.shape[0] * 256,
    )(docs, cents)
    parts = exchange(parts, ROWS)
    parts, tile, top, f, w, docs_all = call(
        functools.partial(first_columns, scale, col_peers),
        (
            shape((col_peers, cent_rows, LANES), F32),
            tile_shape,
            small,
            shape((doc_rows, LANES), F32),
            shape((doc_rows, LANES), F32),
            pltpu.VMEM((n_doc, 256), BF16),
        ),
        8,
        smem=(0, 1),
        flops=2 * n_doc * n_cent * 256,
    )(at, shard_mass, parts, ids, other_ids, docs, other_docs, cents)

    def rows_out(dtype):
        return (shape((row_peers, doc_rows, LANES), dtype), small)

    parts = exchange(parts, COLS)
    log_target = math.log2(target)
    parts, c = call(functools.partial(rows_after_first, log_target), rows_out(BF16), 3, flops=2 * n_doc * n_cent)(parts, top, tile)
    for turn in range(2):
        parts = exchange(parts, ROWS)
        parts = call(columns_after, shape((col_peers, cent_rows, LANES), F32), 4, flops=2 * n_doc * n_cent)(parts, w, c, tile)
        parts = exchange(parts, COLS)
        parts, c = call(functools.partial(rows_after, target), rows_out(F32 if turn else BF16), 3, flops=2 * n_doc * n_cent)(parts, c, tile)
    parts = exchange(parts, ROWS)
    chunk = n_cent // col_peers
    sums, pot = call(
        functools.partial(final_sums, n_y, n_core),
        (shape((col_peers, chunk + 16, 256), BF16), shape((doc_rows // 2, LANES), F32)),
        7,
        smem=(0,),
        scratch=[pltpu.VMEM((n_cent, n_doc), BF16)],
        flops=2 * n_doc * n_cent * 256,
    )(at, parts, w, f, c, tile, docs_all)
    sums = exchange(sums, COLS)
    new = call(divide, shape((n_y, chunk, 256), BF16), 2, smem=(0,), scratch=[pltpu.VMEM((LANES, LANES), F32)])(half, sums)
    own = exchange(new, "y").reshape(n_y * chunk, 256)
    by_zl = lax.ppermute(own, "zl", swap)
    by_core = lax.ppermute(own, "core", swap)
    by_both = lax.ppermute(by_zl, "core", swap)
    anywhere = pl.BlockSpec(memory_space=pl.ANY)
    new = call(
        assemble,
        shape((cents.shape[0], 256), BF16),
        5,
        in_specs=[pl.BlockSpec(memory_space=pltpu.SMEM)] + [anywhere] * 4,
        out_specs=anywhere,
        scratch=[pltpu.SemaphoreType.DMA((4,))],
    )(at, own, by_zl, by_core, by_both)
    return new, pot.reshape(-1)


SIZES = (8, 2, 2, 4, 4)


def solution(mesh, sizes=SIZES):
    fine = Mesh(mesh.devices.reshape(sizes), ("y", "zl", "core", "zh", "x"))
    docs, cents = ("y", "zl", "core"), ("zh", "x")
    return jax.shard_map(
        functools.partial(per_device, sizes),
        mesh=fine,
        in_specs=(P(docs, None), P(cents, None), P(docs), P()),
        out_specs=(P(cents, None), P(docs)),
        check_vma=False,
    )
```

time: 971 us -> 189 us (0.19)
  blocking collectives: 709 us -> 97.7 us
  waiting for transfers between devices: 172 us -> 31.2 us
  other arithmetic: 62.8 us -> 0.08 us
  starting transfers between devices: 0.04 us -> 34 us
  Pallas kernels: 0 us -> 18.4 us
  between operations: 14.2 us -> 0.91 us
  matrix products: 12 us -> 0 us
    psum x8 -> x0, blocking collectives: 359 us -> none  [the longest x3 162 us: col_lse(): total = lax.psum(jnp.sum(jnp.exp(tile - top[None, :]), axis=0), 'doc')]
    pmax x7 -> x0, blocking collectives: 351 us -> none  [the longest x3 205 us: col_lse(): top = lax.pmax(jnp.max(tile, axis=0), 'doc')]
    psum x1 -> x0, waiting for transfers between devices: 172 us -> none  [per_device(): all_sums, all_mass = lax.psum((sums, mass), 'doc')]
    all_to_all x0 -> x7, blocking collectives: none -> 97.7 us  [exchange(): return lax.all_to_all(x, axes, 0, 0)]
    reduce_sum x9 -> x0, other arithmetic: 35 us -> none  [the longest x4 17.7 us: row_lse(): total = lax.psum(jnp.sum(jnp.exp(tile - top[:, None]), axis=1), 'cent')]
    all_to_all x0 -> x2, waiting for transfers between devices: none -> 24.5 us  [exchange(): return lax.all_to_all(x, axes, 0, 0)]
    reduce_max x6 -> x0, other arithmetic: 24.1 us -> none  [the longest x3 12.1 us: row_lse(): top = lax.pmax(jnp.max(tile, axis=1), 'cent')]
    pallas_call x0 -> x10, Pallas kernels: none -> 18.4 us  [the longest x1 4.46 us: per_device(): call(functools.partial(first_columns, scale, col_peers), (shape((col_peer...]
  transfers between devices with their start and end apart: 1 -> 7, of which waited for: 1 -> 5; matrix products, arithmetic and copies ran while one was open for 0% -> 0% of each run, Pallas kernels for 0% -> 2%
where the time goes in v1:
time: 189 us; the launch traced here: 188 us
  blocking collectives  97.7 us (52%)
  starting transfers between devices  34 us (18%)
  waiting for transfers between devices  31.2 us (17%)
  Pallas kernels  18.4 us (10%)
  local copies, waits for them, and re-layouts  5.87 us (3%)
    all_to_all x7, blocking collectives, exchange(): return lax.all_to_all(x, axes, 0, 0)  97.7 us
    all_to_all x2, waiting for transfers between devices, exchange(): return lax.all_to_all(x, axes, 0, 0)  24.5 us
    all_to_all x2, starting transfers between devices, exchange(): return lax.all_to_all(x, axes, 0, 0)  17.4 us
    unnamed x12, local copies, waits for them, and re-layouts  5.87 us
    ppermute x1, starting transfers between devices, per_device(): other_docs = lax.ppermute(docs, 'zl', swap)  4.83 us
    pallas_call x1, Pallas kernels, per_device(): call(functools.partial(first_columns, scale, col_peers), (shape((col_peer...  4.46 us
    pallas_call x1, Pallas kernels, per_device(): call(functools.partial(first_rows, scale, row_peers), shape((row_peers, d...  3.97 us
    ppermute x1, waiting for transfers between devices, per_device(): by_zl = lax.ppermute(own, 'zl', swap)  3.85 us
  transfers between devices with their start and end apart: 7, of which 5 were waited for; matrix products, arithmetic and copies ran while one was open for 0% of the time, Pallas kernels for 2%

profile of v1, /device:TPU:1, one launch (start us, length us, event | category | flops | bytes accessed | tf_op | source)
XLA Modules:
  0.0 188.1 jit_solution(13939310336131538092)
XLA Ops:
  0.6 4.8 %collective-permute-start.1 = (bf16[1024,256]{1,0:T(8,128)(2,1)}, bf16[1024,256]{1,0:T(8,128)(2,1)S(1)}, u32[]{:S(2)}, u32[]{:S(2)}) collective-permute-start(bf16[1024,256]{1,0:T(8,128)(2,1)} %docs_ref.3), channel_id=1, source_target_pairs={{0,32},{32,0},{1,33},{33,1},{2,34},{34,2},{3,35},{35,3},{4,36},{36... | collective-permute-start | bytes 1572872 | tf_op jit(solution)/shard_map/ppermute | solution.py:256
  5.5 0.0 copy-start
  5.5 1.2 copy-done
  6.7 0.0 copy-start.2
  6.7 1.0 copy-done.2
  7.7 4.0 %shard_map.59 = f32[32,8,128]{2,1,0:T(8,128)} custom-call(bf16[1024,256]{1,0:T(8,128)(2,1)S(1)} %copy-done.2, bf16[2048,256]{1,0:T(8,128)(2,1)S(1)} %copy-done), custom_call_target="tpu_custom_call" | custom-call | flops 1073741824 | bytes 1048576 | tf_op jit(solution)/shard_map/pallas_call | solution.py:259
  11.7 12.0 %all-to-all-start = ((f32[32,8,128]{2,1,0:T(8,128)}), f32[32,8,128]{2,1,0:T(8,128)S(1)}, u32[]{:S(2)}, u32[]{:S(2)}) async-start(f32[32,8,128]{2,1,0:T(8,128)} %shard_map.59), calls=%async_computation | async-start | bytes 262144 | tf_op jit(solution)/shard_map/all_to_all | solution.py:237
  23.7 3.1 %collective-permute-start = (s32[8,128]{1,0:T(8,128)}, s32[8,128]{1,0:T(8,128)S(1)}, u32[]{:S(2)}, u32[]{:S(2)}) collective-permute-start(s32[8,128]{1,0:T(8,128)} %bitcast.9), channel_id=1, source_target_pairs={{0,32},{32,0},{1,33},{33,1},{2,34},{34,2},{3,35},{35,3},{4,36},{36... | collective-permute-start | bytes 12296 | tf_op jit(solution)/shard_map/ppermute | solution.py:258
  26.9 0.1 pad_add_fusion.zl_ref.at_ref
  26.9 1.7 collective-permute-done.other_ids_ref
  28.6 4.5 %all-to-all-done.parts_ref = f32[32,8,128]{2,1,0:T(8,128)S(1)} async-done(((f32[32,8,128]{2,1,0:T(8,128)}), f32[32,8,128]{2,1,0:T(8,128)S(1)}, u32[]{:S(2)}, u32[]{:S(2)}) %all-to-all-start) | async-done | bytes 131104 | tf_op jit(solution)/shard_map/all_to_all | solution.py:237
  33.1 0.0 collective-permute-done.1.other_ref
  33.1 0.0 copy-start.1
  33.1 1.2 copy-done.1
  34.3 0.0 copy-start.3
  34.3 1.0 copy-done.3
  35.4 0.0 copy-start.4
  35.4 0.7 copy-done.4
  36.1 0.0 copy-start.5
  36.1 0.7 copy-done.5
  36.7 4.5 %shard_map.60 = (f32[16,8,128]{2,1,0:T(8,128)S(1)}, f32[1024,2048]{1,0:T(8,128)S(1)}, f32[8,128]{1,0:T(8,128)S(1)}, f32[16,128]{1,0:T(8,128)S(1)}, f32[16,128]{1,0:T(8,128)S(1)}, /*index=5*/bf16[2048,256]{1,0:T(8,128)(2,1)S(1)}) custom-call(s32[2]{0:T(128)S(1)} %pad_add_fusion.zl_ref.at_ref, s32[64]{0:T(128)S(1)} %copy-done.5, ...), custom_call_target="tpu_custom_call" | custom-call | flops 1073741824 | bytes 1048576 | tf_op jit(solution)/shard_map/pallas_call | solution.py:267
  41.2 17.2 %all_to_all.45.parts_ref = f32[16,8,128]{2,1,0:T(8,128)S(1)} all-to-all(f32[16,8,128]{2,1,0:T(8,128)S(1)} %get-tuple-element.16), channel_id=1, replica_groups=mesh['y'=8,'zl'=2,'core'=2,'zh'=4,'x'=4] {'y','core'}, dimensions={0} | all-to-all | bytes 131072 | tf_op jit(solution)/shard_map/all_to_all | solution.py:237
  58.4 1.0 shard_map.61
  59.4 14.3 %all_to_all.46.parts_ref = bf16[32,16,128]{2,1,0:T(8,128)(2,1)S(1)} all-to-all(bf16[32,16,128]{2,1,0:T(8,128)(2,1)S(1)} %get-tuple-element.19), channel_id=1, replica_groups=mesh['y'=8,'zl'=2,'core'=2,'zh'=4,'x'=4] {'zl','zh','x'}, dimensions={0} | all-to-all | bytes 262144 | tf_op jit(solution)/shard_map/all_to_all | solution.py:237
  73.7 0.7 shard_map.62
  74.4 11.8 %all_to_all.47.parts_ref = f32[16,8,128]{2,1,0:T(8,128)S(1)} all-to-all(f32[16,8,128]{2,1,0:T(8,128)S(1)} %shard_map.62), channel_id=1, replica_groups=mesh['y'=8,'zl'=2,'core'=2,'zh'=4,'x'=4] {'y','core'}, dimensions={0} | all-to-all | bytes 131072 | tf_op jit(solution)/shard_map/all_to_all | solution.py:237
  86.2 1.0 shard_map.63
  87.2 12.9 %all_to_all.48.parts_ref = bf16[32,16,128]{2,1,0:T(8,128)(2,1)S(1)} all-to-all(bf16[32,16,128]{2,1,0:T(8,128)(2,1)S(1)} %get-tuple-element.22), channel_id=1, replica_groups=mesh['y'=8,'zl'=2,'core'=2,'zh'=4,'x'=4] {'zl','zh','x'}, dimensions={0} | all-to-all | bytes 262144 | tf_op jit(solution)/shard_map/all_to_all | solution.py:237
  100.1 0.7 shard_map.64
  100.8 11.8 %all_to_all.49.parts_ref = f32[16,8,128]{2,1,0:T(8,128)S(1)} all-to-all(f32[16,8,128]{2,1,0:T(8,128)S(1)} %shard_map.64), channel_id=1, replica_groups=mesh['y'=8,'zl'=2,'core'=2,'zh'=4,'x'=4] {'y','core'}, dimensions={0} | all-to-all | bytes 131072 | tf_op jit(solution)/shard_map/all_to_all | solution.py:237
  112.6 1.0 shard_map.65
  113.6 15.1 %all_to_all.50.parts_ref = f32[32,16,128]{2,1,0:T(8,128)S(1)} all-to-all(f32[32,16,128]{2,1,0:T(8,128)S(1)} %get-tuple-element.24), channel_id=1, replica_groups=mesh['y'=8,'zl'=2,'core'=2,'zh'=4,'x'=4] {'zl','zh','x'}, dimensions={0} | all-to-all | bytes 524288 | tf_op jit(solution)/shard_map/all_to_all | solution.py:237
  128.6 3.8 %shard_map.66 = (bf16[16,80,256]{2,1,0:T(8,128)(2,1)}, f32[8,128]{1,0:T(8,128)}) custom-call(s32[2]{0:T(128)S(1)} %pad_add_fusion.zl_ref.at_ref, f32[32,16,128]{2,1,0:T(8,128)S(1)} %all_to_all.50.parts_ref, f32[16,128]{1,0:T(8,128)S(1)} %get-tuple-element.20.w_ref, f32[16,128]{1,0:T(8,128)S(1)} %get-tuple-element.25.f_ref, ...), custom_call_target="tpu_custom_call" | custom-call | flops 1073741824 | bytes 1048576 | tf_op jit(solution)/shard_map/pallas_call | solution.py:295
  132.5 5.4 %all-to-all-start.7 = ((bf16[16,80,256]{2,1,0:T(8,128)(2,1)}), bf16[16,80,256]{2,1,0:T(8,128)(2,1)S(1)}, u32[]{:S(2)}, u32[]{:S(2)}) async-start(bf16[16,80,256]{2,1,0:T(8,128)(2,1)} %get-tuple-element.28), calls=%async_computation.7 | async-start | bytes 1310720 | tf_op jit(solution)/shard_map/all_to_all | solution.py:237
  137.9 20.0 %all-to-all-done.7.parts_ref = bf16[16,80,256]{2,1,0:T(8,128)(2,1)S(1)} async-done(((bf16[16,80,256]{2,1,0:T(8,128)(2,1)}), bf16[16,80,256]{2,1,0:T(8,128)(2,1)S(1)}, u32[]{:S(2)}, u32[]{:S(2)}) %all-to-all-start.7) | async-done | bytes 655392 | tf_op jit(solution)/shard_map/all_to_all | solution.py:237
  157.9 0.1 shard_map.67
  158.1 14.7 %all_to_all.51 = bf16[8,64,256]{2,1,0:T(8,128)(2,1)S(1)} all-to-all(bf16[8,64,256]{2,1,0:T(8,128)(2,1)S(1)} %shard_map.67), channel_id=1, replica_groups=mesh['y'=8,'zl'=2,'core'=2,'zh'=4,'x'=4] {'y'}, dimensions={0} | all-to-all | bytes 524288 | tf_op jit(solution)/shard_map/all_to_all | solution.py:237
  172.8 2.7 %collective-permute-start.2 = (bf16[512,256]{1,0:T(8,128)(2,1)S(1)}, bf16[512,256]{1,0:T(8,128)(2,1)S(1)}, u32[]{:S(2)}, u32[]{:S(2)}) collective-permute-start(bf16[512,256]{1,0:T(8,128)(2,1)S(1)} %bitcast.6), channel_id=1, source_target_pairs={{0,32},{32,0},{1,33},{33,1},{2,34},{34,2},{3,35},{35,3},{4,36},{36... | collective-permute-start | bytes 786440 | tf_op jit(solution)/shard_map/ppermute | solution.py:306
  175.5 2.7 %collective-permute-start.3 = (bf16[512,256]{1,0:T(8,128)(2,1)S(1)}, bf16[512,256]{1,0:T(8,128)(2,1)S(1)}, u32[]{:S(2)}, u32[]{:S(2)}) collective-permute-start(bf16[512,256]{1,0:T(8,128)(2,1)S(1)} %bitcast.7), channel_id=1, source_target_pairs={{0,16},{16,0},{1,17},{17,1},{2,18},{18,2},{3,19},{19,3},{4,20},{20... | collective-permute-start | bytes 786440 | tf_op jit(solution)/shard_map/ppermute | solution.py:307
  178.2 3.9 %collective-permute-done.2.zl_ref = bf16[512,256]{1,0:T(8,128)(2,1)S(1)} collective-permute-done((bf16[512,256]{1,0:T(8,128)(2,1)S(1)}, bf16[512,256]{1,0:T(8,128)(2,1)S(1)}, u32[]{:S(2)}, u32[]{:S(2)}) %collective-permute-start.2) | collective-permute-done | bytes 262176 | tf_op jit(solution)/shard_map/ppermute | solution.py:306
  182.0 3.3 %collective-permute-start.4 = (bf16[512,256]{1,0:T(8,128)(2,1)S(1)}, bf16[512,256]{1,0:T(8,128)(2,1)S(1)}, u32[]{:S(2)}, u32[]{:S(2)}) collective-permute-start(bf16[512,256]{1,0:T(8,128)(2,1)S(1)} %collective-permute-done.2.zl_ref), channel_id=1, source_target_pairs={{0,16},{16,0},{1,17},{17,1},{2,18},{18,2},{3,19},{19,3},{4,20},{20... | collective-permute-start | bytes 786440 | tf_op jit(solution)/shard_map/ppermute | solution.py:308
  185.3 0.0 collective-permute-done.3.core_ref
  185.3 1.1 collective-permute-done.4.both_ref
  186.4 1.5 shard_map.68
Async XLA Ops:
  0.6 32.5 %collective-permute-start.1 = (bf16[1024,256]{1,0:T(8,128)(2,1)}, bf16[1024,256]{1,0:T(8,128)(2,1)S(1)}, u32[]{:S(2)}, u32[]{:S(2)}) collective-permute-start(bf16[1024,256]{1,0:T(8,128)(2,1)} %docs_ref.3), channel_id=1, source_target_pairs={{0,32},{32,0},{1,33},{33,1},{2,34},{34,2},{3,35},{35,3},{4,36},{36... | collective-permute-start | bytes 1572872 | tf_op jit(solution)/shard_map/ppermute | solution.py:256
  5.5 1.2 copy-start
  6.7 1.0 copy-start.2
  11.7 21.4 %all-to-all-start = ((f32[32,8,128]{2,1,0:T(8,128)}), f32[32,8,128]{2,1,0:T(8,128)S(1)}, u32[]{:S(2)}, u32[]{:S(2)}) async-start(f32[32,8,128]{2,1,0:T(8,128)} %shard_map.59), calls=%async_computation | async-start | bytes 262144 | tf_op jit(solution)/shard_map/all_to_all | solution.py:237
  23.7 4.9 %collective-permute-start = (s32[8,128]{1,0:T(8,128)}, s32[8,128]{1,0:T(8,128)S(1)}, u32[]{:S(2)}, u32[]{:S(2)}) collective-permute-start(s32[8,128]{1,0:T(8,128)} %bitcast.9), channel_id=1, source_target_pairs={{0,32},{32,0},{1,33},{33,1},{2,34},{34,2},{3,35},{35,3},{4,36},{36... | collective-permute-start | bytes 12296 | tf_op jit(solution)/shard_map/ppermute | solution.py:258
  33.1 1.2 copy-start.1
  34.3 1.0 copy-start.3
  35.4 0.7 copy-start.4
  36.1 0.7 copy-start.5
  132.5 25.4 %all-to-all-start.7 = ((bf16[16,80,256]{2,1,0:T(8,128)(2,1)}), bf16[16,80,256]{2,1,0:T(8,128)(2,1)S(1)}, u32[]{:S(2)}, u32[]{:S(2)}) async-start(bf16[16,80,256]{2,1,0:T(8,128)(2,1)} %get-tuple-element.28), calls=%async_computation.7 | async-start | bytes 1310720 | tf_op jit(solution)/shard_map/all_to_all | solution.py:237
  172.8 9.2 %collective-permute-start.2 = (bf16[512,256]{1,0:T(8,128)(2,1)S(1)}, bf16[512,256]{1,0:T(8,128)(2,1)S(1)}, u32[]{:S(2)}, u32[]{:S(2)}) collective-permute-start(bf16[512,256]{1,0:T(8,128)(2,1)S(1)} %bitcast.6), channel_id=1, source_target_pairs={{0,32},{32,0},{1,33},{33,1},{2,34},{34,2},{3,35},{35,3},{4,36},{36... | collective-permute-start | bytes 786440 | tf_op jit(solution)/shard_map/ppermute | solution.py:306
  175.5 9.8 %collective-permute-start.3 = (bf16[512,256]{1,0:T(8,128)(2,1)S(1)}, bf16[512,256]{1,0:T(8,128)(2,1)S(1)}, u32[]{:S(2)}, u32[]{:S(2)}) collective-permute-start(bf16[512,256]{1,0:T(8,128)(2,1)S(1)} %bitcast.7), channel_id=1, source_target_pairs={{0,16},{16,0},{1,17},{17,1},{2,18},{18,2},{3,19},{19,3},{4,20},{20... | collective-permute-start | bytes 786440 | tf_op jit(solution)/shard_map/ppermute | solution.py:307
  182.0 4.4 %collective-permute-start.4 = (bf16[512,256]{1,0:T(8,128)(2,1)S(1)}, bf16[512,256]{1,0:T(8,128)(2,1)S(1)}, u32[]{:S(2)}, u32[]{:S(2)}) collective-permute-start(bf16[512,256]{1,0:T(8,128)(2,1)S(1)} %collective-permute-done.2.zl_ref), channel_id=1, source_target_pairs={{0,16},{16,0},{1,17},{17,1},{2,18},{18,2},{3,19},{19,3},{4,20},{20... | collective-permute-start | bytes 786440 | tf_op jit(solution)/shard_map/ppermute | solution.py:308

commit v2 on v1

--- a/solution.py
+++ b/solution.py
@@ -19,7 +19,7 @@
 BF16 = jnp.bfloat16
 
 
-def call(kernel, out_shape, n_in, smem=(), scratch=(), flops=0, out_specs=None, in_specs=None):
+def call(kernel, out_shape, n_in, smem=(), scratch=(), flops=0, out_specs=None, in_specs=None, alias=None):
     vmem = pl.BlockSpec(memory_space=pltpu.VMEM)
     if in_specs is None:
         in_specs = [pl.BlockSpec(memory_space=pltpu.SMEM) if i in smem else vmem for i in range(n_in)]
@@ -31,6 +31,7 @@
         in_specs=in_specs,
         out_specs=out_specs,
         scratch_shapes=list(scratch),
+        input_output_aliases=alias or {},
         compiler_params=pltpu.CompilerParams(vmem_limit_bytes=VMEM_LIMIT),
         cost_estimate=pl.CostEstimate(flops=flops, bytes_accessed=1 << 20, transcendentals=0),
     )
@@ -55,44 +56,55 @@
     return lax.fori_loop(0, mass_ref.shape[0], step, jnp.zeros(ids.shape, F32)) * 0.125
 
 
-def first_rows(scale, peers, docs_ref, cents_ref, out_ref, s_ref):
-    n_cent = cents_ref.shape[0]
-    block = 64
-
-    def group(g, _):
-        docs = docs_ref[pl.ds(pl.multiple_of(g * 256, 256), 256), :]
-        top = jnp.full((8, 256), -jnp.inf, F32)
-        for q in range(n_cent // 256):
-            s = nt_dot(cents_ref[q * 256 : (q + 1) * 256, :], docs)
-            s_ref[q * 256 : (q + 1) * 256, :] = s
-            top = jnp.maximum(top, jnp.max(s.reshape(32, 8, 256), axis=0))
-        top = jnp.max(top, axis=0, keepdims=True) * scale
-
-        def part(q, total):
-            s = s_ref[pl.ds(pl.multiple_of(q * block, block), block), :]
-            return total + jnp.sum(jnp.exp2(s * scale - top).reshape(block // 8, 8, 256), axis=0)
-
-        total = lax.fori_loop(0, n_cent // block, part, jnp.zeros((8, 256), F32), unroll=8)
-        lse = top + jnp.log2(jnp.sum(total, axis=0, keepdims=True))
-        for h in range(2):
-            row = lse[:, h * LANES : (h + 1) * LANES]
-            out_ref[:, pl.ds(g * 2 + h, 1), :] = jnp.broadcast_to(row[None], (peers, 1, LANES))
-        return 0
-
-    lax.fori_loop(0, docs_ref.shape[0] // 256, group, 0)
+def first_rows(
+    scale, peers, mass_ref, ids_ref, docs_hbm, cents_hbm, out_ref, docs_ref, cents_ref, sems
+):
+    n_doc, n_cent = docs_hbm.shape[0], cents_hbm.shape[0]
+    block = 512
+    steps = n_cent // block
+    copies = [pltpu.make_async_copy(docs_hbm, docs_ref.at[0:n_doc, :], sems.at[steps])]
+    for q in range(steps):
+        rows = pl.ds(q * block, block)
+        copies.append(pltpu.make_async_copy(cents_hbm.at[rows, :], cents_ref.at[rows, :], sems.at[q]))
+    for copy in copies:
+        copy.start()
+    w = weights_of(ids_ref[...], mass_ref)
+    pad = jnp.concatenate([jnp.concatenate([w, w], axis=0)] * 2, axis=1)
+    docs_ref[n_doc : n_doc + 16, :] = pad.astype(BF16)
+    copies[0].wait()
+    groups = n_doc // 256
+    tops = [jnp.full((8, 256), -jnp.inf, F32)] * groups
+    totals = [jnp.zeros((8, 256), F32)] * groups
+    for q in range(steps):
+        copies[q + 1].wait()
+        cents = cents_ref[q * block : (q + 1) * block, :]
+        for g in range(groups):
+            s = nt_dot(cents, docs_ref[g * 256 : (g + 1) * 256, :]).reshape(block // 8, 8, 256)
+            top = jnp.maximum(tops[g], jnp.max(s, axis=0) * scale)
+            totals[g] = totals[g] * jnp.exp2(tops[g] - top) + jnp.sum(jnp.exp2(s * scale - top[None]), axis=0)
+            tops[g] = top
+    rows = []
+    for g in range(groups):
+        top = jnp.max(tops[g], axis=0, keepdims=True)
+        lse = top + jnp.log2(jnp.sum(totals[g] * jnp.exp2(tops[g] - top), axis=0, keepdims=True))
+        rows += [lse[:, 0:LANES], lse[:, LANES:256]]
+    out_ref[...] = jnp.broadcast_to(jnp.concatenate(rows, axis=0)[None], out_ref.shape)
 
 
 def first_columns(
-    scale, peers, zl_ref, mass_ref, parts_ref, ids_ref, other_ids_ref, docs_ref, other_ref, cents_ref,
-    out_ref, tile_ref, top_ref, f_ref, w_ref, docs_all_ref,
+    scale, chunk, zl_ref, parts_ref, docs_ref, other_ref, cents_ref,
+    out_ref, tile_ref, top_ref, f_ref, w_ref, docs_all_ref, half_ref,
 ):
     zl = zl_ref[0]
-    n_doc, n_cent = docs_ref.shape[0], cents_ref.shape[0] // 2
+    n_doc, n_cent = docs_ref.shape[0] - 16, cents_ref.shape[0] // 2
     groups = 2 * n_doc // LANES
-    docs_all_ref[pl.ds(pl.multiple_of(zl * n_doc, n_doc), n_doc), :] = docs_ref[...]
-    docs_all_ref[pl.ds(pl.multiple_of((1 - zl) * n_doc, n_doc), n_doc), :] = other_ref[...]
-    own = weights_of(ids_ref[...], mass_ref)
-    other = weights_of(other_ids_ref[...], mass_ref)
+    docs_all_ref[pl.ds(pl.multiple_of(zl * n_doc, n_doc), n_doc), :] = docs_ref[0:n_doc, :]
+    docs_all_ref[pl.ds(pl.multiple_of((1 - zl) * n_doc, n_doc), n_doc), :] = other_ref[0:n_doc, :]
+    for q in range(n_cent // chunk):
+        rows = pl.ds(pl.multiple_of(q * 2 * chunk + zl * chunk, chunk), chunk)
+        half_ref[q * chunk : (q + 1) * chunk, :] = cents_ref[rows, :]
+    own = docs_ref[n_doc : n_doc + 16, 0:LANES].astype(F32)[0:8]
+    other = other_ref[n_doc : n_doc + 16, 0:LANES].astype(F32)[0:8]
     w_ref[0:8, :] = jnp.where(zl == 0, own, other)
     w_ref[8:16, :] = jnp.where(zl == 0, other, own)
     half = parts_ref.shape[0] // 2
@@ -101,13 +113,12 @@
         top = jnp.max(parts, axis=0)
         lse = top + jnp.log2(jnp.sum(jnp.exp2(parts - top[None]), axis=0))
         f_ref[z * 8 : (z + 1) * 8, :] = jnp.log2(w_ref[z * 8 : (z + 1) * 8, :]) - lse
-    base = pl.multiple_of(zl * n_cent, n_cent)
 
     for g in range(groups // 2):
         f = jnp.concatenate([f_ref[2 * g : 2 * g + 1, :], f_ref[2 * g + 1 : 2 * g + 2, :]], axis=1)
         docs = docs_all_ref[g * 256 : (g + 1) * 256, :]
         for q in range(n_cent // 256):
-            cents = cents_ref[pl.ds(pl.multiple_of(base + q * 256, 256), 256), :]
+            cents = half_ref[q * 256 : (q + 1) * 256, :]
             tile_ref[q * 256 : (q + 1) * 256, g * 256 : (g + 1) * 256] = nt_dot(cents, docs) * scale + f
     lane = lane_iota()
     tops = jnp.zeros((LANES, LANES), F32)
@@ -126,7 +137,7 @@
         tops = jnp.where(lane == r, top, tops)
         lses = jnp.where(lane == r, top + jnp.log2(jnp.sum(total, axis=1, keepdims=True)), lses)
     top_ref[...] = tops.T[0:8, :]
-    out_ref[...] = jnp.broadcast_to(lses.T[0:8, :][None], (peers, 8, LANES))
+    out_ref[...] = jnp.broadcast_to(lses.T[0:8, :][None], out_ref.shape)
 
 
 def weigh_columns(c, tile_ref, out_ref):
@@ -191,46 +202,50 @@
             p_ref[rows, lanes] = p.astype(BF16)
         masses = jnp.where(lane == r, jnp.sum(total, axis=1, keepdims=True), masses)
     mass = masses.T[0:8, :]
-    high = mass.astype(BF16)
-    low = (mass - high.astype(F32)).astype(BF16)
+    high = mass.astype(BF16).astype(F32)
+    low = mass - high
     chunk = n_cent // (n_y * n_core)
     for b in range(n_cent // 256):
         sums = jnp.dot(p_ref[b * 256 : (b + 1) * 256, :], docs_ref[...], preferred_element_type=F32).astype(BF16)
         for k in range(256 // chunk):
             q = b * (256 // chunk) + k
             peer = (q % n_y) * n_core + q // n_y
-            out_ref[peer, 0:chunk, :] = sums[k * chunk : (k + 1) * chunk, :]
+            for i in range(chunk // 16):
+                for h in range(2):
+                    at = (i * 2 + h) * LANES
+                    out_ref[peer, :, at : at + LANES] = sums[k * chunk + i * 16 : k * chunk + (i + 1) * 16, h * LANES : (h + 1) * LANES]
             r = q * chunk // LANES
-            pair = jnp.concatenate([high[r : r + 1, :], low[r : r + 1, :]], axis=1)
-            out_ref[peer, chunk : chunk + 16, :] = jnp.broadcast_to(pair.astype(F32), (16, 256)).astype(BF16)
+            pair = [jnp.broadcast_to(x[r : r + 1, :], (8, LANES)) for x in (high, low)]
+            out_ref[peer, :, 2 * LANES * (chunk // 16) :] = jnp.concatenate(pair, axis=0).astype(BF16)
 
 
 def divide(half_ref, parts_ref, out_ref, mass_ref):
-    chunk = parts_ref.shape[1] - 16
-    total = jnp.zeros((chunk, 256), F32)
-    mass = jnp.zeros((16, 256), F32)
-    for p in range(parts_ref.shape[0]):
-        total = total + parts_ref[p, 0:chunk, :].astype(F32)
-        mass = mass + parts_ref[p, chunk : chunk + 16, :].astype(F32)
-    mass = mass[0:8, 0:LANES] + mass[0:8, LANES:256]
+    total = parts_ref[0].astype(F32)
+    for p in range(1, parts_ref.shape[0]):
+        total = total + parts_ref[p].astype(F32)
+    tiles = total.shape[1] // LANES - 1
+    chunk = tiles * 8
+    mass = total[0:8, tiles * LANES :] + total[8:16, tiles * LANES :]
     mass_ref[...] = to_columns(mass)
     col = mass_ref[pl.ds(pl.multiple_of(half_ref[0] * chunk, chunk), chunk), :]
-    new = (total / jnp.concatenate([col, col], axis=1)).astype(BF16)
-    out_ref[...] = jnp.broadcast_to(new[None], out_ref.shape)
-
-
-def assemble(at_ref, own_ref, zl_ref, core_ref, both_ref, out_ref, sems):
-    rows = own_ref.shape[0]
-    zl, core = at_ref[0], at_ref[1]
-    places = (zl * 2 + core, (1 - zl) * 2 + core, zl * 2 + 1 - core, (1 - zl) * 2 + 1 - core)
-    copies = []
-    for k, (place, ref) in enumerate(zip(places, (own_ref, zl_ref, core_ref, both_ref))):
-        dst = out_ref.at[pl.ds(pl.multiple_of(place * rows, rows), rows), :]
-        copies.append(pltpu.make_async_copy(ref, dst, sems.at[k]))
-    for copy in copies:
-        copy.start()
-    for copy in copies:
-        copy.wait()
+    for i in range(chunk // 16):
+        pair = [total[:, (i * 2 + h) * LANES : (i * 2 + h + 1) * LANES] / col[i * 16 : (i + 1) * 16, :] for h in range(2)]
+        new = jnp.concatenate(pair, axis=1).astype(BF16)
+        out_ref[:, i * 16 : (i + 1) * 16, :] = jnp.broadcast_to(new[None], (out_ref.shape[0], 16, 256))
+
+
+def place_own(at_ref, x_ref, out_ref, sem):
+    rows = x_ref.shape[0]
+    copy = pltpu.make_async_copy(x_ref, out_ref.at[pl.ds(pl.multiple_of(at_ref[1] * rows, rows), rows), :], sem)
+    copy.start()
+    copy.wait()
+
+
+def place_other(at_ref, x_ref, _, out_ref, sem):
+    rows = x_ref.shape[0]
+    copy = pltpu.make_async_copy(x_ref, out_ref.at[pl.ds(pl.multiple_of((1 - at_ref[1]) * rows, rows), rows), :], sem)
+    copy.start()
+    copy.wait()
 
 
 def exchange(x, axes):
@@ -253,19 +268,26 @@
     tile_shape = pltpu.VMEM((n_cent, n_doc), F32)
     small = shape((cent_rows, LANES), F32)
 
+    any_space = pl.BlockSpec(memory_space=pl.ANY)
+    vmem = pl.BlockSpec(memory_space=pltpu.VMEM)
+    smem = pl.BlockSpec(memory_space=pltpu.SMEM)
+    parts, docs, cents = call(
+        functools.partial(first_rows, scale, row_peers),
+        (
+            shape((row_peers, doc_rows // 2, LANES), F32),
+            pltpu.VMEM((docs.shape[0] + 16, 256), BF16),
+            pltpu.VMEM(cents.shape, BF16),
+        ),
+        4,
+        in_specs=[smem, vmem, any_space, any_space],
+        scratch=[pltpu.SemaphoreType.DMA((5,))],
+        flops=2 * docs.shape[0] * cents.shape[0] * 256,
+    )(shard_mass, shard_ids.reshape(-1, LANES), docs, cents)
     other_docs = lax.ppermute(docs, "zl", swap)
-    ids = shard_ids.reshape(-1, LANES)
-    other_ids = lax.ppermute(ids, "zl", swap)
-    parts = call(
-        functools.partial(first_rows, scale, row_peers),
-        shape((row_peers, doc_rows // 2, LANES), F32),
-        2,
-        scratch=[pltpu.VMEM((cents.shape[0], 256), F32)],
-        flops=2 * docs.shape[0] * cents.shape[0] * 256,
-    )(docs, cents)
     parts = exchange(parts, ROWS)
+    chunk = n_cent // col_peers
     parts, tile, top, f, w, docs_all = call(
-        functools.partial(first_columns, scale, col_peers),
+        functools.partial(first_columns, scale, chunk),
         (
             shape((col_peers, cent_rows, LANES), F32),
             tile_shape,
@@ -274,10 +296,11 @@
             shape((doc_rows, LANES), F32),
             pltpu.VMEM((n_doc, 256), BF16),
         ),
-        8,
-        smem=(0, 1),
+        5,
+        smem=(0,),
+        scratch=[pltpu.VMEM((n_cent, 256), BF16)],
         flops=2 * n_doc * n_cent * 256,
-    )(at, shard_mass, parts, ids, other_ids, docs, other_docs, cents)
+    )(at, parts, docs, other_docs, cents)
 
     def rows_out(dtype):
         return (shape((row_peers, doc_rows, LANES), dtype), small)
@@ -291,30 +314,23 @@
         parts = exchange(parts, COLS)
         parts, c = call(functools.partial(rows_after, target), rows_out(F32 if turn else BF16), 3, flops=2 * n_doc * n_cent)(parts, c, tile)
     parts = exchange(parts, ROWS)
-    chunk = n_cent // col_peers
     sums, pot = call(
         functools.partial(final_sums, n_y, n_core),
-        (shape((col_peers, chunk + 16, 256), BF16), shape((doc_rows // 2, LANES), F32)),
+        (shape((col_peers, 16, 2 * LANES * (chunk // 16) + LANES), BF16), shape((doc_rows // 2, LANES), F32)),
         7,
         smem=(0,),
         scratch=[pltpu.VMEM((n_cent, n_doc), BF16)],
         flops=2 * n_doc * n_cent * 256,
     )(at, parts, w, f, c, tile, docs_all)
     sums = exchange(sums, COLS)
-    new = call(divide, shape((n_y, chunk, 256), BF16), 2, smem=(0,), scratch=[pltpu.VMEM((LANES, LANES), F32)])(half, sums)
-    own = exchange(new, "y").reshape(n_y * chunk, 256)
-    by_zl = lax.ppermute(own, "zl", swap)
-    by_core = lax.ppermute(own, "core", swap)
-    by_both = lax.ppermute(by_zl, "core", swap)
-    anywhere = pl.BlockSpec(memory_space=pl.ANY)
+    new = call(divide, shape((n_y * n_zl, chunk, 256), BF16), 2, smem=(0,), scratch=[pltpu.VMEM((LANES, LANES), F32)])(half, sums)
+    own = exchange(new, ("y", "zl")).reshape(n_y * n_zl * chunk, 256)
+    other = lax.ppermute(own, "core", swap)
+    placed = shape((cents.shape[0], 256), BF16)
+    new = call(place_own, placed, 2, in_specs=[smem, any_space], out_specs=any_space, scratch=[pltpu.SemaphoreType.DMA])(at, own)
     new = call(
-        assemble,
-        shape((cents.shape[0], 256), BF16),
-        5,
-        in_specs=[pl.BlockSpec(memory_space=pltpu.SMEM)] + [anywhere] * 4,
-        out_specs=anywhere,
-        scratch=[pltpu.SemaphoreType.DMA((4,))],
-    )(at, own, by_zl, by_core, by_both)
+        place_other, placed, 3, in_specs=[smem, any_space, any_space], out_specs=any_space, scratch=[pltpu.SemaphoreType.DMA], alias={2: 0}
+    )(at, other, new)
     return new, pot.reshape(-1)
 
 

time: 189 us -> 184 us (0.974)
  starting transfers between devices: 34 us -> 26.7 us
  blocking collectives: 97.7 us -> 101 us
  local copies, waits for them, and re-layouts: 5.87 us -> 3.6 us
    ppermute x4 -> x1, starting transfers between devices: 11.8 us -> 4.5 us  [per_device(): other = lax.ppermute(own, 'core', swap)]
    ppermute x4 -> x1, waiting for transfers between devices: 6.69 us -> 0.16 us  [per_device(): other = lax.ppermute(own, 'core', swap)]
    all_to_all x2, waiting for transfers between devices: 24.5 us -> 30.2 us  [exchange(): return lax.all_to_all(x, axes, 0, 0)]
    all_to_all x7, blocking collectives: 97.7 us -> 101 us  [exchange(): return lax.all_to_all(x, axes, 0, 0)]
    unnamed x12 -> x8, local copies, waits for them, and re-layouts: 5.87 us -> 3.6 us
    pallas_call x5 -> x6, Pallas kernels: 14 us -> 15.4 us  [the longest x1 5.02 us: per_device(): call(functools.partial(first_rows, scale, row_peers), (shape((row_peers,...]
  transfers between devices with their start and end apart: 7 -> 4, of which waited for: 5 -> 3; matrix products, arithmetic and copies ran while one was open for 0% -> 0% of each run, Pallas kernels for 2% -> 1%
where the time goes in v2:
time: 184 us; the launch traced here: 183 us
  blocking collectives  101 us (55%)
  waiting for transfers between devices  30.4 us (17%)
  starting transfers between devices  26.7 us (15%)
  Pallas kernels  19.9 us (11%)
  local copies, waits for them, and re-layouts  3.6 us (2%)
    all_to_all x7, blocking collectives, exchange(): return lax.all_to_all(x, axes, 0, 0)  101 us
    all_to_all x2, waiting for transfers between devices, exchange(): return lax.all_to_all(x, axes, 0, 0)  30.2 us
    all_to_all x2, starting transfers between devices, exchange(): return lax.all_to_all(x, axes, 0, 0)  17.4 us
    pallas_call x1, Pallas kernels, per_device(): call(functools.partial(first_rows, scale, row_peers), (shape((row_peers,...  5.02 us
    ppermute x1, starting transfers between devices, per_device(): other_docs = lax.ppermute(docs, 'zl', swap)  4.83 us
    ppermute x1, starting transfers between devices, per_device(): other = lax.ppermute(own, 'core', swap)  4.5 us
    pallas_call x1, Pallas kernels, per_device(): call(functools.partial(final_sums, n_y, n_core), (shape((col_peers, 16, 2...  3.86 us
  transfers between devices with their start and end apart: 4, of which 3 were waited for; matrix products, arithmetic and copies ran while one was open for 0% of the time, Pallas kernels for 1%

profile of v2, /device:TPU:1, one launch (start us, length us, event | category | flops | bytes accessed | tf_op | source)
XLA Modules:
  0.0 182.9 jit_solution(3530714722223824990)
XLA Ops:
  0.6 0.0 copy-start
  0.6 1.2 copy-done
  1.9 0.0 copy-start.1
  1.9 1.0 copy-done.1
  2.9 0.0 copy-start.2
  2.9 0.7 copy-done.2
  3.6 0.0 copy-start.3
  3.6 0.7 copy-done.3
  4.2 5.0 %shard_map.59 = (f32[32,8,128]{2,1,0:T(8,128)}, bf16[1040,256]{1,0:T(8,128)(2,1)S(1)}, bf16[2048,256]{1,0:T(8,128)(2,1)S(1)}) custom-call(s32[64]{0:T(128)S(1)} %copy-done.3, s32[8,128]{1,0:T(8,128)S(1)} %bitcast.8, bf16[1024,256]{1,0:T(8,128)(2,1)S(1)} %copy-done.1, bf16[2048,256]{1,0:T(8,128)(2,1)S(1)} %copy-done), custom_call_target="tpu_custom_call" | custom-call | flops 1073741824 | bytes 1048576 | tf_op jit(solution)/shard_map/pallas_call | solution.py:274
  9.3 4.8 %collective-permute-start = (bf16[1040,256]{1,0:T(8,128)(2,1)S(1)}, bf16[1040,256]{1,0:T(8,128)(2,1)S(1)}, u32[]{:S(2)}, u32[]{:S(2)}) collective-permute-start(bf16[1040,256]{1,0:T(8,128)(2,1)S(1)} %get-tuple-element.20.docs_ref), channel_id=1, source_target_pairs={{0,32},{32,0},{1,33},{33,1},{2,34},{34,2},{3,35},{35,3},{4,36},{36... | collective-permute-start | bytes 1597448 | tf_op jit(solution)/shard_map/ppermute | solution.py:286
  14.1 12.0 %all-to-all-start = ((f32[32,8,128]{2,1,0:T(8,128)}), f32[32,8,128]{2,1,0:T(8,128)S(1)}, u32[]{:S(2)}, u32[]{:S(2)}) async-start(f32[32,8,128]{2,1,0:T(8,128)} %get-tuple-element.19), calls=%async_computation | async-start | bytes 262144 | tf_op jit(solution)/shard_map/all_to_all | solution.py:252
  26.1 0.1 pad_add_fusion.zl_ref.at_ref
  26.2 11.6 %all-to-all-done.parts_ref = f32[32,8,128]{2,1,0:T(8,128)S(1)} async-done(((f32[32,8,128]{2,1,0:T(8,128)}), f32[32,8,128]{2,1,0:T(8,128)S(1)}, u32[]{:S(2)}, u32[]{:S(2)}) %all-to-all-start) | async-done | bytes 131104 | tf_op jit(solution)/shard_map/all_to_all | solution.py:252
  37.7 0.0 collective-permute-done.other_ref
  37.7 3.6 %shard_map.60 = (f32[16,8,128]{2,1,0:T(8,128)S(1)}, f32[1024,2048]{1,0:T(8,128)S(1)}, f32[8,128]{1,0:T(8,128)S(1)}, f32[16,128]{1,0:T(8,128)S(1)}, f32[16,128]{1,0:T(8,128)S(1)}, /*index=5*/bf16[2048,256]{1,0:T(8,128)(2,1)S(1)}) custom-call(s32[2]{0:T(128)S(1)} %pad_add_fusion.zl_ref.at_ref, f32[32,8,128]{2,1,0:T(8,128)S(1)} %all-to-all-done.parts_ref, ...), custom_call_target="tpu_custom_call" | custom-call | flops 1073741824 | bytes 1048576 | tf_op jit(solution)/shard_map/pallas_call | solution.py:289
  41.4 17.0 %all_to_all.45.parts_ref = f32[16,8,128]{2,1,0:T(8,128)S(1)} all-to-all(f32[16,8,128]{2,1,0:T(8,128)S(1)} %get-tuple-element.22), channel_id=1, replica_groups=mesh['y'=8,'zl'=2,'core'=2,'zh'=4,'x'=4] {'y','core'}, dimensions={0} | all-to-all | bytes 131072 | tf_op jit(solution)/shard_map/all_to_all | solution.py:252
  58.4 1.0 shard_map.61
  59.5 14.2 %all_to_all.46.parts_ref = bf16[32,16,128]{2,1,0:T(8,128)(2,1)S(1)} all-to-all(bf16[32,16,128]{2,1,0:T(8,128)(2,1)S(1)} %get-tuple-element.25), channel_id=1, replica_groups=mesh['y'=8,'zl'=2,'core'=2,'zh'=4,'x'=4] {'zl','zh','x'}, dimensions={0} | all-to-all | bytes 262144 | tf_op jit(solution)/shard_map/all_to_all | solution.py:252
  73.7 0.7 shard_map.62
  74.4 11.8 %all_to_all.47.parts_ref = f32[16,8,128]{2,1,0:T(8,128)S(1)} all-to-all(f32[16,8,128]{2,1,0:T(8,128)S(1)} %shard_map.62), channel_id=1, replica_groups=mesh['y'=8,'zl'=2,'core'=2,'zh'=4,'x'=4] {'y','core'}, dimensions={0} | all-to-all | bytes 131072 | tf_op jit(solution)/shard_map/all_to_all | solution.py:252
  86.1 1.0 shard_map.63
  87.2 12.9 %all_to_all.48.parts_ref = bf16[32,16,128]{2,1,0:T(8,128)(2,1)S(1)} all-to-all(bf16[32,16,128]{2,1,0:T(8,128)(2,1)S(1)} %get-tuple-element.28), channel_id=1, replica_groups=mesh['y'=8,'zl'=2,'core'=2,'zh'=4,'x'=4] {'zl','zh','x'}, dimensions={0} | all-to-all | bytes 262144 | tf_op jit(solution)/shard_map/all_to_all | solution.py:252
  100.1 0.7 shard_map.64
  100.7 11.8 %all_to_all.49.parts_ref = f32[16,8,128]{2,1,0:T(8,128)S(1)} all-to-all(f32[16,8,128]{2,1,0:T(8,128)S(1)} %shard_map.64), channel_id=1, replica_groups=mesh['y'=8,'zl'=2,'core'=2,'zh'=4,'x'=4] {'y','core'}, dimensions={0} | all-to-all | bytes 131072 | tf_op jit(solution)/shard_map/all_to_all | solution.py:252
  112.5 1.0 shard_map.65
  113.6 15.1 %all_to_all.50.parts_ref = f32[32,16,128]{2,1,0:T(8,128)S(1)} all-to-all(f32[32,16,128]{2,1,0:T(8,128)S(1)} %get-tuple-element.30), channel_id=1, replica_groups=mesh['y'=8,'zl'=2,'core'=2,'zh'=4,'x'=4] {'zl','zh','x'}, dimensions={0} | all-to-all | bytes 524288 | tf_op jit(solution)/shard_map/all_to_all | solution.py:252
  128.6 3.9 %shard_map.66 = (bf16[16,16,1152]{2,1,0:T(8,128)(2,1)}, f32[8,128]{1,0:T(8,128)}) custom-call(s32[2]{0:T(128)S(1)} %pad_add_fusion.zl_ref.at_ref, f32[32,16,128]{2,1,0:T(8,128)S(1)} %all_to_all.50.parts_ref, f32[16,128]{1,0:T(8,128)S(1)} %get-tuple-element.26.w_ref, f32[16,128]{1,0:T(8,128)S(1)} %get-tuple-element.31.f_ref, ...), custom_call_target="tpu_custom_call" | custom-call | flops 1073741824 | bytes 1048576 | tf_op jit(solution)/shard_map/pallas_call | solution.py:317
  132.5 5.4 %all-to-all-start.7 = ((bf16[16,16,1152]{2,1,0:T(8,128)(2,1)}), bf16[16,16,1152]{2,1,0:T(8,128)(2,1)S(1)}, u32[]{:S(2)}, u32[]{:S(2)}) async-start(bf16[16,16,1152]{2,1,0:T(8,128)(2,1)} %get-tuple-element.34), calls=%async_computation.7 | async-start | bytes 1179648 | tf_op jit(solution)/shard_map/all_to_all | solution.py:252
  137.9 18.6 %all-to-all-done.7.parts_ref = bf16[16,16,1152]{2,1,0:T(8,128)(2,1)S(1)} async-done(((bf16[16,16,1152]{2,1,0:T(8,128)(2,1)}), bf16[16,16,1152]{2,1,0:T(8,128)(2,1)S(1)}, u32[]{:S(2)}, u32[]{:S(2)}) %all-to-all-start.7) | async-done | bytes 589856 | tf_op jit(solution)/shard_map/all_to_all | solution.py:252
  156.5 0.2 shard_map.67
  156.7 18.6 %all_to_all.51 = bf16[16,64,256]{2,1,0:T(8,128)(2,1)S(1)} all-to-all(bf16[16,64,256]{2,1,0:T(8,128)(2,1)S(1)} %shard_map.67), channel_id=1, replica_groups=mesh['y'=8,'zl'=2,'core'=2,'zh'=4,'x'=4] {'y','zl'}, dimensions={0} | all-to-all | bytes 1048576 | tf_op jit(solution)/shard_map/all_to_all | solution.py:252
  175.3 4.5 %collective-permute-start.1 = (bf16[1024,256]{1,0:T(8,128)(2,1)S(1)}, bf16[1024,256]{1,0:T(8,128)(2,1)S(1)}, u32[]{:S(2)}, u32[]{:S(2)}) collective-permute-start(bf16[1024,256]{1,0:T(8,128)(2,1)S(1)} %bitcast.6), channel_id=1, source_target_pairs={{0,16},{16,0},{1,17},{17,1},{2,18},{18,2},{3,19},{19,3},{4,20},{20... | collective-permute-start | bytes 1572872 | tf_op jit(solution)/shard_map/ppermute | solution.py:328
  179.9 1.3 shard_map.68._
  181.2 0.2 collective-permute-done.1.x_ref
  181.4 1.3 shard_map.69
Async XLA Ops:
  0.6 1.2 copy-start
  1.9 1.0 copy-start.1
  2.9 0.7 copy-start.2
  3.6 0.7 copy-start.3
  9.3 28.5 %collective-permute-start = (bf16[1040,256]{1,0:T(8,128)(2,1)S(1)}, bf16[1040,256]{1,0:T(8,128)(2,1)S(1)}, u32[]{:S(2)}, u32[]{:S(2)}) collective-permute-start(bf16[1040,256]{1,0:T(8,128)(2,1)S(1)} %get-tuple-element.20.docs_ref), channel_id=1, source_target_pairs={{0,32},{32,0},{1,33},{33,1},{2,34},{34,2},{3,35},{35,3},{4,36},{36... | collective-permute-start | bytes 1597448 | tf_op jit(solution)/shard_map/ppermute | solution.py:286
  14.1 23.6 %all-to-all-start = ((f32[32,8,128]{2,1,0:T(8,128)}), f32[32,8,128]{2,1,0:T(8,128)S(1)}, u32[]{:S(2)}, u32[]{:S(2)}) async-start(f32[32,8,128]{2,1,0:T(8,128)} %get-tuple-element.19), calls=%async_computation | async-start | bytes 262144 | tf_op jit(solution)/shard_map/all_to_all | solution.py:252
  132.5 24.0 %all-to-all-start.7 = ((bf16[16,16,1152]{2,1,0:T(8,128)(2,1)}), bf16[16,16,1152]{2,1,0:T(8,128)(2,1)S(1)}, u32[]{:S(2)}, u32[]{:S(2)}) async-start(bf16[16,16,1152]{2,1,0:T(8,128)(2,1)} %get-tuple-element.34), calls=%async_computation.7 | async-start | bytes 1179648 | tf_op jit(solution)/shard_map/all_to_all | solution.py:252
  175.3 6.0 %collective-permute-start.1 = (bf16[1024,256]{1,0:T(8,128)(2,1)S(1)}, bf16[1024,256]{1,0:T(8,128)(2,1)S(1)}, u32[]{:S(2)}, u32[]{:S(2)}) collective-permute-start(bf16[1024,256]{1,0:T(8,128)(2,1)S(1)} %bitcast.6), channel_id=1, source_target_pairs={{0,16},{16,0},{1,17},{17,1},{2,18},{18,2},{3,19},{19,3},{4,20},{20... | collective-permute-start | bytes 1572872 | tf_op jit(solution)/shard_map/ppermute | solution.py:328

commit v3 on v2

--- a/solution.py
+++ b/solution.py
@@ -57,7 +57,7 @@
 
 
 def first_rows(
-    scale, peers, mass_ref, ids_ref, docs_hbm, cents_hbm, out_ref, docs_ref, cents_ref, sems
+    scale, mass_hbm, ids_hbm, docs_hbm, cents_hbm, out_ref, docs_ref, cents_ref, mass_ref, ids_ref, sems
 ):
     n_doc, n_cent = docs_hbm.shape[0], cents_hbm.shape[0]
     block = 512
@@ -66,11 +66,10 @@
     for q in range(steps):
         rows = pl.ds(q * block, block)
         copies.append(pltpu.make_async_copy(cents_hbm.at[rows, :], cents_ref.at[rows, :], sems.at[q]))
+    copies.append(pltpu.make_async_copy(mass_hbm, mass_ref, sems.at[steps + 1]))
+    copies.append(pltpu.make_async_copy(ids_hbm, ids_ref, sems.at[steps + 2]))
     for copy in copies:
         copy.start()
-    w = weights_of(ids_ref[...], mass_ref)
-    pad = jnp.concatenate([jnp.concatenate([w, w], axis=0)] * 2, axis=1)
-    docs_ref[n_doc : n_doc + 16, :] = pad.astype(BF16)
     copies[0].wait()
     groups = n_doc // 256
     tops = [jnp.full((8, 256), -jnp.inf, F32)] * groups
@@ -89,6 +88,11 @@
         lse = top + jnp.log2(jnp.sum(totals[g] * jnp.exp2(tops[g] - top), axis=0, keepdims=True))
         rows += [lse[:, 0:LANES], lse[:, LANES:256]]
     out_ref[...] = jnp.broadcast_to(jnp.concatenate(rows, axis=0)[None], out_ref.shape)
+    copies[steps + 1].wait()
+    copies[steps + 2].wait()
+    w = weights_of(ids_ref[...], mass_ref)
+    pad = jnp.concatenate([jnp.concatenate([w, w], axis=0)] * 2, axis=1)
+    docs_ref[n_doc : n_doc + 16, :] = pad.astype(BF16)
 
 
 def first_columns(
@@ -182,41 +186,57 @@
     out_ref[...] = jnp.broadcast_to(out[None], out_ref.shape).astype(out_ref.dtype)
 
 
-def final_sums(n_y, n_core, zl_ref, parts_ref, w_ref, f_ref, c_ref, tile_ref, docs_ref, out_ref, pot_ref, p_ref):
-    n_cent, n_doc = tile_ref.shape
+def half_sums(side, u, c_ref, tile_ref, docs_ref, out_ref, p_ref):
+    n_half, n_doc = p_ref.shape
     groups = n_doc // LANES
-    u = w_ref[...] / jnp.sum(parts_ref[...], axis=0)
-    pot = (f_ref[...] + jnp.log2(u)) * LN2
-    pot_ref[...] = jnp.where(zl_ref[0] == 0, pot[0:8, :], pot[8:16, :])
-    cols = to_columns(c_ref[...])
+    blocks = n_half // LANES
+    cols = to_columns(c_ref[pl.ds(side * blocks, blocks), :])
+    base = pl.multiple_of(side * n_half, n_half)
     lane = lane_iota()
     masses = jnp.zeros((LANES, LANES), F32)
-    for r in range(n_cent // LANES):
-        rows = slice(r * LANES, (r + 1) * LANES)
+    for r in range(blocks):
+        rows = pl.ds(pl.multiple_of(base + r * LANES, LANES), LANES)
         col = jnp.broadcast_to(cols[:, r : r + 1], (LANES, LANES))
         total = jnp.zeros((LANES, LANES), F32)
         for g in range(groups):
             lanes = slice(g * LANES, (g + 1) * LANES)
             p = tile_ref[rows, lanes] * u[g : g + 1, :] * col
             total = total + p
-            p_ref[rows, lanes] = p.astype(BF16)
+            p_ref[r * LANES : (r + 1) * LANES, lanes] = p.astype(BF16)
         masses = jnp.where(lane == r, jnp.sum(total, axis=1, keepdims=True), masses)
     mass = masses.T[0:8, :]
+    out_ref[n_half : n_half + 8, :] = jnp.concatenate([mass, mass], axis=1)
+    for b in range(n_half // 256):
+        rows = slice(b * 256, (b + 1) * 256)
+        out_ref[rows, :] = jnp.dot(p_ref[rows, :], docs_ref[...], preferred_element_type=F32)
+
+
+def final_other(at_ref, parts_ref, w_ref, f_ref, c_ref, tile_ref, docs_ref, out_ref, pot_ref, u_ref, p_ref):
+    u = w_ref[...] / jnp.sum(parts_ref[...].astype(F32), axis=0)
+    u_ref[...] = u
+    pot = (f_ref[...] + jnp.log2(u)) * LN2
+    pot_ref[...] = jnp.where(at_ref[0] == 0, pot[0:8, :], pot[8:16, :])
+    half_sums(1 - at_ref[1], u, c_ref, tile_ref, docs_ref, out_ref, p_ref)
+
+
+def final_own(at_ref, u_ref, c_ref, tile_ref, docs_ref, out_ref, p_ref):
+    half_sums(at_ref[1], u_ref[...], c_ref, tile_ref, docs_ref, out_ref, p_ref)
+
+
+def final_join(own_ref, other_ref, out_ref):
+    peers = out_ref.shape[0]
+    n_half = own_ref.shape[0] - 8
+    chunk = n_half // peers
+    mass = own_ref[n_half:, 0:LANES] + other_ref[n_half:, 0:LANES]
     high = mass.astype(BF16).astype(F32)
     low = mass - high
-    chunk = n_cent // (n_y * n_core)
-    for b in range(n_cent // 256):
-        sums = jnp.dot(p_ref[b * 256 : (b + 1) * 256, :], docs_ref[...], preferred_element_type=F32).astype(BF16)
-        for k in range(256 // chunk):
-            q = b * (256 // chunk) + k
-            peer = (q % n_y) * n_core + q // n_y
-            for i in range(chunk // 16):
-                for h in range(2):
-                    at = (i * 2 + h) * LANES
-                    out_ref[peer, :, at : at + LANES] = sums[k * chunk + i * 16 : k * chunk + (i + 1) * 16, h * LANES : (h + 1) * LANES]
-            r = q * chunk // LANES
-            pair = [jnp.broadcast_to(x[r : r + 1, :], (8, LANES)) for x in (high, low)]
-            out_ref[peer, :, 2 * LANES * (chunk // 16) :] = jnp.concatenate(pair, axis=0).astype(BF16)
+    for q in range(peers):
+        for i in range(chunk // 16):
+            rows = slice(q * chunk + i * 16, q * chunk + (i + 1) * 16)
+            out_ref[q, :, i * 256 : (i + 1) * 256] = (own_ref[rows, :] + other_ref[rows, :]).astype(BF16)
+        r = q * chunk // LANES
+        pair = [jnp.broadcast_to(x[r : r + 1, :], (8, LANES)) for x in (high, low)]
+        out_ref[q, :, 256 * (chunk // 16) :] = jnp.concatenate(pair, axis=0).astype(BF16)
 
 
 def divide(half_ref, parts_ref, out_ref, mass_ref):
@@ -269,20 +289,20 @@
     small = shape((cent_rows, LANES), F32)
 
     any_space = pl.BlockSpec(memory_space=pl.ANY)
-    vmem = pl.BlockSpec(memory_space=pltpu.VMEM)
+    hbm = pl.BlockSpec(memory_space=pltpu.HBM)
     smem = pl.BlockSpec(memory_space=pltpu.SMEM)
     parts, docs, cents = call(
-        functools.partial(first_rows, scale, row_peers),
+        functools.partial(first_rows, scale),
         (
             shape((row_peers, doc_rows // 2, LANES), F32),
             pltpu.VMEM((docs.shape[0] + 16, 256), BF16),
             pltpu.VMEM(cents.shape, BF16),
         ),
         4,
-        in_specs=[smem, vmem, any_space, any_space],
-        scratch=[pltpu.SemaphoreType.DMA((5,))],
+        in_specs=[hbm] * 4,
+        scratch=[pltpu.SMEM(shard_mass.shape, jnp.int32), pltpu.VMEM((doc_rows // 2, LANES), jnp.int32), pltpu.SemaphoreType.DMA((7,))],
         flops=2 * docs.shape[0] * cents.shape[0] * 256,
-    )(shard_mass, shard_ids.reshape(-1, LANES), docs, cents)
+    )(*[pltpu.with_memory_space_constraint(x, pltpu.HBM) for x in (shard_mass, shard_ids.reshape(-1, LANES), docs, cents)])
     other_docs = lax.ppermute(docs, "zl", swap)
     parts = exchange(parts, ROWS)
     chunk = n_cent // col_peers
@@ -302,27 +322,32 @@
         flops=2 * n_doc * n_cent * 256,
     )(at, parts, docs, other_docs, cents)
 
-    def rows_out(dtype):
-        return (shape((row_peers, doc_rows, LANES), dtype), small)
-
+    rows_out = (shape((row_peers, doc_rows, LANES), BF16), small)
     parts = exchange(parts, COLS)
     log_target = math.log2(target)
-    parts, c = call(functools.partial(rows_after_first, log_target), rows_out(BF16), 3, flops=2 * n_doc * n_cent)(parts, top, tile)
+    parts, c = call(functools.partial(rows_after_first, log_target), rows_out, 3, flops=2 * n_doc * n_cent)(parts, top, tile)
     for turn in range(2):
         parts = exchange(parts, ROWS)
         parts = call(columns_after, shape((col_peers, cent_rows, LANES), F32), 4, flops=2 * n_doc * n_cent)(parts, w, c, tile)
         parts = exchange(parts, COLS)
-        parts, c = call(functools.partial(rows_after, target), rows_out(F32 if turn else BF16), 3, flops=2 * n_doc * n_cent)(parts, c, tile)
+        parts, c = call(functools.partial(rows_after, target), rows_out, 3, flops=2 * n_doc * n_cent)(parts, c, tile)
     parts = exchange(parts, ROWS)
-    sums, pot = call(
-        functools.partial(final_sums, n_y, n_core),
-        (shape((col_peers, 16, 2 * LANES * (chunk // 16) + LANES), BF16), shape((doc_rows // 2, LANES), F32)),
+    n_half = n_cent // n_core
+    half_flops = 2 * n_doc * n_half * 256
+    part_shape = pltpu.VMEM((n_half + 8, 256), F32)
+    p_scratch = [pltpu.VMEM((n_half, n_doc), BF16)]
+    for_other, pot, u = call(
+        final_other,
+        (part_shape, shape((doc_rows // 2, LANES), F32), shape((doc_rows, LANES), F32)),
         7,
         smem=(0,),
-        scratch=[pltpu.VMEM((n_cent, n_doc), BF16)],
-        flops=2 * n_doc * n_cent * 256,
+        scratch=p_scratch,
+        flops=half_flops,
     )(at, parts, w, f, c, tile, docs_all)
-    sums = exchange(sums, COLS)
+    from_other = lax.ppermute(for_other, "core", swap)
+    for_own = call(final_own, part_shape, 5, smem=(0,), scratch=p_scratch, flops=half_flops)(at, u, c, tile, docs_all)
+    sums = call(final_join, shape((n_y, 16, 2 * LANES * (chunk // 16) + LANES), BF16), 2)(for_own, from_other)
+    sums = exchange(sums, "y")
     new = call(divide, shape((n_y * n_zl, chunk, 256), BF16), 2, smem=(0,), scratch=[pltpu.VMEM((LANES, LANES), F32)])(half, sums)
     own = exchange(new, ("y", "zl")).reshape(n_y * n_zl * chunk, 256)
     other = lax.ppermute(own, "core", swap)

time: 184 us -> 176 us (0.957)
  waiting for transfers between devices: 30.4 us -> 24.7 us
  local copies, waits for them, and re-layouts: 3.6 us -> 0 us
    all_to_all x2, waiting for transfers between devices: 30.2 us -> 24.5 us  [exchange(): return lax.all_to_all(x, axes, 0, 0)]
    unnamed x8 -> x0, local copies, waits for them, and re-layouts: 3.6 us -> none
    ppermute x0 -> x1, starting transfers between devices: none -> 3.45 us  [per_device(): from_other = lax.ppermute(for_other, 'core', swap)]
    all_to_all x2, starting transfers between devices: 17.4 us -> 15.4 us  [exchange(): return lax.all_to_all(x, axes, 0, 0)]
    all_to_all x7, blocking collectives: 101 us -> 99.4 us  [exchange(): return lax.all_to_all(x, axes, 0, 0)]
    pallas_call x5 -> x7, Pallas kernels: 12 us -> 13.8 us  [the longest x1 5.52 us: per_device(): call(functools.partial(first_rows, scale), (shape((row_peers, doc_rows //...]
  transfers between devices with their start and end apart: 4 -> 5, of which waited for: 3 -> 3; matrix products, arithmetic and copies ran while one was open for 0% -> 0% of each run, Pallas kernels for 1% -> 2%
where the time goes in v3:
time: 176 us; the launch traced here: 175 us
  blocking collectives  99.4 us (56%)
  starting transfers between devices  28.3 us (16%)
  waiting for transfers between devices  24.7 us (14%)
  Pallas kernels  21.6 us (12%)
    all_to_all x7, blocking collectives, exchange(): return lax.all_to_all(x, axes, 0, 0)  99.4 us
    all_to_all x2, waiting for transfers between devices, exchange(): return lax.all_to_all(x, axes, 0, 0)  24.5 us
    all_to_all x2, starting transfers between devices, exchange(): return lax.all_to_all(x, axes, 0, 0)  15.4 us
    pallas_call x1, Pallas kernels, per_device(): call(functools.partial(first_rows, scale), (shape((row_peers, doc_rows //...  5.52 us
    ppermute x1, starting transfers between devices, per_device(): other_docs = lax.ppermute(docs, 'zl', swap)  4.83 us
    ppermute x1, starting transfers between devices, per_device(): other = lax.ppermute(own, 'core', swap)  4.57 us
    pallas_call x1, Pallas kernels, per_device(): call(functools.partial(first_columns, scale, chunk), (shape((col_peers, c...  3.65 us
  transfers between devices with their start and end apart: 5, of which 3 were waited for; matrix products, arithmetic and copies ran while one was open for 0% of the time, Pallas kernels for 2%

profile of v3, /device:TPU:1, one launch (start us, length us, event | category | flops | bytes accessed | tf_op | source)
XLA Modules:
  0.0 175.0 jit_solution(6001204760242472921)
XLA Ops:
  0.6 5.5 %shard_map.59 = (f32[32,8,128]{2,1,0:T(8,128)}, bf16[1040,256]{1,0:T(8,128)(2,1)S(1)}, bf16[2048,256]{1,0:T(8,128)(2,1)S(1)}) custom-call(s32[64]{0:T(128)} %mass_hbm.1, s32[8,128]{1,0:T(8,128)} %bitcast.8, bf16[1024,256]{1,0:T(8,128)(2,1)} %docs_hbm.1, bf16[2048,256]{1,0:T(8,128)(2,1)} %cents_hbm.1), custom_call_target="tpu_custom_call" | custom-call | flops 1073741824 | bytes 1048576 | tf_op jit(solution)/shard_map/pallas_call | solution.py:294
  6.2 4.8 %collective-permute-start = (bf16[1040,256]{1,0:T(8,128)(2,1)S(1)}, bf16[1040,256]{1,0:T(8,128)(2,1)S(1)}, u32[]{:S(2)}, u32[]{:S(2)}) collective-permute-start(bf16[1040,256]{1,0:T(8,128)(2,1)S(1)} %get-tuple-element.21.docs_ref), channel_id=1, source_target_pairs={{0,32},{32,0},{1,33},{33,1},{2,34},{34,2},{3,35},{35,3},{4,36},{36... | collective-permute-start | bytes 1597448 | tf_op jit(solution)/shard_map/ppermute | solution.py:306
  11.0 12.0 %all-to-all-start = ((f32[32,8,128]{2,1,0:T(8,128)}), f32[32,8,128]{2,1,0:T(8,128)S(1)}, u32[]{:S(2)}, u32[]{:S(2)}) async-start(f32[32,8,128]{2,1,0:T(8,128)} %get-tuple-element.20), calls=%async_computation | async-start | bytes 262144 | tf_op jit(solution)/shard_map/all_to_all | solution.py:272
  23.0 0.1 pad_add_fusion.zl_ref.at_ref
  23.1 11.5 %all-to-all-done.parts_ref = f32[32,8,128]{2,1,0:T(8,128)S(1)} async-done(((f32[32,8,128]{2,1,0:T(8,128)}), f32[32,8,128]{2,1,0:T(8,128)S(1)}, u32[]{:S(2)}, u32[]{:S(2)}) %all-to-all-start) | async-done | bytes 131104 | tf_op jit(solution)/shard_map/all_to_all | solution.py:272
  34.6 0.0 collective-permute-done.other_ref
  34.6 3.6 %shard_map.60 = (f32[16,8,128]{2,1,0:T(8,128)S(1)}, f32[1024,2048]{1,0:T(8,128)S(1)}, f32[8,128]{1,0:T(8,128)S(1)}, f32[16,128]{1,0:T(8,128)S(1)}, f32[16,128]{1,0:T(8,128)S(1)}, /*index=5*/bf16[2048,256]{1,0:T(8,128)(2,1)S(1)}) custom-call(s32[2]{0:T(128)S(1)} %pad_add_fusion.zl_ref.at_ref, f32[32,8,128]{2,1,0:T(8,128)S(1)} %all-to-all-done.parts_ref, ...), custom_call_target="tpu_custom_call" | custom-call | flops 1073741824 | bytes 1048576 | tf_op jit(solution)/shard_map/pallas_call | solution.py:309
  38.3 17.0 %all_to_all.45.parts_ref = f32[16,8,128]{2,1,0:T(8,128)S(1)} all-to-all(f32[16,8,128]{2,1,0:T(8,128)S(1)} %get-tuple-element.23), channel_id=1, replica_groups=mesh['y'=8,'zl'=2,'core'=2,'zh'=4,'x'=4] {'y','core'}, dimensions={0} | all-to-all | bytes 131072 | tf_op jit(solution)/shard_map/all_to_all | solution.py:272
  55.3 1.0 shard_map.61
  56.3 14.2 %all_to_all.46.parts_ref = bf16[32,16,128]{2,1,0:T(8,128)(2,1)S(1)} all-to-all(bf16[32,16,128]{2,1,0:T(8,128)(2,1)S(1)} %get-tuple-element.26), channel_id=1, replica_groups=mesh['y'=8,'zl'=2,'core'=2,'zh'=4,'x'=4] {'zl','zh','x'}, dimensions={0} | all-to-all | bytes 262144 | tf_op jit(solution)/shard_map/all_to_all | solution.py:272
  70.6 0.7 shard_map.62
  71.2 11.8 %all_to_all.47.parts_ref = f32[16,8,128]{2,1,0:T(8,128)S(1)} all-to-all(f32[16,8,128]{2,1,0:T(8,128)S(1)} %shard_map.62), channel_id=1, replica_groups=mesh['y'=8,'zl'=2,'core'=2,'zh'=4,'x'=4] {'y','core'}, dimensions={0} | all-to-all | bytes 131072 | tf_op jit(solution)/shard_map/all_to_all | solution.py:272
  83.0 1.0 shard_map.63
  84.1 12.9 %all_to_all.48.parts_ref = bf16[32,16,128]{2,1,0:T(8,128)(2,1)S(1)} all-to-all(bf16[32,16,128]{2,1,0:T(8,128)(2,1)S(1)} %get-tuple-element.29), channel_id=1, replica_groups=mesh['y'=8,'zl'=2,'core'=2,'zh'=4,'x'=4] {'zl','zh','x'}, dimensions={0} | all-to-all | bytes 262144 | tf_op jit(solution)/shard_map/all_to_all | solution.py:272
  97.0 0.7 shard_map.64
  97.6 11.8 %all_to_all.49.parts_ref = f32[16,8,128]{2,1,0:T(8,128)S(1)} all-to-all(f32[16,8,128]{2,1,0:T(8,128)S(1)} %shard_map.64), channel_id=1, replica_groups=mesh['y'=8,'zl'=2,'core'=2,'zh'=4,'x'=4] {'y','core'}, dimensions={0} | all-to-all | bytes 131072 | tf_op jit(solution)/shard_map/all_to_all | solution.py:272
  109.4 1.0 shard_map.65
  110.5 12.9 %all_to_all.50.parts_ref = bf16[32,16,128]{2,1,0:T(8,128)(2,1)S(1)} all-to-all(bf16[32,16,128]{2,1,0:T(8,128)(2,1)S(1)} %get-tuple-element.31), channel_id=1, replica_groups=mesh['y'=8,'zl'=2,'core'=2,'zh'=4,'x'=4] {'zl','zh','x'}, dimensions={0} | all-to-all | bytes 262144 | tf_op jit(solution)/shard_map/all_to_all | solution.py:272
  123.4 2.4 %shard_map.66 = (f32[520,256]{1,0:T(8,128)S(1)}, f32[8,128]{1,0:T(8,128)}, f32[16,128]{1,0:T(8,128)S(1)}) custom-call(s32[2]{0:T(128)S(1)} %pad_add_fusion.zl_ref.at_ref, bf16[32,16,128]{2,1,0:T(8,128)(2,1)S(1)} %all_to_all.50.parts_ref, f32[16,128]{1,0:T(8,128)S(1)} %get-tuple-element.27.w_ref, f32[16,128]{1,0:T(8,128)S(1)} %get-tuple-element.32.f_ref, ...), custom_call_target="tpu_custom_call" | custom-call | flops 536870912 | bytes 1048576 | tf_op jit(solution)/shard_map/pallas_call | solution.py:339
  125.8 3.5 %collective-permute-start.1 = (f32[520,256]{1,0:T(8,128)S(1)}, f32[520,256]{1,0:T(8,128)S(1)}, u32[]{:S(2)}, u32[]{:S(2)}) collective-permute-start(f32[520,256]{1,0:T(8,128)S(1)} %get-tuple-element.36), channel_id=1, source_target_pairs={{0,16},{16,0},{1,17},{17,1},{2,18},{18,2},{3,19},{19,3},{4,20},{20... | collective-permute-start | bytes 1597448 | tf_op jit(solution)/shard_map/ppermute | solution.py:347
  129.2 1.9 %shard_map.67.own_ref = f32[520,256]{1,0:T(8,128)S(1)} custom-call(s32[2]{0:T(128)S(1)} %pad_add_fusion.zl_ref.at_ref, f32[16,128]{1,0:T(8,128)S(1)} %get-tuple-element.35.u_ref, f32[8,128]{1,0:T(8,128)S(1)} %get-tuple-element.33.c_ref, f32[1024,2048]{1,0:T(8,128)S(1)} %get-tuple-element.25.tile_ref, bf16[2048,256]{1,0:T(8,128)(2,1)S(1)} %get-tuple-element.34.docs_ref), custom_call_target="tpu_custom_call" | custom-call | flops 536870912 | bytes 1048576 | tf_op jit(solution)/shard_map/pallas_call | solution.py:348
  131.2 0.0 collective-permute-done.1.other_ref
  131.2 0.8 shard_map.68
  132.0 3.4 %all-to-all-start.7 = ((bf16[8,16,1152]{2,1,0:T(8,128)(2,1)}), bf16[8,16,1152]{2,1,0:T(8,128)(2,1)S(1)}, u32[]{:S(2)}, u32[]{:S(2)}) async-start(bf16[8,16,1152]{2,1,0:T(8,128)(2,1)} %shard_map.68), calls=%async_computation.7 | async-start | bytes 589824 | tf_op jit(solution)/shard_map/all_to_all | solution.py:272
  135.4 13.0 %all-to-all-done.7.parts_ref = bf16[8,16,1152]{2,1,0:T(8,128)(2,1)S(1)} async-done(((bf16[8,16,1152]{2,1,0:T(8,128)(2,1)}), bf16[8,16,1152]{2,1,0:T(8,128)(2,1)S(1)}, u32[]{:S(2)}, u32[]{:S(2)}) %all-to-all-start.7) | async-done | bytes 294944 | tf_op jit(solution)/shard_map/all_to_all | solution.py:272
  148.4 0.2 shard_map.69
  148.6 18.8 %all_to_all.51 = bf16[16,64,256]{2,1,0:T(8,128)(2,1)S(1)} all-to-all(bf16[16,64,256]{2,1,0:T(8,128)(2,1)S(1)} %shard_map.69), channel_id=1, replica_groups=mesh['y'=8,'zl'=2,'core'=2,'zh'=4,'x'=4] {'y','zl'}, dimensions={0} | all-to-all | bytes 1048576 | tf_op jit(solution)/shard_map/all_to_all | solution.py:272
  167.4 4.6 %collective-permute-start.2 = (bf16[1024,256]{1,0:T(8,128)(2,1)S(1)}, bf16[1024,256]{1,0:T(8,128)(2,1)S(1)}, u32[]{:S(2)}, u32[]{:S(2)}) collective-permute-start(bf16[1024,256]{1,0:T(8,128)(2,1)S(1)} %bitcast.6), channel_id=1, source_target_pairs={{0,16},{16,0},{1,17},{17,1},{2,18},{18,2},{3,19},{19,3},{4,20},{20... | collective-permute-start | bytes 1572872 | tf_op jit(solution)/shard_map/ppermute | solution.py:353
  172.0 1.3 shard_map.70._
  173.3 0.2 collective-permute-done.2.x_ref
  173.5 1.3 shard_map.71
Async XLA Ops:
  6.2 28.4 %collective-permute-start = (bf16[1040,256]{1,0:T(8,128)(2,1)S(1)}, bf16[1040,256]{1,0:T(8,128)(2,1)S(1)}, u32[]{:S(2)}, u32[]{:S(2)}) collective-permute-start(bf16[1040,256]{1,0:T(8,128)(2,1)S(1)} %get-tuple-element.21.docs_ref), channel_id=1, source_target_pairs={{0,32},{32,0},{1,33},{33,1},{2,34},{34,2},{3,35},{35,3},{4,36},{36... | collective-permute-start | bytes 1597448 | tf_op jit(solution)/shard_map/ppermute | solution.py:306
  11.0 23.6 %all-to-all-start = ((f32[32,8,128]{2,1,0:T(8,128)}), f32[32,8,128]{2,1,0:T(8,128)S(1)}, u32[]{:S(2)}, u32[]{:S(2)}) async-start(f32[32,8,128]{2,1,0:T(8,128)} %get-tuple-element.20), calls=%async_computation | async-start | bytes 262144 | tf_op jit(solution)/shard_map/all_to_all | solution.py:272
  125.8 5.4 %collective-permute-start.1 = (f32[520,256]{1,0:T(8,128)S(1)}, f32[520,256]{1,0:T(8,128)S(1)}, u32[]{:S(2)}, u32[]{:S(2)}) collective-permute-start(f32[520,256]{1,0:T(8,128)S(1)} %get-tuple-element.36), channel_id=1, source_target_pairs={{0,16},{16,0},{1,17},{17,1},{2,18},{18,2},{3,19},{19,3},{4,20},{20... | collective-permute-start | bytes 1597448 | tf_op jit(solution)/shard_map/ppermute | solution.py:347
  132.0 16.4 %all-to-all-start.7 = ((bf16[8,16,1152]{2,1,0:T(8,128)(2,1)}), bf16[8,16,1152]{2,1,0:T(8,128)(2,1)S(1)}, u32[]{:S(2)}, u32[]{:S(2)}) async-start(bf16[8,16,1152]{2,1,0:T(8,128)(2,1)} %shard_map.68), calls=%async_computation.7 | async-start | bytes 589824 | tf_op jit(solution)/shard_map/all_to_all | solution.py:272
  167.4 6.1 %collective-permute-start.2 = (bf16[1024,256]{1,0:T(8,128)(2,1)S(1)}, bf16[1024,256]{1,0:T(8,128)(2,1)S(1)}, u32[]{:S(2)}, u32[]{:S(2)}) collective-permute-start(bf16[1024,256]{1,0:T(8,128)(2,1)S(1)} %bitcast.6), channel_id=1, source_target_pairs={{0,16},{16,0},{1,17},{17,1},{2,18},{18,2},{3,19},{19,3},{4,20},{20... | collective-permute-start | bytes 1572872 | tf_op jit(solution)/shard_map/ppermute | solution.py:353

commit v4 on v3

--- a/solution.py
+++ b/solution.py
@@ -53,23 +53,26 @@
     def step(s, total):
         return jnp.where(ids == s, mass_ref[s].astype(F32), total)
 
-    return lax.fori_loop(0, mass_ref.shape[0], step, jnp.zeros(ids.shape, F32)) * 0.125
+    return lax.fori_loop(0, mass_ref.shape[0], step, jnp.zeros(ids.shape, F32), unroll=True) * 0.125
 
 
 def first_rows(
-    scale, mass_hbm, ids_hbm, docs_hbm, cents_hbm, out_ref, docs_ref, cents_ref, mass_ref, ids_ref, sems
+    scale, mass_hbm, ids_hbm, docs_hbm, cents_hbm, out_ref, docs_ref, cents_ref, w_ref, mass_ref, ids_ref, sems
 ):
     n_doc, n_cent = docs_hbm.shape[0], cents_hbm.shape[0]
     block = 512
     steps = n_cent // block
-    copies = [pltpu.make_async_copy(docs_hbm, docs_ref.at[0:n_doc, :], sems.at[steps])]
+    copies = [pltpu.make_async_copy(docs_hbm, docs_ref, sems.at[steps])]
     for q in range(steps):
         rows = pl.ds(q * block, block)
         copies.append(pltpu.make_async_copy(cents_hbm.at[rows, :], cents_ref.at[rows, :], sems.at[q]))
     copies.append(pltpu.make_async_copy(mass_hbm, mass_ref, sems.at[steps + 1]))
     copies.append(pltpu.make_async_copy(ids_hbm, ids_ref, sems.at[steps + 2]))
-    for copy in copies:
+    for copy in copies[-2:] + copies[:-2]:
         copy.start()
+    copies[steps + 1].wait()
+    copies[steps + 2].wait()
+    w_ref[...] = weights_of(ids_ref[...], mass_ref)
     copies[0].wait()
     groups = n_doc // 256
     tops = [jnp.full((8, 256), -jnp.inf, F32)] * groups
@@ -88,27 +91,21 @@
         lse = top + jnp.log2(jnp.sum(totals[g] * jnp.exp2(tops[g] - top), axis=0, keepdims=True))
         rows += [lse[:, 0:LANES], lse[:, LANES:256]]
     out_ref[...] = jnp.broadcast_to(jnp.concatenate(rows, axis=0)[None], out_ref.shape)
-    copies[steps + 1].wait()
-    copies[steps + 2].wait()
-    w = weights_of(ids_ref[...], mass_ref)
-    pad = jnp.concatenate([jnp.concatenate([w, w], axis=0)] * 2, axis=1)
-    docs_ref[n_doc : n_doc + 16, :] = pad.astype(BF16)
 
 
 def first_columns(
-    scale, chunk, zl_ref, parts_ref, docs_ref, other_ref, cents_ref,
+    scale, chunk, zl_ref, parts_ref, own_w_ref, other_w_ref, docs_ref, other_ref, cents_ref,
     out_ref, tile_ref, top_ref, f_ref, w_ref, docs_all_ref, half_ref,
 ):
     zl = zl_ref[0]
-    n_doc, n_cent = docs_ref.shape[0] - 16, cents_ref.shape[0] // 2
+    n_doc, n_cent = docs_ref.shape[0], cents_ref.shape[0] // 2
     groups = 2 * n_doc // LANES
-    docs_all_ref[pl.ds(pl.multiple_of(zl * n_doc, n_doc), n_doc), :] = docs_ref[0:n_doc, :]
-    docs_all_ref[pl.ds(pl.multiple_of((1 - zl) * n_doc, n_doc), n_doc), :] = other_ref[0:n_doc, :]
+    docs_all_ref[pl.ds(pl.multiple_of(zl * n_doc, n_doc), n_doc), :] = docs_ref[...]
+    docs_all_ref[pl.ds(pl.multiple_of((1 - zl) * n_doc, n_doc), n_doc), :] = other_ref[...]
     for q in range(n_cent // chunk):
         rows = pl.ds(pl.multiple_of(q * 2 * chunk + zl * chunk, chunk), chunk)
         half_ref[q * chunk : (q + 1) * chunk, :] = cents_ref[rows, :]
-    own = docs_ref[n_doc : n_doc + 16, 0:LANES].astype(F32)[0:8]
-    other = other_ref[n_doc : n_doc + 16, 0:LANES].astype(F32)[0:8]
+    own, other = own_w_ref[...], other_w_ref[...]
     w_ref[0:8, :] = jnp.where(zl == 0, own, other)
     w_ref[8:16, :] = jnp.where(zl == 0, other, own)
     half = parts_ref.shape[0] // 2
@@ -239,7 +236,7 @@
         out_ref[q, :, 256 * (chunk // 16) :] = jnp.concatenate(pair, axis=0).astype(BF16)
 
 
-def divide(half_ref, parts_ref, out_ref, mass_ref):
+def divide(at_ref, parts_ref, out_ref, mass_ref):
     total = parts_ref[0].astype(F32)
     for p in range(1, parts_ref.shape[0]):
         total = total + parts_ref[p].astype(F32)
@@ -247,7 +244,7 @@
     chunk = tiles * 8
     mass = total[0:8, tiles * LANES :] + total[8:16, tiles * LANES :]
     mass_ref[...] = to_columns(mass)
-    col = mass_ref[pl.ds(pl.multiple_of(half_ref[0] * chunk, chunk), chunk), :]
+    col = mass_ref[pl.ds(pl.multiple_of(at_ref[2] * chunk, chunk), chunk), :]
     for i in range(chunk // 16):
         pair = [total[:, (i * 2 + h) * LANES : (i * 2 + h + 1) * LANES] / col[i * 16 : (i + 1) * 16, :] for h in range(2)]
         new = jnp.concatenate(pair, axis=1).astype(BF16)
@@ -281,8 +278,7 @@
     target = 0.5 * (docs.shape[0] * n_y * n_zl * n_core) / (cents.shape[0] * n_zh * n_x)
     zl = lax.axis_index("zl")
     core = lax.axis_index("core")
-    at = jnp.stack([zl, core]).astype(jnp.int32)
-    half = (lax.axis_index("y") % 2).astype(jnp.int32).reshape(1)
+    at = jnp.stack([zl, core, lax.axis_index("y") & 1]).astype(jnp.int32)
     swap = [(0, 1), (1, 0)]
     shape = jax.ShapeDtypeStruct
     tile_shape = pltpu.VMEM((n_cent, n_doc), F32)
@@ -291,19 +287,21 @@
     any_space = pl.BlockSpec(memory_space=pl.ANY)
     hbm = pl.BlockSpec(memory_space=pltpu.HBM)
     smem = pl.BlockSpec(memory_space=pltpu.SMEM)
-    parts, docs, cents = call(
+    other_docs = lax.ppermute(docs, "zl", swap)
+    parts, docs, cents, own_w = call(
         functools.partial(first_rows, scale),
         (
             shape((row_peers, doc_rows // 2, LANES), F32),
-            pltpu.VMEM((docs.shape[0] + 16, 256), BF16),
+            pltpu.VMEM(docs.shape, BF16),
             pltpu.VMEM(cents.shape, BF16),
+            shape((doc_rows // 2, LANES), F32),
         ),
         4,
         in_specs=[hbm] * 4,
         scratch=[pltpu.SMEM(shard_mass.shape, jnp.int32), pltpu.VMEM((doc_rows // 2, LANES), jnp.int32), pltpu.SemaphoreType.DMA((7,))],
         flops=2 * docs.shape[0] * cents.shape[0] * 256,
     )(*[pltpu.with_memory_space_constraint(x, pltpu.HBM) for x in (shard_mass, shard_ids.reshape(-1, LANES), docs, cents)])
-    other_docs = lax.ppermute(docs, "zl", swap)
+    other_w = lax.ppermute(own_w, "zl", swap)
     parts = exchange(parts, ROWS)
     chunk = n_cent // col_peers
     parts, tile, top, f, w, docs_all = call(
@@ -316,11 +314,11 @@
             shape((doc_rows, LANES), F32),
             pltpu.VMEM((n_doc, 256), BF16),
         ),
-        5,
+        7,
         smem=(0,),
         scratch=[pltpu.VMEM((n_cent, 256), BF16)],
         flops=2 * n_doc * n_cent * 256,
-    )(at, parts, docs, other_docs, cents)
+    )(at, parts, own_w, other_w, docs, other_docs, cents)
 
     rows_out = (shape((row_peers, doc_rows, LANES), BF16), small)
     parts = exchange(parts, COLS)
@@ -348,7 +346,7 @@
     for_own = call(final_own, part_shape, 5, smem=(0,), scratch=p_scratch, flops=half_flops)(at, u, c, tile, docs_all)
     sums = call(final_join, shape((n_y, 16, 2 * LANES * (chunk // 16) + LANES), BF16), 2)(for_own, from_other)
     sums = exchange(sums, "y")
-    new = call(divide, shape((n_y * n_zl, chunk, 256), BF16), 2, smem=(0,), scratch=[pltpu.VMEM((LANES, LANES), F32)])(half, sums)
+    new = call(divide, shape((n_y * n_zl, chunk, 256), BF16), 2, smem=(0,), scratch=[pltpu.VMEM((LANES, LANES), F32)])(at, sums)
     own = exchange(new, ("y", "zl")).reshape(n_y * n_zl * chunk, 256)
     other = lax.ppermute(own, "core", swap)
     placed = shape((cents.shape[0], 256), BF16)

time: 176 us -> 171 us (0.972)
  waiting for transfers between devices: 24.7 us -> 6.34 us
  blocking collectives: 99.4 us -> 114 us
    all_to_all x2 -> x1, waiting for transfers between devices: 24.5 us -> 4.53 us  [exchange(): return lax.all_to_all(x, axes, 0, 0)]
    all_to_all x7 -> x8, blocking collectives: 99.4 us -> 114 us  [exchange(): return lax.all_to_all(x, axes, 0, 0)]
    all_to_all x2 -> x1, starting transfers between devices: 15.4 us -> 12 us  [exchange(): return lax.all_to_all(x, axes, 0, 0)]
    ppermute x0 -> x1, starting transfers between devices: none -> 3.15 us  [per_device(): other_w = lax.ppermute(own_w, 'zl', swap)]
  transfers between devices with their start and end apart: 5 -> 5, of which waited for: 3 -> 3; matrix products, arithmetic and copies ran while one was open for 0% -> 0% of each run, Pallas kernels for 2% -> 5%
where the time goes in v4:
time: 171 us; the launch traced here: 170 us
  blocking collectives  114 us (67%)
  starting transfers between devices  28.5 us (17%)
  Pallas kernels  20.4 us (12%)
  waiting for transfers between devices  6.34 us (4%)
    all_to_all x8, blocking collectives, exchange(): return lax.all_to_all(x, axes, 0, 0)  114 us
    all_to_all x1, starting transfers between devices, exchange(): return lax.all_to_all(x, axes, 0, 0)  12 us
    pallas_call x1, Pallas kernels, per_device(): call(functools.partial(first_rows, scale), (shape((row_peers, doc_rows //...  5.14 us
    ppermute x1, starting transfers between devices, per_device(): other = lax.ppermute(own, 'core', swap)  5.06 us
    ppermute x1, starting transfers between devices, per_device(): other_docs = lax.ppermute(docs, 'zl', swap)  4.83 us
    all_to_all x1, waiting for transfers between devices, exchange(): return lax.all_to_all(x, axes, 0, 0)  4.53 us
    pallas_call x1, Pallas kernels, per_device(): call(functools.partial(first_columns, scale, chunk), (shape((col_peers, c...  3.53 us
    ppermute x1, starting transfers between devices, per_device(): from_other = lax.ppermute(for_other, 'core', swap)  3.45 us
  transfers between devices with their start and end apart: 5, of which 3 were waited for; matrix products, arithmetic and copies ran while one was open for 0% of the time, Pallas kernels for 5%

profile of v4, /device:TPU:1, one launch (start us, length us, event | category | flops | bytes accessed | tf_op | source)
XLA Modules:
  0.0 170.3 jit_solution(14768245277408918302)
XLA Ops:
  0.6 4.8 %collective-permute-start.1 = (bf16[1024,256]{1,0:T(8,128)(2,1)}, bf16[1024,256]{1,0:T(8,128)(2,1)S(1)}, u32[]{:S(2)}, u32[]{:S(2)}) collective-permute-start(bf16[1024,256]{1,0:T(8,128)(2,1)} %docs_hbm.1), channel_id=1, source_target_pairs={{0,32},{32,0},{1,33},{33,1},{2,34},{34,2},{3,35},{35,3},{4,36},{36... | collective-permute-start | bytes 1572872 | tf_op jit(solution)/shard_map/ppermute | solution.py:290
  5.5 5.1 %shard_map.59 = (f32[32,8,128]{2,1,0:T(8,128)}, bf16[1024,256]{1,0:T(8,128)(2,1)S(1)}, bf16[2048,256]{1,0:T(8,128)(2,1)S(1)}, f32[8,128]{1,0:T(8,128)S(1)}) custom-call(s32[64]{0:T(128)} %mass_hbm.1, s32[8,128]{1,0:T(8,128)} %bitcast.8, bf16[1024,256]{1,0:T(8,128)(2,1)} %docs_hbm.1, bf16[2048,256]{1,0:T(8,128)(2,1)} %cents_hbm.1), custom_call_target="tpu_custom_call" | custom-call | flops 1073741824 | bytes 1048576 | tf_op jit(solution)/shard_map/pallas_call | solution.py:291
  10.6 12.0 %all-to-all-start = ((f32[32,8,128]{2,1,0:T(8,128)}), f32[32,8,128]{2,1,0:T(8,128)S(1)}, u32[]{:S(2)}, u32[]{:S(2)}) async-start(f32[32,8,128]{2,1,0:T(8,128)} %get-tuple-element.21), calls=%async_computation | async-start | bytes 262144 | tf_op jit(solution)/shard_map/all_to_all | solution.py:269
  22.6 3.1 %collective-permute-start = (f32[8,128]{1,0:T(8,128)S(1)}, f32[8,128]{1,0:T(8,128)S(1)}, u32[]{:S(2)}, u32[]{:S(2)}) collective-permute-start(f32[8,128]{1,0:T(8,128)S(1)} %get-tuple-element.22.own_w_ref), channel_id=1, source_target_pairs={{0,32},{32,0},{1,33},{33,1},{2,34},{34,2},{3,35},{35,3},{4,36},{36... | collective-permute-start | bytes 12296 | tf_op jit(solution)/shard_map/ppermute | solution.py:304
  25.8 0.1 pad_add_fusion.zl_ref.at_ref
  25.8 1.6 collective-permute-done.other_w_ref
  27.5 4.5 %all-to-all-done.parts_ref = f32[32,8,128]{2,1,0:T(8,128)S(1)} async-done(((f32[32,8,128]{2,1,0:T(8,128)}), f32[32,8,128]{2,1,0:T(8,128)S(1)}, u32[]{:S(2)}, u32[]{:S(2)}) %all-to-all-start) | async-done | bytes 131104 | tf_op jit(solution)/shard_map/all_to_all | solution.py:269
  32.0 0.0 collective-permute-done.1.other_ref
  32.0 3.5 %shard_map.60 = (f32[16,8,128]{2,1,0:T(8,128)S(1)}, f32[1024,2048]{1,0:T(8,128)S(1)}, f32[8,128]{1,0:T(8,128)S(1)}, f32[16,128]{1,0:T(8,128)S(1)}, f32[16,128]{1,0:T(8,128)S(1)}, /*index=5*/bf16[2048,256]{1,0:T(8,128)(2,1)S(1)}) custom-call(s32[3]{0:T(128)S(1)} %pad_add_fusion.zl_ref.at_ref, f32[32,8,128]{2,1,0:T(8,128)S(1)} %all-to-all-done.parts_ref, ...), custom_call_target="tpu_custom_call" | custom-call | flops 1073741824 | bytes 1048576 | tf_op jit(solution)/shard_map/pallas_call | solution.py:307
  35.5 17.2 %all_to_all.45.parts_ref = f32[16,8,128]{2,1,0:T(8,128)S(1)} all-to-all(f32[16,8,128]{2,1,0:T(8,128)S(1)} %get-tuple-element.25), channel_id=1, replica_groups=mesh['y'=8,'zl'=2,'core'=2,'zh'=4,'x'=4] {'y','core'}, dimensions={0} | all-to-all | bytes 131072 | tf_op jit(solution)/shard_map/all_to_all | solution.py:269
  52.8 0.9 shard_map.61
  53.7 14.1 %all_to_all.46.parts_ref = bf16[32,16,128]{2,1,0:T(8,128)(2,1)S(1)} all-to-all(bf16[32,16,128]{2,1,0:T(8,128)(2,1)S(1)} %get-tuple-element.28), channel_id=1, replica_groups=mesh['y'=8,'zl'=2,'core'=2,'zh'=4,'x'=4] {'zl','zh','x'}, dimensions={0} | all-to-all | bytes 262144 | tf_op jit(solution)/shard_map/all_to_all | solution.py:269
  67.7 0.7 shard_map.62
  68.4 11.8 %all_to_all.47.parts_ref = f32[16,8,128]{2,1,0:T(8,128)S(1)} all-to-all(f32[16,8,128]{2,1,0:T(8,128)S(1)} %shard_map.62), channel_id=1, replica_groups=mesh['y'=8,'zl'=2,'core'=2,'zh'=4,'x'=4] {'y','core'}, dimensions={0} | all-to-all | bytes 131072 | tf_op jit(solution)/shard_map/all_to_all | solution.py:269
  80.2 0.9 shard_map.63
  81.1 12.9 %all_to_all.48.parts_ref = bf16[32,16,128]{2,1,0:T(8,128)(2,1)S(1)} all-to-all(bf16[32,16,128]{2,1,0:T(8,128)(2,1)S(1)} %get-tuple-element.31), channel_id=1, replica_groups=mesh['y'=8,'zl'=2,'core'=2,'zh'=4,'x'=4] {'zl','zh','x'}, dimensions={0} | all-to-all | bytes 262144 | tf_op jit(solution)/shard_map/all_to_all | solution.py:269
  94.0 0.7 shard_map.64
  94.7 11.8 %all_to_all.49.parts_ref = f32[16,8,128]{2,1,0:T(8,128)S(1)} all-to-all(f32[16,8,128]{2,1,0:T(8,128)S(1)} %shard_map.64), channel_id=1, replica_groups=mesh['y'=8,'zl'=2,'core'=2,'zh'=4,'x'=4] {'y','core'}, dimensions={0} | all-to-all | bytes 131072 | tf_op jit(solution)/shard_map/all_to_all | solution.py:269
  106.4 0.9 shard_map.65
  107.3 12.9 %all_to_all.50.parts_ref = bf16[32,16,128]{2,1,0:T(8,128)(2,1)S(1)} all-to-all(bf16[32,16,128]{2,1,0:T(8,128)(2,1)S(1)} %get-tuple-element.33), channel_id=1, replica_groups=mesh['y'=8,'zl'=2,'core'=2,'zh'=4,'x'=4] {'zl','zh','x'}, dimensions={0} | all-to-all | bytes 262144 | tf_op jit(solution)/shard_map/all_to_all | solution.py:269
  120.2 2.4 %shard_map.66 = (f32[520,256]{1,0:T(8,128)S(1)}, f32[8,128]{1,0:T(8,128)}, f32[16,128]{1,0:T(8,128)S(1)}) custom-call(s32[3]{0:T(128)S(1)} %pad_add_fusion.zl_ref.at_ref, bf16[32,16,128]{2,1,0:T(8,128)(2,1)S(1)} %all_to_all.50.parts_ref, f32[16,128]{1,0:T(8,128)S(1)} %get-tuple-element.29.w_ref, f32[16,128]{1,0:T(8,128)S(1)} %get-tuple-element.34.f_ref, ...), custom_call_target="tpu_custom_call" | custom-call | flops 536870912 | bytes 1048576 | tf_op jit(solution)/shard_map/pallas_call | solution.py:337
  122.6 3.4 %collective-permute-start.2 = (f32[520,256]{1,0:T(8,128)S(1)}, f32[520,256]{1,0:T(8,128)S(1)}, u32[]{:S(2)}, u32[]{:S(2)}) collective-permute-start(f32[520,256]{1,0:T(8,128)S(1)} %get-tuple-element.38), channel_id=1, source_target_pairs={{0,16},{16,0},{1,17},{17,1},{2,18},{18,2},{3,19},{19,3},{4,20},{20... | collective-permute-start | bytes 1597448 | tf_op jit(solution)/shard_map/ppermute | solution.py:345
  126.1 1.9 %shard_map.67.own_ref = f32[520,256]{1,0:T(8,128)S(1)} custom-call(s32[3]{0:T(128)S(1)} %pad_add_fusion.zl_ref.at_ref, f32[16,128]{1,0:T(8,128)S(1)} %get-tuple-element.37.u_ref, f32[8,128]{1,0:T(8,128)S(1)} %get-tuple-element.35.c_ref, f32[1024,2048]{1,0:T(8,128)S(1)} %get-tuple-element.27.tile_ref, bf16[2048,256]{1,0:T(8,128)(2,1)S(1)} %get-tuple-element.36.docs_ref), custom_call_target="tpu_custom_call" | custom-call | flops 536870912 | bytes 1048576 | tf_op jit(solution)/shard_map/pallas_call | solution.py:346
  128.0 0.0 collective-permute-done.2.other_ref
  128.0 0.1 shard_map.68
  128.1 15.1 %all_to_all.51.parts_ref = bf16[8,16,1152]{2,1,0:T(8,128)(2,1)S(1)} all-to-all(bf16[8,16,1152]{2,1,0:T(8,128)(2,1)S(1)} %shard_map.68), channel_id=1, replica_groups=mesh['y'=8,'zl'=2,'core'=2,'zh'=4,'x'=4] {'y'}, dimensions={0} | all-to-all | bytes 589824 | tf_op jit(solution)/shard_map/all_to_all | solution.py:269
  143.1 0.7 shard_map.69
  143.8 18.3 %all_to_all.52 = bf16[16,64,256]{2,1,0:T(8,128)(2,1)S(1)} all-to-all(bf16[16,64,256]{2,1,0:T(8,128)(2,1)S(1)} %shard_map.69), channel_id=1, replica_groups=mesh['y'=8,'zl'=2,'core'=2,'zh'=4,'x'=4] {'y','zl'}, dimensions={0} | all-to-all | bytes 1048576 | tf_op jit(solution)/shard_map/all_to_all | solution.py:269
  162.2 5.1 %collective-permute-start.3 = (bf16[1024,256]{1,0:T(8,128)(2,1)S(1)}, bf16[1024,256]{1,0:T(8,128)(2,1)S(1)}, u32[]{:S(2)}, u32[]{:S(2)}) collective-permute-start(bf16[1024,256]{1,0:T(8,128)(2,1)S(1)} %bitcast.6), channel_id=1, source_target_pairs={{0,16},{16,0},{1,17},{17,1},{2,18},{18,2},{3,19},{19,3},{4,20},{20... | collective-permute-start | bytes 1572872 | tf_op jit(solution)/shard_map/ppermute | solution.py:351
  167.2 1.3 shard_map.70._
  168.6 0.2 collective-permute-done.3.x_ref
  168.8 1.3 shard_map.71
Async XLA Ops:
  0.6 31.4 %collective-permute-start.1 = (bf16[1024,256]{1,0:T(8,128)(2,1)}, bf16[1024,256]{1,0:T(8,128)(2,1)S(1)}, u32[]{:S(2)}, u32[]{:S(2)}) collective-permute-start(bf16[1024,256]{1,0:T(8,128)(2,1)} %docs_hbm.1), channel_id=1, source_target_pairs={{0,32},{32,0},{1,33},{33,1},{2,34},{34,2},{3,35},{35,3},{4,36},{36... | collective-permute-start | bytes 1572872 | tf_op jit(solution)/shard_map/ppermute | solution.py:290
  10.6 21.4 %all-to-all-start = ((f32[32,8,128]{2,1,0:T(8,128)}), f32[32,8,128]{2,1,0:T(8,128)S(1)}, u32[]{:S(2)}, u32[]{:S(2)}) async-start(f32[32,8,128]{2,1,0:T(8,128)} %get-tuple-element.21), calls=%async_computation | async-start | bytes 262144 | tf_op jit(solution)/shard_map/all_to_all | solution.py:269
  22.6 4.9 %collective-permute-start = (f32[8,128]{1,0:T(8,128)S(1)}, f32[8,128]{1,0:T(8,128)S(1)}, u32[]{:S(2)}, u32[]{:S(2)}) collective-permute-start(f32[8,128]{1,0:T(8,128)S(1)} %get-tuple-element.22.own_w_ref), channel_id=1, source_target_pairs={{0,32},{32,0},{1,33},{33,1},{2,34},{34,2},{3,35},{35,3},{4,36},{36... | collective-permute-start | bytes 12296 | tf_op jit(solution)/shard_map/ppermute | solution.py:304
  122.6 5.4 %collective-permute-start.2 = (f32[520,256]{1,0:T(8,128)S(1)}, f32[520,256]{1,0:T(8,128)S(1)}, u32[]{:S(2)}, u32[]{:S(2)}) collective-permute-start(f32[520,256]{1,0:T(8,128)S(1)} %get-tuple-element.38), channel_id=1, source_target_pairs={{0,16},{16,0},{1,17},{17,1},{2,18},{18,2},{3,19},{19,3},{4,20},{20... | collective-permute-start | bytes 1597448 | tf_op jit(solution)/shard_map/ppermute | solution.py:345
  162.2 6.6 %collective-permute-start.3 = (bf16[1024,256]{1,0:T(8,128)(2,1)S(1)}, bf16[1024,256]{1,0:T(8,128)(2,1)S(1)}, u32[]{:S(2)}, u32[]{:S(2)}) collective-permute-start(bf16[1024,256]{1,0:T(8,128)(2,1)S(1)} %bitcast.6), channel_id=1, source_target_pairs={{0,16},{16,0},{1,17},{17,1},{2,18},{18,2},{3,19},{19,3},{4,20},{20... | collective-permute-start | bytes 1572872 | tf_op jit(solution)/shard_map/ppermute | solution.py:351

commit v5 on v4

--- a/solution.py
+++ b/solution.py
@@ -19,10 +19,10 @@
 BF16 = jnp.bfloat16
 
 
-def call(kernel, out_shape, n_in, smem=(), scratch=(), flops=0, out_specs=None, in_specs=None, alias=None):
+def call(kernel, out_shape, n_in, scratch=(), flops=0, out_specs=None, in_specs=None, alias=None):
     vmem = pl.BlockSpec(memory_space=pltpu.VMEM)
     if in_specs is None:
-        in_specs = [pl.BlockSpec(memory_space=pltpu.SMEM) if i in smem else vmem for i in range(n_in)]
+        in_specs = [vmem] * n_in
     if out_specs is None:
         out_specs = jax.tree.map(lambda _: vmem, out_shape)
     return pl.pallas_call(
@@ -94,10 +94,10 @@
 
 
 def first_columns(
-    scale, chunk, zl_ref, parts_ref, own_w_ref, other_w_ref, docs_ref, other_ref, cents_ref,
+    scale, chunk, parts_ref, own_w_ref, other_w_ref, docs_ref, other_ref, cents_ref,
     out_ref, tile_ref, top_ref, f_ref, w_ref, docs_all_ref, half_ref,
 ):
-    zl = zl_ref[0]
+    zl = lax.axis_index("zl")
     n_doc, n_cent = docs_ref.shape[0], cents_ref.shape[0] // 2
     groups = 2 * n_doc // LANES
     docs_all_ref[pl.ds(pl.multiple_of(zl * n_doc, n_doc), n_doc), :] = docs_ref[...]
@@ -208,16 +208,16 @@
         out_ref[rows, :] = jnp.dot(p_ref[rows, :], docs_ref[...], preferred_element_type=F32)
 
 
-def final_other(at_ref, parts_ref, w_ref, f_ref, c_ref, tile_ref, docs_ref, out_ref, pot_ref, u_ref, p_ref):
+def final_other(parts_ref, w_ref, f_ref, c_ref, tile_ref, docs_ref, out_ref, pot_ref, u_ref, p_ref):
     u = w_ref[...] / jnp.sum(parts_ref[...].astype(F32), axis=0)
     u_ref[...] = u
     pot = (f_ref[...] + jnp.log2(u)) * LN2
-    pot_ref[...] = jnp.where(at_ref[0] == 0, pot[0:8, :], pot[8:16, :])
-    half_sums(1 - at_ref[1], u, c_ref, tile_ref, docs_ref, out_ref, p_ref)
-
-
-def final_own(at_ref, u_ref, c_ref, tile_ref, docs_ref, out_ref, p_ref):
-    half_sums(at_ref[1], u_ref[...], c_ref, tile_ref, docs_ref, out_ref, p_ref)
+    pot_ref[...] = jnp.where(lax.axis_index("zl") == 0, pot[0:8, :], pot[8:16, :])
+    half_sums(1 - lax.axis_index("core"), u, c_ref, tile_ref, docs_ref, out_ref, p_ref)
+
+
+def final_own(u_ref, c_ref, tile_ref, docs_ref, out_ref, p_ref):
+    half_sums(lax.axis_index("core"), u_ref[...], c_ref, tile_ref, docs_ref, out_ref, p_ref)
 
 
 def final_join(own_ref, other_ref, out_ref):
@@ -236,7 +236,7 @@
         out_ref[q, :, 256 * (chunk // 16) :] = jnp.concatenate(pair, axis=0).astype(BF16)
 
 
-def divide(at_ref, parts_ref, out_ref, mass_ref):
+def divide(parts_ref, out_ref, mass_ref):
     total = parts_ref[0].astype(F32)
     for p in range(1, parts_ref.shape[0]):
         total = total + parts_ref[p].astype(F32)
@@ -244,23 +244,23 @@
     chunk = tiles * 8
     mass = total[0:8, tiles * LANES :] + total[8:16, tiles * LANES :]
     mass_ref[...] = to_columns(mass)
-    col = mass_ref[pl.ds(pl.multiple_of(at_ref[2] * chunk, chunk), chunk), :]
+    col = mass_ref[pl.ds(pl.multiple_of((lax.axis_index("y") & 1) * chunk, chunk), chunk), :]
     for i in range(chunk // 16):
         pair = [total[:, (i * 2 + h) * LANES : (i * 2 + h + 1) * LANES] / col[i * 16 : (i + 1) * 16, :] for h in range(2)]
         new = jnp.concatenate(pair, axis=1).astype(BF16)
         out_ref[:, i * 16 : (i + 1) * 16, :] = jnp.broadcast_to(new[None], (out_ref.shape[0], 16, 256))
 
 
-def place_own(at_ref, x_ref, out_ref, sem):
+def place_own(x_ref, out_ref, sem):
     rows = x_ref.shape[0]
-    copy = pltpu.make_async_copy(x_ref, out_ref.at[pl.ds(pl.multiple_of(at_ref[1] * rows, rows), rows), :], sem)
+    copy = pltpu.make_async_copy(x_ref, out_ref.at[pl.ds(pl.multiple_of(lax.axis_index("core") * rows, rows), rows), :], sem)
     copy.start()
     copy.wait()
 
 
-def place_other(at_ref, x_ref, _, out_ref, sem):
+def place_other(x_ref, _, out_ref, sem):
     rows = x_ref.shape[0]
-    copy = pltpu.make_async_copy(x_ref, out_ref.at[pl.ds(pl.multiple_of((1 - at_ref[1]) * rows, rows), rows), :], sem)
+    copy = pltpu.make_async_copy(x_ref, out_ref.at[pl.ds(pl.multiple_of((1 - lax.axis_index("core")) * rows, rows), rows), :], sem)
     copy.start()
     copy.wait()
 
@@ -276,9 +276,6 @@
     doc_rows, cent_rows = n_doc // LANES, n_cent // LANES
     scale = 4.0 * docs.shape[1] ** -0.5 * LOG2E
     target = 0.5 * (docs.shape[0] * n_y * n_zl * n_core) / (cents.shape[0] * n_zh * n_x)
-    zl = lax.axis_index("zl")
-    core = lax.axis_index("core")
-    at = jnp.stack([zl, core, lax.axis_index("y") & 1]).astype(jnp.int32)
     swap = [(0, 1), (1, 0)]
     shape = jax.ShapeDtypeStruct
     tile_shape = pltpu.VMEM((n_cent, n_doc), F32)
@@ -286,7 +283,6 @@
 
     any_space = pl.BlockSpec(memory_space=pl.ANY)
     hbm = pl.BlockSpec(memory_space=pltpu.HBM)
-    smem = pl.BlockSpec(memory_space=pltpu.SMEM)
     other_docs = lax.ppermute(docs, "zl", swap)
     parts, docs, cents, own_w = call(
         functools.partial(first_rows, scale),
@@ -314,11 +310,10 @@
             shape((doc_rows, LANES), F32),
             pltpu.VMEM((n_doc, 256), BF16),
         ),
-        7,
-        smem=(0,),
+        6,
         scratch=[pltpu.VMEM((n_cent, 256), BF16)],
         flops=2 * n_doc * n_cent * 256,
-    )(at, parts, own_w, other_w, docs, other_docs, cents)
+    )(parts, own_w, other_w, docs, other_docs, cents)
 
     rows_out = (shape((row_peers, doc_rows, LANES), BF16), small)
     parts = exchange(parts, COLS)
@@ -337,23 +332,22 @@
     for_other, pot, u = call(
         final_other,
         (part_shape, shape((doc_rows // 2, LANES), F32), shape((doc_rows, LANES), F32)),
-        7,
-        smem=(0,),
+        6,
         scratch=p_scratch,
         flops=half_flops,
-    )(at, parts, w, f, c, tile, docs_all)
+    )(parts, w, f, c, tile, docs_all)
     from_other = lax.ppermute(for_other, "core", swap)
-    for_own = call(final_own, part_shape, 5, smem=(0,), scratch=p_scratch, flops=half_flops)(at, u, c, tile, docs_all)
+    for_own = call(final_own, part_shape, 4, scratch=p_scratch, flops=half_flops)(u, c, tile, docs_all)
     sums = call(final_join, shape((n_y, 16, 2 * LANES * (chunk // 16) + LANES), BF16), 2)(for_own, from_other)
     sums = exchange(sums, "y")
-    new = call(divide, shape((n_y * n_zl, chunk, 256), BF16), 2, smem=(0,), scratch=[pltpu.VMEM((LANES, LANES), F32)])(at, sums)
+    new = call(divide, shape((n_y * n_zl, chunk, 256), BF16), 1, scratch=[pltpu.VMEM((LANES, LANES), F32)])(sums)
     own = exchange(new, ("y", "zl")).reshape(n_y * n_zl * chunk, 256)
     other = lax.ppermute(own, "core", swap)
     placed = shape((cents.shape[0], 256), BF16)
-    new = call(place_own, placed, 2, in_specs=[smem, any_space], out_specs=any_space, scratch=[pltpu.SemaphoreType.DMA])(at, own)
+    new = call(place_own, placed, 1, in_specs=[any_space], out_specs=any_space, scratch=[pltpu.SemaphoreType.DMA])(own)
     new = call(
-        place_other, placed, 3, in_specs=[smem, any_space, any_space], out_specs=any_space, scratch=[pltpu.SemaphoreType.DMA], alias={2: 0}
-    )(at, other, new)
+        place_other, placed, 2, in_specs=[any_space, any_space], out_specs=any_space, scratch=[pltpu.SemaphoreType.DMA], alias={1: 0}
+    )(other, new)
     return new, pot.reshape(-1)
 
 

time: 171 us -> 169 us (0.988)
  Pallas kernels: 20.4 us -> 17.9 us
    pallas_call x4, Pallas kernels: 5.28 us -> 3.16 us  [the longest x1 1.39 us: per_device(): call(final_own, part_shape, 4, scratch=p_scratch, flops=half_flops)]
  transfers between devices with their start and end apart: 5 -> 5, of which waited for: 3 -> 4; matrix products, arithmetic and copies ran while one was open for 0% -> 0% of each run, Pallas kernels for 5% -> 4%
where the time goes in v5:
time: 169 us; the launch traced here: 168 us
  blocking collectives  114 us (67%)
  starting transfers between devices  28.5 us (17%)
  Pallas kernels  17.9 us (11%)
  waiting for transfers between devices  7.07 us (4%)
    all_to_all x8, blocking collectives, exchange(): return lax.all_to_all(x, axes, 0, 0)  114 us
    all_to_all x1, starting transfers between devices, exchange(): return lax.all_to_all(x, axes, 0, 0)  12 us
    pallas_call x1, Pallas kernels, per_device(): call(functools.partial(first_rows, scale), (shape((row_peers, doc_rows //...  5.14 us
    ppermute x1, starting transfers between devices, per_device(): other = lax.ppermute(own, 'core', swap)  5.11 us
    ppermute x1, starting transfers between devices, per_device(): other_docs = lax.ppermute(docs, 'zl', swap)  4.83 us
    all_to_all x1, waiting for transfers between devices, exchange(): return lax.all_to_all(x, axes, 0, 0)  4.53 us
    ppermute x1, starting transfers between devices, per_device(): from_other = lax.ppermute(for_other, 'core', swap)  3.44 us
  transfers between devices with their start and end apart: 5, of which 4 were waited for; matrix products, arithmetic and copies ran while one was open for 0% of the time, Pallas kernels for 4%

profile of v5, /device:TPU:1, one launch (start us, length us, event | category | flops | bytes accessed | tf_op | source)
XLA Modules:
  0.0 168.4 jit_solution(4499265028503775396)
XLA Ops:
  0.6 4.8 %collective-permute-start.1 = (bf16[1024,256]{1,0:T(8,128)(2,1)}, bf16[1024,256]{1,0:T(8,128)(2,1)S(1)}, u32[]{:S(2)}, u32[]{:S(2)}) collective-permute-start(bf16[1024,256]{1,0:T(8,128)(2,1)} %docs_hbm.1), channel_id=1, source_target_pairs={{0,32},{32,0},{1,33},{33,1},{2,34},{34,2},{3,35},{35,3},{4,36},{36... | collective-permute-start | bytes 1572872 | tf_op jit(solution)/shard_map/ppermute | solution.py:286
  5.5 5.1 %shard_map.59 = (f32[32,8,128]{2,1,0:T(8,128)}, bf16[1024,256]{1,0:T(8,128)(2,1)S(1)}, bf16[2048,256]{1,0:T(8,128)(2,1)S(1)}, f32[8,128]{1,0:T(8,128)S(1)}) custom-call(s32[64]{0:T(128)} %mass_hbm.1, s32[8,128]{1,0:T(8,128)} %bitcast.5, bf16[1024,256]{1,0:T(8,128)(2,1)} %docs_hbm.1, bf16[2048,256]{1,0:T(8,128)(2,1)} %cents_hbm.1), custom_call_target="tpu_custom_call" | custom-call | flops 1073741824 | bytes 1048576 | tf_op jit(solution)/shard_map/pallas_call | solution.py:287
  10.6 12.0 %all-to-all-start = ((f32[32,8,128]{2,1,0:T(8,128)}), f32[32,8,128]{2,1,0:T(8,128)S(1)}, u32[]{:S(2)}, u32[]{:S(2)}) async-start(f32[32,8,128]{2,1,0:T(8,128)} %get-tuple-element.21), calls=%async_computation | async-start | bytes 262144 | tf_op jit(solution)/shard_map/all_to_all | solution.py:269
  22.6 3.1 %collective-permute-start = (f32[8,128]{1,0:T(8,128)S(1)}, f32[8,128]{1,0:T(8,128)S(1)}, u32[]{:S(2)}, u32[]{:S(2)}) collective-permute-start(f32[8,128]{1,0:T(8,128)S(1)} %get-tuple-element.22.own_w_ref), channel_id=1, source_target_pairs={{0,32},{32,0},{1,33},{33,1},{2,34},{34,2},{3,35},{35,3},{4,36},{36... | collective-permute-start | bytes 12296 | tf_op jit(solution)/shard_map/ppermute | solution.py:300
  25.8 1.7 %collective-permute-done.other_w_ref = f32[8,128]{1,0:T(8,128)S(1)} collective-permute-done((f32[8,128]{1,0:T(8,128)S(1)}, f32[8,128]{1,0:T(8,128)S(1)}, u32[]{:S(2)}, u32[]{:S(2)}) %collective-permute-start) | collective-permute-done | bytes 4128 | tf_op jit(solution)/shard_map/ppermute | solution.py:300
  27.5 4.5 %all-to-all-done.parts_ref = f32[32,8,128]{2,1,0:T(8,128)S(1)} async-done(((f32[32,8,128]{2,1,0:T(8,128)}), f32[32,8,128]{2,1,0:T(8,128)S(1)}, u32[]{:S(2)}, u32[]{:S(2)}) %all-to-all-start) | async-done | bytes 131104 | tf_op jit(solution)/shard_map/all_to_all | solution.py:269
  32.0 0.0 collective-permute-done.1.other_ref
  32.0 3.3 %shard_map.60 = (f32[16,8,128]{2,1,0:T(8,128)S(1)}, f32[1024,2048]{1,0:T(8,128)S(1)}, f32[8,128]{1,0:T(8,128)S(1)}, f32[16,128]{1,0:T(8,128)S(1)}, f32[16,128]{1,0:T(8,128)S(1)}, /*index=5*/bf16[2048,256]{1,0:T(8,128)(2,1)S(1)}) custom-call(f32[32,8,128]{2,1,0:T(8,128)S(1)} %all-to-all-done.parts_ref, f32[8,128]{1,0:T(8,128)S(1)} %get-tuple-element.22.own_w_ref, ...), custom_call_target="tpu_custom_call" | custom-call | flops 1073741824 | bytes 1048576 | tf_op jit(solution)/shard_map/pallas_call | solution.py:303
  35.3 17.2 %all_to_all.45.parts_ref = f32[16,8,128]{2,1,0:T(8,128)S(1)} all-to-all(f32[16,8,128]{2,1,0:T(8,128)S(1)} %get-tuple-element.25), channel_id=1, replica_groups=mesh['y'=8,'zl'=2,'core'=2,'zh'=4,'x'=4] {'y','core'}, dimensions={0} | all-to-all | bytes 131072 | tf_op jit(solution)/shard_map/all_to_all | solution.py:269
  52.5 1.0 shard_map.61
  53.6 14.1 %all_to_all.46.parts_ref = bf16[32,16,128]{2,1,0:T(8,128)(2,1)S(1)} all-to-all(bf16[32,16,128]{2,1,0:T(8,128)(2,1)S(1)} %get-tuple-element.28), channel_id=1, replica_groups=mesh['y'=8,'zl'=2,'core'=2,'zh'=4,'x'=4] {'zl','zh','x'}, dimensions={0} | all-to-all | bytes 262144 | tf_op jit(solution)/shard_map/all_to_all | solution.py:269
  67.6 0.7 shard_map.62
  68.3 11.8 %all_to_all.47.parts_ref = f32[16,8,128]{2,1,0:T(8,128)S(1)} all-to-all(f32[16,8,128]{2,1,0:T(8,128)S(1)} %shard_map.62), channel_id=1, replica_groups=mesh['y'=8,'zl'=2,'core'=2,'zh'=4,'x'=4] {'y','core'}, dimensions={0} | all-to-all | bytes 131072 | tf_op jit(solution)/shard_map/all_to_all | solution.py:269
  80.1 1.0 shard_map.63
  81.1 12.9 %all_to_all.48.parts_ref = bf16[32,16,128]{2,1,0:T(8,128)(2,1)S(1)} all-to-all(bf16[32,16,128]{2,1,0:T(8,128)(2,1)S(1)} %get-tuple-element.31), channel_id=1, replica_groups=mesh['y'=8,'zl'=2,'core'=2,'zh'=4,'x'=4] {'zl','zh','x'}, dimensions={0} | all-to-all | bytes 262144 | tf_op jit(solution)/shard_map/all_to_all | solution.py:269
  94.0 0.7 shard_map.64
  94.7 11.8 %all_to_all.49.parts_ref = f32[16,8,128]{2,1,0:T(8,128)S(1)} all-to-all(f32[16,8,128]{2,1,0:T(8,128)S(1)} %shard_map.64), channel_id=1, replica_groups=mesh['y'=8,'zl'=2,'core'=2,'zh'=4,'x'=4] {'y','core'}, dimensions={0} | all-to-all | bytes 131072 | tf_op jit(solution)/shard_map/all_to_all | solution.py:269
  106.5 1.0 shard_map.65
  107.5 12.9 %all_to_all.50.parts_ref = bf16[32,16,128]{2,1,0:T(8,128)(2,1)S(1)} all-to-all(bf16[32,16,128]{2,1,0:T(8,128)(2,1)S(1)} %get-tuple-element.33), channel_id=1, replica_groups=mesh['y'=8,'zl'=2,'core'=2,'zh'=4,'x'=4] {'zl','zh','x'}, dimensions={0} | all-to-all | bytes 262144 | tf_op jit(solution)/shard_map/all_to_all | solution.py:269
  120.4 1.9 %shard_map.66 = (f32[520,256]{1,0:T(8,128)S(1)}, f32[8,128]{1,0:T(8,128)}, f32[16,128]{1,0:T(8,128)S(1)}) custom-call(bf16[32,16,128]{2,1,0:T(8,128)(2,1)S(1)} %all_to_all.50.parts_ref, f32[16,128]{1,0:T(8,128)S(1)} %get-tuple-element.29.w_ref, f32[16,128]{1,0:T(8,128)S(1)} %get-tuple-element.34.f_ref, f32[8,128]{1,0:T(8,128)S(1)} %get-tuple-element.35.c_ref, ...), custom_call_target="tpu_custom_call" | custom-call | flops 536870912 | bytes 1048576 | tf_op jit(solution)/shard_map/pallas_call | solution.py:332
  122.2 3.4 %collective-permute-start.2 = (f32[520,256]{1,0:T(8,128)S(1)}, f32[520,256]{1,0:T(8,128)S(1)}, u32[]{:S(2)}, u32[]{:S(2)}) collective-permute-start(f32[520,256]{1,0:T(8,128)S(1)} %get-tuple-element.38), channel_id=1, source_target_pairs={{0,16},{16,0},{1,17},{17,1},{2,18},{18,2},{3,19},{19,3},{4,20},{20... | collective-permute-start | bytes 1597448 | tf_op jit(solution)/shard_map/ppermute | solution.py:339
  125.7 1.4 shard_map.67.own_ref
  127.1 0.1 collective-permute-done.2.other_ref
  127.2 0.1 shard_map.68
  127.3 15.0 %all_to_all.51.parts_ref = bf16[8,16,1152]{2,1,0:T(8,128)(2,1)S(1)} all-to-all(bf16[8,16,1152]{2,1,0:T(8,128)(2,1)S(1)} %shard_map.68), channel_id=1, replica_groups=mesh['y'=8,'zl'=2,'core'=2,'zh'=4,'x'=4] {'y'}, dimensions={0} | all-to-all | bytes 589824 | tf_op jit(solution)/shard_map/all_to_all | solution.py:269
  142.3 0.2 shard_map.69
  142.5 18.3 %all_to_all.52 = bf16[16,64,256]{2,1,0:T(8,128)(2,1)S(1)} all-to-all(bf16[16,64,256]{2,1,0:T(8,128)(2,1)S(1)} %shard_map.69), channel_id=1, replica_groups=mesh['y'=8,'zl'=2,'core'=2,'zh'=4,'x'=4] {'y','zl'}, dimensions={0} | all-to-all | bytes 1048576 | tf_op jit(solution)/shard_map/all_to_all | solution.py:269
  160.8 5.1 %collective-permute-start.3 = (bf16[1024,256]{1,0:T(8,128)(2,1)S(1)}, bf16[1024,256]{1,0:T(8,128)(2,1)S(1)}, u32[]{:S(2)}, u32[]{:S(2)}) collective-permute-start(bf16[1024,256]{1,0:T(8,128)(2,1)S(1)} %bitcast.3), channel_id=1, source_target_pairs={{0,16},{16,0},{1,17},{17,1},{2,18},{18,2},{3,19},{19,3},{4,20},{20... | collective-permute-start | bytes 1572872 | tf_op jit(solution)/shard_map/ppermute | solution.py:345
  165.9 0.8 shard_map.70._
  166.7 0.7 collective-permute-done.3.x_ref
  167.4 0.8 shard_map.71
Async XLA Ops:
  0.6 31.4 %collective-permute-start.1 = (bf16[1024,256]{1,0:T(8,128)(2,1)}, bf16[1024,256]{1,0:T(8,128)(2,1)S(1)}, u32[]{:S(2)}, u32[]{:S(2)}) collective-permute-start(bf16[1024,256]{1,0:T(8,128)(2,1)} %docs_hbm.1), channel_id=1, source_target_pairs={{0,32},{32,0},{1,33},{33,1},{2,34},{34,2},{3,35},{35,3},{4,36},{36... | collective-permute-start | bytes 1572872 | tf_op jit(solution)/shard_map/ppermute | solution.py:286
  10.6 21.4 %all-to-all-start = ((f32[32,8,128]{2,1,0:T(8,128)}), f32[32,8,128]{2,1,0:T(8,128)S(1)}, u32[]{:S(2)}, u32[]{:S(2)}) async-start(f32[32,8,128]{2,1,0:T(8,128)} %get-tuple-element.21), calls=%async_computation | async-start | bytes 262144 | tf_op jit(solution)/shard_map/all_to_all | solution.py:269
  22.6 4.9 %collective-permute-start = (f32[8,128]{1,0:T(8,128)S(1)}, f32[8,128]{1,0:T(8,128)S(1)}, u32[]{:S(2)}, u32[]{:S(2)}) collective-permute-start(f32[8,128]{1,0:T(8,128)S(1)} %get-tuple-element.22.own_w_ref), channel_id=1, source_target_pairs={{0,32},{32,0},{1,33},{33,1},{2,34},{34,2},{3,35},{35,3},{4,36},{36... | collective-permute-start | bytes 12296 | tf_op jit(solution)/shard_map/ppermute | solution.py:300
  122.2 5.0 %collective-permute-start.2 = (f32[520,256]{1,0:T(8,128)S(1)}, f32[520,256]{1,0:T(8,128)S(1)}, u32[]{:S(2)}, u32[]{:S(2)}) collective-permute-start(f32[520,256]{1,0:T(8,128)S(1)} %get-tuple-element.38), channel_id=1, source_target_pairs={{0,16},{16,0},{1,17},{17,1},{2,18},{18,2},{3,19},{19,3},{4,20},{20... | collective-permute-start | bytes 1597448 | tf_op jit(solution)/shard_map/ppermute | solution.py:339
  160.8 6.6 %collective-permute-start.3 = (bf16[1024,256]{1,0:T(8,128)(2,1)S(1)}, bf16[1024,256]{1,0:T(8,128)(2,1)S(1)}, u32[]{:S(2)}, u32[]{:S(2)}) collective-permute-start(bf16[1024,256]{1,0:T(8,128)(2,1)S(1)} %bitcast.3), channel_id=1, source_target_pairs={{0,16},{16,0},{1,17},{17,1},{2,18},{18,2},{3,19},{19,3},{4,20},{20... | collective-permute-start | bytes 1572872 | tf_op jit(solution)/shard_map/ppermute | solution.py:345

commit v6 on v5

--- a/solution.py
+++ b/solution.py
@@ -13,7 +13,7 @@
 LN2 = 0.6931471805599453
 LANES = 128
 VMEM_LIMIT = 32 * 1024 * 1024
-ROWS = ("zl", "zh", "x")
+ROWS = ("x", "zl", "zh")
 COLS = ("y", "core")
 F32 = jnp.float32
 BF16 = jnp.bfloat16
@@ -94,7 +94,7 @@
 
 
 def first_columns(
-    scale, chunk, parts_ref, own_w_ref, other_w_ref, docs_ref, other_ref, cents_ref,
+    scale, n_x, chunk, parts_ref, own_w_ref, other_w_ref, docs_ref, other_ref, cents_ref,
     out_ref, tile_ref, top_ref, f_ref, w_ref, docs_all_ref, half_ref,
 ):
     zl = lax.axis_index("zl")
@@ -108,9 +108,9 @@
     own, other = own_w_ref[...], other_w_ref[...]
     w_ref[0:8, :] = jnp.where(zl == 0, own, other)
     w_ref[8:16, :] = jnp.where(zl == 0, other, own)
-    half = parts_ref.shape[0] // 2
+    by_zl = parts_ref[...].reshape(n_x, 2, parts_ref.shape[0] // (2 * n_x), 8, LANES)
     for z in range(2):
-        parts = parts_ref[z * half : (z + 1) * half]
+        parts = by_zl[:, z].reshape(parts_ref.shape[0] // 2, 8, LANES)
         top = jnp.max(parts, axis=0)
         lse = top + jnp.log2(jnp.sum(jnp.exp2(parts - top[None]), axis=0))
         f_ref[z * 8 : (z + 1) * 8, :] = jnp.log2(w_ref[z * 8 : (z + 1) * 8, :]) - lse
@@ -301,7 +301,7 @@
     parts = exchange(parts, ROWS)
     chunk = n_cent // col_peers
     parts, tile, top, f, w, docs_all = call(
-        functools.partial(first_columns, scale, chunk),
+        functools.partial(first_columns, scale, n_x, chunk),
         (
             shape((col_peers, cent_rows, LANES), F32),
             tile_shape,

time: 169 us -> 168 us (level)
  no operation moved by 1% of the time
where the time goes in v6:
time: 168 us; the launch traced here: 167 us
  blocking collectives  114 us (68%)
  starting transfers between devices  28 us (17%)
  Pallas kernels  17.9 us (11%)
  waiting for transfers between devices  6.57 us (4%)
    all_to_all x8, blocking collectives, exchange(): return lax.all_to_all(x, axes, 0, 0)  114 us
    all_to_all x1, starting transfers between devices, exchange(): return lax.all_to_all(x, axes, 0, 0)  12 us
    pallas_call x1, Pallas kernels, per_device(): call(functools.partial(first_rows, scale), (shape((row_peers, doc_rows //...  5.14 us
    ppermute x1, starting transfers between devices, per_device(): other_docs = lax.ppermute(docs, 'zl', swap)  4.83 us
    all_to_all x1, waiting for transfers between devices, exchange(): return lax.all_to_all(x, axes, 0, 0)  4.46 us
    ppermute x1, starting transfers between devices, per_device(): other = lax.ppermute(own, 'core', swap)  4.41 us
    ppermute x1, starting transfers between devices, per_device(): from_other = lax.ppermute(for_other, 'core', swap)  3.64 us
  transfers between devices with their start and end apart: 5, of which 4 were waited for; matrix products, arithmetic and copies ran while one was open for 0% of the time, Pallas kernels for 4%

profile of v6, /device:TPU:1, one launch (start us, length us, event | category | flops | bytes accessed | tf_op | source)
XLA Modules:
  0.0 167.0 jit_solution(3924880596099362992)
XLA Ops:
  0.6 4.8 %collective-permute-start.1 = (bf16[1024,256]{1,0:T(8,128)(2,1)}, bf16[1024,256]{1,0:T(8,128)(2,1)S(1)}, u32[]{:S(2)}, u32[]{:S(2)}) collective-permute-start(bf16[1024,256]{1,0:T(8,128)(2,1)} %docs_hbm.1), channel_id=1, source_target_pairs={{0,32},{32,0},{1,33},{33,1},{2,34},{34,2},{3,35},{35,3},{4,36},{36... | collective-permute-start | bytes 1572872 | tf_op jit(solution)/shard_map/ppermute | solution.py:286
  5.5 5.1 %shard_map.59 = (f32[32,8,128]{2,1,0:T(8,128)}, bf16[1024,256]{1,0:T(8,128)(2,1)S(1)}, bf16[2048,256]{1,0:T(8,128)(2,1)S(1)}, f32[8,128]{1,0:T(8,128)S(1)}) custom-call(s32[64]{0:T(128)} %mass_hbm.1, s32[8,128]{1,0:T(8,128)} %bitcast.5, bf16[1024,256]{1,0:T(8,128)(2,1)} %docs_hbm.1, bf16[2048,256]{1,0:T(8,128)(2,1)} %cents_hbm.1), custom_call_target="tpu_custom_call" | custom-call | flops 1073741824 | bytes 1048576 | tf_op jit(solution)/shard_map/pallas_call | solution.py:287
  10.6 12.0 %all-to-all-start = ((f32[32,8,128]{2,1,0:T(8,128)}), f32[32,8,128]{2,1,0:T(8,128)S(1)}, u32[]{:S(2)}, u32[]{:S(2)}) async-start(f32[32,8,128]{2,1,0:T(8,128)} %get-tuple-element.21), calls=%async_computation | async-start | bytes 262144 | tf_op jit(solution)/shard_map/all_to_all | solution.py:269
  22.6 3.1 %collective-permute-start = (f32[8,128]{1,0:T(8,128)S(1)}, f32[8,128]{1,0:T(8,128)S(1)}, u32[]{:S(2)}, u32[]{:S(2)}) collective-permute-start(f32[8,128]{1,0:T(8,128)S(1)} %get-tuple-element.22.own_w_ref), channel_id=1, source_target_pairs={{0,32},{32,0},{1,33},{33,1},{2,34},{34,2},{3,35},{35,3},{4,36},{36... | collective-permute-start | bytes 12296 | tf_op jit(solution)/shard_map/ppermute | solution.py:300
  25.8 1.3 collective-permute-done.other_w_ref
  27.0 4.5 %all-to-all-done.parts_ref = f32[32,8,128]{2,1,0:T(8,128)S(1)} async-done(((f32[32,8,128]{2,1,0:T(8,128)}), f32[32,8,128]{2,1,0:T(8,128)S(1)}, u32[]{:S(2)}, u32[]{:S(2)}) %all-to-all-start) | async-done | bytes 131104 | tf_op jit(solution)/shard_map/all_to_all | solution.py:269
  31.5 0.0 collective-permute-done.1.other_ref
  31.5 3.3 %shard_map.60 = (f32[16,8,128]{2,1,0:T(8,128)S(1)}, f32[1024,2048]{1,0:T(8,128)S(1)}, f32[8,128]{1,0:T(8,128)S(1)}, f32[16,128]{1,0:T(8,128)S(1)}, f32[16,128]{1,0:T(8,128)S(1)}, /*index=5*/bf16[2048,256]{1,0:T(8,128)(2,1)S(1)}) custom-call(f32[32,8,128]{2,1,0:T(8,128)S(1)} %all-to-all-done.parts_ref, f32[8,128]{1,0:T(8,128)S(1)} %get-tuple-element.22.own_w_ref, ...), custom_call_target="tpu_custom_call" | custom-call | flops 1073741824 | bytes 1048576 | tf_op jit(solution)/shard_map/pallas_call | solution.py:303
  34.8 17.0 %all_to_all.45.parts_ref = f32[16,8,128]{2,1,0:T(8,128)S(1)} all-to-all(f32[16,8,128]{2,1,0:T(8,128)S(1)} %get-tuple-element.25), channel_id=1, replica_groups=mesh['y'=8,'zl'=2,'core'=2,'zh'=4,'x'=4] {'y','core'}, dimensions={0} | all-to-all | bytes 131072 | tf_op jit(solution)/shard_map/all_to_all | solution.py:269
  51.8 1.0 shard_map.61
  52.9 13.7 %all_to_all.46.parts_ref = bf16[32,16,128]{2,1,0:T(8,128)(2,1)S(1)} all-to-all(bf16[32,16,128]{2,1,0:T(8,128)(2,1)S(1)} %get-tuple-element.28), channel_id=1, replica_groups=mesh['y'=8,'zl'=2,'core'=2,'zh'=4,'x'=4] {'x','zl','zh'}, dimensions={0} | all-to-all | bytes 262144 | tf_op jit(solution)/shard_map/all_to_all | solution.py:269
  66.6 0.7 shard_map.62
  67.3 12.0 %all_to_all.47.parts_ref = f32[16,8,128]{2,1,0:T(8,128)S(1)} all-to-all(f32[16,8,128]{2,1,0:T(8,128)S(1)} %shard_map.62), channel_id=1, replica_groups=mesh['y'=8,'zl'=2,'core'=2,'zh'=4,'x'=4] {'y','core'}, dimensions={0} | all-to-all | bytes 131072 | tf_op jit(solution)/shard_map/all_to_all | solution.py:269
  79.3 1.0 shard_map.63
  80.3 12.8 %all_to_all.48.parts_ref = bf16[32,16,128]{2,1,0:T(8,128)(2,1)S(1)} all-to-all(bf16[32,16,128]{2,1,0:T(8,128)(2,1)S(1)} %get-tuple-element.31), channel_id=1, replica_groups=mesh['y'=8,'zl'=2,'core'=2,'zh'=4,'x'=4] {'x','zl','zh'}, dimensions={0} | all-to-all | bytes 262144 | tf_op jit(solution)/shard_map/all_to_all | solution.py:269
  93.0 0.7 shard_map.64
  93.7 12.0 %all_to_all.49.parts_ref = f32[16,8,128]{2,1,0:T(8,128)S(1)} all-to-all(f32[16,8,128]{2,1,0:T(8,128)S(1)} %shard_map.64), channel_id=1, replica_groups=mesh['y'=8,'zl'=2,'core'=2,'zh'=4,'x'=4] {'y','core'}, dimensions={0} | all-to-all | bytes 131072 | tf_op jit(solution)/shard_map/all_to_all | solution.py:269
  105.7 1.0 shard_map.65
  106.7 12.8 %all_to_all.50.parts_ref = bf16[32,16,128]{2,1,0:T(8,128)(2,1)S(1)} all-to-all(bf16[32,16,128]{2,1,0:T(8,128)(2,1)S(1)} %get-tuple-element.33), channel_id=1, replica_groups=mesh['y'=8,'zl'=2,'core'=2,'zh'=4,'x'=4] {'x','zl','zh'}, dimensions={0} | all-to-all | bytes 262144 | tf_op jit(solution)/shard_map/all_to_all | solution.py:269
  119.5 1.9 %shard_map.66 = (f32[520,256]{1,0:T(8,128)S(1)}, f32[8,128]{1,0:T(8,128)}, f32[16,128]{1,0:T(8,128)S(1)}) custom-call(bf16[32,16,128]{2,1,0:T(8,128)(2,1)S(1)} %all_to_all.50.parts_ref, f32[16,128]{1,0:T(8,128)S(1)} %get-tuple-element.29.w_ref, f32[16,128]{1,0:T(8,128)S(1)} %get-tuple-element.34.f_ref, f32[8,128]{1,0:T(8,128)S(1)} %get-tuple-element.35.c_ref, ...), custom_call_target="tpu_custom_call" | custom-call | flops 536870912 | bytes 1048576 | tf_op jit(solution)/shard_map/pallas_call | solution.py:332
  121.4 3.6 %collective-permute-start.2 = (f32[520,256]{1,0:T(8,128)S(1)}, f32[520,256]{1,0:T(8,128)S(1)}, u32[]{:S(2)}, u32[]{:S(2)}) collective-permute-start(f32[520,256]{1,0:T(8,128)S(1)} %get-tuple-element.38), channel_id=1, source_target_pairs={{0,16},{16,0},{1,17},{17,1},{2,18},{18,2},{3,19},{19,3},{4,20},{20... | collective-permute-start | bytes 1597448 | tf_op jit(solution)/shard_map/ppermute | solution.py:339
  125.0 1.4 shard_map.67.own_ref
  126.4 0.1 collective-permute-done.2.other_ref
  126.5 0.1 shard_map.68
  126.6 15.0 %all_to_all.51.parts_ref = bf16[8,16,1152]{2,1,0:T(8,128)(2,1)S(1)} all-to-all(bf16[8,16,1152]{2,1,0:T(8,128)(2,1)S(1)} %shard_map.68), channel_id=1, replica_groups=mesh['y'=8,'zl'=2,'core'=2,'zh'=4,'x'=4] {'y'}, dimensions={0} | all-to-all | bytes 589824 | tf_op jit(solution)/shard_map/all_to_all | solution.py:269
  141.6 0.2 shard_map.69
  141.8 18.3 %all_to_all.52 = bf16[16,64,256]{2,1,0:T(8,128)(2,1)S(1)} all-to-all(bf16[16,64,256]{2,1,0:T(8,128)(2,1)S(1)} %shard_map.69), channel_id=1, replica_groups=mesh['y'=8,'zl'=2,'core'=2,'zh'=4,'x'=4] {'y','zl'}, dimensions={0} | all-to-all | bytes 1048576 | tf_op jit(solution)/shard_map/all_to_all | solution.py:269
  160.1 4.4 %collective-permute-start.3 = (bf16[1024,256]{1,0:T(8,128)(2,1)S(1)}, bf16[1024,256]{1,0:T(8,128)(2,1)S(1)}, u32[]{:S(2)}, u32[]{:S(2)}) collective-permute-start(bf16[1024,256]{1,0:T(8,128)(2,1)S(1)} %bitcast.3), channel_id=1, source_target_pairs={{0,16},{16,0},{1,17},{17,1},{2,18},{18,2},{3,19},{19,3},{4,20},{20... | collective-permute-start | bytes 1572872 | tf_op jit(solution)/shard_map/ppermute | solution.py:345
  164.5 0.8 shard_map.70._
  165.4 0.7 collective-permute-done.3.x_ref
  166.1 0.8 shard_map.71
Async XLA Ops:
  0.6 30.9 %collective-permute-start.1 = (bf16[1024,256]{1,0:T(8,128)(2,1)}, bf16[1024,256]{1,0:T(8,128)(2,1)S(1)}, u32[]{:S(2)}, u32[]{:S(2)}) collective-permute-start(bf16[1024,256]{1,0:T(8,128)(2,1)} %docs_hbm.1), channel_id=1, source_target_pairs={{0,32},{32,0},{1,33},{33,1},{2,34},{34,2},{3,35},{35,3},{4,36},{36... | collective-permute-start | bytes 1572872 | tf_op jit(solution)/shard_map/ppermute | solution.py:286
  10.6 20.9 %all-to-all-start = ((f32[32,8,128]{2,1,0:T(8,128)}), f32[32,8,128]{2,1,0:T(8,128)S(1)}, u32[]{:S(2)}, u32[]{:S(2)}) async-start(f32[32,8,128]{2,1,0:T(8,128)} %get-tuple-element.21), calls=%async_computation | async-start | bytes 262144 | tf_op jit(solution)/shard_map/all_to_all | solution.py:269
  22.6 4.4 %collective-permute-start = (f32[8,128]{1,0:T(8,128)S(1)}, f32[8,128]{1,0:T(8,128)S(1)}, u32[]{:S(2)}, u32[]{:S(2)}) collective-permute-start(f32[8,128]{1,0:T(8,128)S(1)} %get-tuple-element.22.own_w_ref), channel_id=1, source_target_pairs={{0,32},{32,0},{1,33},{33,1},{2,34},{34,2},{3,35},{35,3},{4,36},{36... | collective-permute-start | bytes 12296 | tf_op jit(solution)/shard_map/ppermute | solution.py:300
  121.4 5.2 %collective-permute-start.2 = (f32[520,256]{1,0:T(8,128)S(1)}, f32[520,256]{1,0:T(8,128)S(1)}, u32[]{:S(2)}, u32[]{:S(2)}) collective-permute-start(f32[520,256]{1,0:T(8,128)S(1)} %get-tuple-element.38), channel_id=1, source_target_pairs={{0,16},{16,0},{1,17},{17,1},{2,18},{18,2},{3,19},{19,3},{4,20},{20... | collective-permute-start | bytes 1597448 | tf_op jit(solution)/shard_map/ppermute | solution.py:339
  160.1 5.9 %collective-permute-start.3 = (bf16[1024,256]{1,0:T(8,128)(2,1)S(1)}, bf16[1024,256]{1,0:T(8,128)(2,1)S(1)}, u32[]{:S(2)}, u32[]{:S(2)}) collective-permute-start(bf16[1024,256]{1,0:T(8,128)(2,1)S(1)} %bitcast.3), channel_id=1, source_target_pairs={{0,16},{16,0},{1,17},{17,1},{2,18},{18,2},{3,19},{19,3},{4,20},{20... | collective-permute-start | bytes 1572872 | tf_op jit(solution)/shard_map/ppermute | solution.py:345

commit v7 on v6

--- a/solution.py
+++ b/solution.py
@@ -61,24 +61,22 @@
 ):
     n_doc, n_cent = docs_hbm.shape[0], cents_hbm.shape[0]
     block = 512
-    steps = n_cent // block
-    copies = [pltpu.make_async_copy(docs_hbm, docs_ref, sems.at[steps])]
-    for q in range(steps):
-        rows = pl.ds(q * block, block)
-        copies.append(pltpu.make_async_copy(cents_hbm.at[rows, :], cents_ref.at[rows, :], sems.at[q]))
-    copies.append(pltpu.make_async_copy(mass_hbm, mass_ref, sems.at[steps + 1]))
-    copies.append(pltpu.make_async_copy(ids_hbm, ids_ref, sems.at[steps + 2]))
-    for copy in copies[-2:] + copies[:-2]:
+    copies = [
+        pltpu.make_async_copy(src, dst, sems.at[k])
+        for k, (src, dst) in enumerate(((mass_hbm, mass_ref), (ids_hbm, ids_ref), (docs_hbm, docs_ref), (cents_hbm, cents_ref)))
+    ]
+    for copy in copies:
         copy.start()
-    copies[steps + 1].wait()
-    copies[steps + 2].wait()
-    w_ref[...] = weights_of(ids_ref[...], mass_ref)
     copies[0].wait()
+    copies[1].wait()
+    w = weights_of(ids_ref[...], mass_ref)
+    w_ref[...] = w
+    copies[2].wait()
+    copies[3].wait()
     groups = n_doc // 256
     tops = [jnp.full((8, 256), -jnp.inf, F32)] * groups
     totals = [jnp.zeros((8, 256), F32)] * groups
-    for q in range(steps):
-        copies[q + 1].wait()
+    for q in range(n_cent // block):
         cents = cents_ref[q * block : (q + 1) * block, :]
         for g in range(groups):
             s = nt_dot(cents, docs_ref[g * 256 : (g + 1) * 256, :]).reshape(block // 8, 8, 256)
@@ -90,12 +88,12 @@
         top = jnp.max(tops[g], axis=0, keepdims=True)
         lse = top + jnp.log2(jnp.sum(totals[g] * jnp.exp2(tops[g] - top), axis=0, keepdims=True))
         rows += [lse[:, 0:LANES], lse[:, LANES:256]]
-    out_ref[...] = jnp.broadcast_to(jnp.concatenate(rows, axis=0)[None], out_ref.shape)
+    out_ref[...] = jnp.broadcast_to((jnp.concatenate(rows, axis=0) - jnp.log2(w))[None], out_ref.shape)
 
 
 def first_columns(
-    scale, n_x, chunk, parts_ref, own_w_ref, other_w_ref, docs_ref, other_ref, cents_ref,
-    out_ref, tile_ref, top_ref, f_ref, w_ref, docs_all_ref, half_ref,
+    scale, n_x, chunk, parts_ref, docs_ref, other_ref, cents_ref,
+    out_ref, tile_ref, top_ref, f_ref, docs_all_ref, half_ref,
 ):
     zl = lax.axis_index("zl")
     n_doc, n_cent = docs_ref.shape[0], cents_ref.shape[0] // 2
@@ -105,15 +103,11 @@
     for q in range(n_cent // chunk):
         rows = pl.ds(pl.multiple_of(q * 2 * chunk + zl * chunk, chunk), chunk)
         half_ref[q * chunk : (q + 1) * chunk, :] = cents_ref[rows, :]
-    own, other = own_w_ref[...], other_w_ref[...]
-    w_ref[0:8, :] = jnp.where(zl == 0, own, other)
-    w_ref[8:16, :] = jnp.where(zl == 0, other, own)
     by_zl = parts_ref[...].reshape(n_x, 2, parts_ref.shape[0] // (2 * n_x), 8, LANES)
     for z in range(2):
         parts = by_zl[:, z].reshape(parts_ref.shape[0] // 2, 8, LANES)
         top = jnp.max(parts, axis=0)
-        lse = top + jnp.log2(jnp.sum(jnp.exp2(parts - top[None]), axis=0))
-        f_ref[z * 8 : (z + 1) * 8, :] = jnp.log2(w_ref[z * 8 : (z + 1) * 8, :]) - lse
+        f_ref[z * 8 : (z + 1) * 8, :] = -(top + jnp.log2(jnp.sum(jnp.exp2(parts - top[None]), axis=0)))
 
     for g in range(groups // 2):
         f = jnp.concatenate([f_ref[2 * g : 2 * g + 1, :], f_ref[2 * g + 1 : 2 * g + 2, :]], axis=1)
@@ -169,9 +163,14 @@
     weigh_columns(c, tile_ref, out_ref)
 
 
-def columns_after(parts_ref, w_ref, c_ref, tile_ref, out_ref):
+def in_order(own, other):
+    first = lax.axis_index("zl") == 0
+    return jnp.concatenate([jnp.where(first, own, other), jnp.where(first, other, own)], axis=0)
+
+
+def columns_after(parts_ref, w_ref, other_w_ref, c_ref, tile_ref, out_ref):
     groups = tile_ref.shape[1] // LANES
-    u = w_ref[...] / jnp.sum(parts_ref[...].astype(F32), axis=0)
+    u = in_order(w_ref[...], other_w_ref[...]) / jnp.sum(parts_ref[...].astype(F32), axis=0)
     lane = lane_iota()
     sums = jnp.zeros((LANES, LANES), F32)
     for r in range(tile_ref.shape[0] // LANES):
@@ -208,8 +207,8 @@
         out_ref[rows, :] = jnp.dot(p_ref[rows, :], docs_ref[...], preferred_element_type=F32)
 
 
-def final_other(parts_ref, w_ref, f_ref, c_ref, tile_ref, docs_ref, out_ref, pot_ref, u_ref, p_ref):
-    u = w_ref[...] / jnp.sum(parts_ref[...].astype(F32), axis=0)
+def final_other(parts_ref, w_ref, other_w_ref, f_ref, c_ref, tile_ref, docs_ref, out_ref, pot_ref, u_ref, p_ref):
+    u = in_order(w_ref[...], other_w_ref[...]) / jnp.sum(parts_ref[...].astype(F32), axis=0)
     u_ref[...] = u
     pot = (f_ref[...] + jnp.log2(u)) * LN2
     pot_ref[...] = jnp.where(lax.axis_index("zl") == 0, pot[0:8, :], pot[8:16, :])
@@ -294,26 +293,25 @@
         ),
         4,
         in_specs=[hbm] * 4,
-        scratch=[pltpu.SMEM(shard_mass.shape, jnp.int32), pltpu.VMEM((doc_rows // 2, LANES), jnp.int32), pltpu.SemaphoreType.DMA((7,))],
+        scratch=[pltpu.SMEM(shard_mass.shape, jnp.int32), pltpu.VMEM((doc_rows // 2, LANES), jnp.int32), pltpu.SemaphoreType.DMA((4,))],
         flops=2 * docs.shape[0] * cents.shape[0] * 256,
     )(*[pltpu.with_memory_space_constraint(x, pltpu.HBM) for x in (shard_mass, shard_ids.reshape(-1, LANES), docs, cents)])
     other_w = lax.ppermute(own_w, "zl", swap)
     parts = exchange(parts, ROWS)
     chunk = n_cent // col_peers
-    parts, tile, top, f, w, docs_all = call(
+    parts, tile, top, f, docs_all = call(
         functools.partial(first_columns, scale, n_x, chunk),
         (
             shape((col_peers, cent_rows, LANES), F32),
             tile_shape,
             small,
             shape((doc_rows, LANES), F32),
-            shape((doc_rows, LANES), F32),
             pltpu.VMEM((n_doc, 256), BF16),
         ),
-        6,
+        4,
         scratch=[pltpu.VMEM((n_cent, 256), BF16)],
         flops=2 * n_doc * n_cent * 256,
-    )(parts, own_w, other_w, docs, other_docs, cents)
+    )(parts, docs, other_docs, cents)
 
     rows_out = (shape((row_peers, doc_rows, LANES), BF16), small)
     parts = exchange(parts, COLS)
@@ -321,7 +319,7 @@
     parts, c = call(functools.partial(rows_after_first, log_target), rows_out, 3, flops=2 * n_doc * n_cent)(parts, top, tile)
     for turn in range(2):
         parts = exchange(parts, ROWS)
-        parts = call(columns_after, shape((col_peers, cent_rows, LANES), F32), 4, flops=2 * n_doc * n_cent)(parts, w, c, tile)
+        parts = call(columns_after, shape((col_peers, cent_rows, LANES), F32), 5, flops=2 * n_doc * n_cent)(parts, own_w, other_w, c, tile)
         parts = exchange(parts, COLS)
         parts, c = call(functools.partial(rows_after, target), rows_out, 3, flops=2 * n_doc * n_cent)(parts, c, tile)
     parts = exchange(parts, ROWS)
@@ -332,10 +330,10 @@
     for_other, pot, u = call(
         final_other,
         (part_shape, shape((doc_rows // 2, LANES), F32), shape((doc_rows, LANES), F32)),
-        6,
+        7,
         scratch=p_scratch,
         flops=half_flops,
-    )(parts, w, f, c, tile, docs_all)
+    )(parts, own_w, other_w, f, c, tile, docs_all)
     from_other = lax.ppermute(for_other, "core", swap)
     for_own = call(final_own, part_shape, 4, scratch=p_scratch, flops=half_flops)(u, c, tile, docs_all)
     sums = call(final_join, shape((n_y, 16, 2 * LANES * (chunk // 16) + LANES), BF16), 2)(for_own, from_other)

time: 168 us -> 173 us (1.030)
  starting transfers between devices: 28 us -> 19.8 us
  blocking collectives: 114 us -> 122 us
  local copies, waits for them, and re-layouts: 0 us -> 6.61 us
    all_to_all x1, starting transfers between devices: 12 us -> 3.86 us  [exchange(): return lax.all_to_all(x, axes, 0, 0)]
    all_to_all x8, blocking collectives: 114 us -> 122 us  [exchange(): return lax.all_to_all(x, axes, 0, 0)]
    unnamed x0 -> x6, local copies, waits for them, and re-layouts: none -> 6.61 us
  transfers between devices with their start and end apart: 5 -> 5, of which waited for: 4 -> 4; matrix products, arithmetic and copies ran while one was open for 0% -> 0% of each run, Pallas kernels for 4% -> 3%
where the time goes in v7:
time: 173 us
  blocking collectives  122 us (71%)
  starting transfers between devices  19.8 us (11%)
  Pallas kernels  17.2 us (10%)
  waiting for transfers between devices  6.67 us (4%)
  local copies, waits for them, and re-layouts  6.61 us (4%)
    all_to_all x8, blocking collectives, exchange(): return lax.all_to_all(x, axes, 0, 0)  122 us
    unnamed x6, local copies, waits for them, and re-layouts  6.61 us
    ppermute x1, starting transfers between devices, per_device(): other_docs = lax.ppermute(docs, 'zl', swap)  4.83 us
    ppermute x1, starting transfers between devices, per_device(): other = lax.ppermute(own, 'core', swap)  4.41 us
    all_to_all x1, waiting for transfers between devices, exchange(): return lax.all_to_all(x, axes, 0, 0)  4.12 us
    all_to_all x1, starting transfers between devices, exchange(): return lax.all_to_all(x, axes, 0, 0)  3.86 us
    pallas_call x1, Pallas kernels, per_device(): call(functools.partial(first_rows, scale), (shape((row_peers, doc_rows //...  3.82 us
    ppermute x1, starting transfers between devices, per_device(): from_other = lax.ppermute(for_other, 'core', swap)  3.64 us
  transfers between devices with their start and end apart: 5, of which 4 were waited for; matrix products, arithmetic and copies ran while one was open for 0% of the time, Pallas kernels for 3%

profile of v7, /device:TPU:1, one launch (start us, length us, event | category | flops | bytes accessed | tf_op | source)
XLA Modules:
  0.0 172.8 jit_solution(15309145562067711551)
XLA Ops:
  0.6 4.8 %collective-permute-start = (bf16[1024,256]{1,0:T(8,128)(2,1)}, bf16[1024,256]{1,0:T(8,128)(2,1)S(1)}, u32[]{:S(2)}, u32[]{:S(2)}) collective-permute-start(bf16[1024,256]{1,0:T(8,128)(2,1)} %docs_hbm.1), channel_id=1, source_target_pairs={{0,32},{32,0},{1,33},{33,1},{2,34},{34,2},{3,35},{35,3},{4,36},{36... | collective-permute-start | bytes 1572872 | tf_op jit(solution)/shard_map/ppermute | solution.py:285
  5.5 3.8 %shard_map.59 = (f32[32,8,128]{2,1,0:T(8,128)S(1)}, bf16[1024,256]{1,0:T(8,128)(2,1)S(1)}, bf16[2048,256]{1,0:T(8,128)(2,1)S(1)}, f32[8,128]{1,0:T(8,128)S(1)}) custom-call(s32[64]{0:T(128)} %mass_hbm.1, s32[8,128]{1,0:T(8,128)} %bitcast.5, bf16[1024,256]{1,0:T(8,128)(2,1)} %docs_hbm.1, bf16[2048,256]{1,0:T(8,128)(2,1)} %cents_hbm.1), custom_call_target="tpu_custom_call" | custom-call | flops 1073741824 | bytes 1048576 | tf_op jit(solution)/shard_map/pallas_call | solution.py:286
  9.3 20.7 %all_to_all.45.parts_ref = f32[32,8,128]{2,1,0:T(8,128)S(1)} all-to-all(f32[32,8,128]{2,1,0:T(8,128)S(1)} %get-tuple-element.20), channel_id=1, replica_groups=mesh['y'=8,'zl'=2,'core'=2,'zh'=4,'x'=4] {'x','zl','zh'}, dimensions={0} | all-to-all | bytes 262144 | tf_op jit(solution)/shard_map/all_to_all | solution.py:268
  30.0 0.0 collective-permute-done.other_ref
  30.0 3.2 %shard_map.60 = (f32[16,8,128]{2,1,0:T(8,128)S(1)}, f32[1024,2048]{1,0:T(8,128)S(1)}, f32[8,128]{1,0:T(8,128)S(1)}, f32[16,128]{1,0:T(8,128)S(1)}, bf16[2048,256]{1,0:T(8,128)(2,1)S(1)}) custom-call(f32[32,8,128]{2,1,0:T(8,128)S(1)} %all_to_all.45.parts_ref, bf16[1024,256]{1,0:T(8,128)(2,1)S(1)} %get-tuple-element.21.docs_ref, ...), custom_call_target="tpu_custom_call" | custom-call | flops 1073741824 | bytes 1048576 | tf_op jit(solution)/shard_map/pallas_call | solution.py:302
  33.2 17.1 %all_to_all.46.parts_ref = f32[16,8,128]{2,1,0:T(8,128)S(1)} all-to-all(f32[16,8,128]{2,1,0:T(8,128)S(1)} %get-tuple-element.23), channel_id=1, replica_groups=mesh['y'=8,'zl'=2,'core'=2,'zh'=4,'x'=4] {'y','core'}, dimensions={0} | all-to-all | bytes 131072 | tf_op jit(solution)/shard_map/all_to_all | solution.py:268
  50.3 1.7 shard_map.61
  52.0 0.0 copy-start
  52.0 3.2 %copy-done = f32[1024,2048]{1,0:T(8,128)} copy-done((f32[1024,2048]{1,0:T(8,128)}, f32[1024,2048]{1,0:T(8,128)S(1)}, u32[]{:S(2)}) %copy-start) | copy-done | bytes 8388632
  55.2 3.9 %all-to-all-start.2 = ((bf16[32,16,128]{2,1,0:T(8,128)(2,1)}), bf16[32,16,128]{2,1,0:T(8,128)(2,1)S(1)}, u32[]{:S(2)}, u32[]{:S(2)}) async-start(bf16[32,16,128]{2,1,0:T(8,128)(2,1)} %get-tuple-element.26), calls=%async_computation.2 | async-start | bytes 262144 | tf_op jit(solution)/shard_map/all_to_all | solution.py:268
  59.1 3.1 %collective-permute-start.1 = (f32[8,128]{1,0:T(8,128)S(1)}, f32[8,128]{1,0:T(8,128)S(1)}, u32[]{:S(2)}, u32[]{:S(2)}) collective-permute-start(f32[8,128]{1,0:T(8,128)S(1)} %get-tuple-element.27.w_ref), channel_id=1, source_target_pairs={{0,32},{32,0},{1,33},{33,1},{2,34},{34,2},{3,35},{35,3},{4,36},{36... | collective-permute-start | bytes 12296 | tf_op jit(solution)/shard_map/ppermute | solution.py:299
  62.1 1.7 %collective-permute-done.1.other_w_ref = f32[8,128]{1,0:T(8,128)S(1)} collective-permute-done((f32[8,128]{1,0:T(8,128)S(1)}, f32[8,128]{1,0:T(8,128)S(1)}, u32[]{:S(2)}, u32[]{:S(2)}) %collective-permute-start.1) | collective-permute-done | bytes 4128 | tf_op jit(solution)/shard_map/ppermute | solution.py:299
  63.9 4.1 %all-to-all-done.2.parts_ref = bf16[32,16,128]{2,1,0:T(8,128)(2,1)S(1)} async-done(((bf16[32,16,128]{2,1,0:T(8,128)(2,1)}), bf16[32,16,128]{2,1,0:T(8,128)(2,1)S(1)}, u32[]{:S(2)}, u32[]{:S(2)}) %all-to-all-start.2) | async-done | bytes 131104 | tf_op jit(solution)/shard_map/all_to_all | solution.py:268
  68.0 0.0 copy-start.1
  68.0 3.4 %copy-done.1 = f32[1024,2048]{1,0:T(8,128)S(1)} copy-done((f32[1024,2048]{1,0:T(8,128)S(1)}, f32[1024,2048]{1,0:T(8,128)}, u32[]{:S(2)}) %copy-start.1) | copy-done | bytes 8388632
  71.4 0.0 copy-start.2
  71.4 0.7 shard_map.62
  72.0 12.3 %all_to_all.47.parts_ref = f32[16,8,128]{2,1,0:T(8,128)S(1)} all-to-all(f32[16,8,128]{2,1,0:T(8,128)S(1)} %shard_map.62), channel_id=1, replica_groups=mesh['y'=8,'zl'=2,'core'=2,'zh'=4,'x'=4] {'y','core'}, dimensions={0} | all-to-all | bytes 131072 | tf_op jit(solution)/shard_map/all_to_all | solution.py:268
  84.3 0.0 copy-done.2
  84.3 1.0 shard_map.63
  85.4 13.5 %all_to_all.48.parts_ref = bf16[32,16,128]{2,1,0:T(8,128)(2,1)S(1)} all-to-all(bf16[32,16,128]{2,1,0:T(8,128)(2,1)S(1)} %get-tuple-element.29), channel_id=1, replica_groups=mesh['y'=8,'zl'=2,'core'=2,'zh'=4,'x'=4] {'x','zl','zh'}, dimensions={0} | all-to-all | bytes 262144 | tf_op jit(solution)/shard_map/all_to_all | solution.py:268
  98.8 0.7 shard_map.64
  99.5 12.0 %all_to_all.49.parts_ref = f32[16,8,128]{2,1,0:T(8,128)S(1)} all-to-all(f32[16,8,128]{2,1,0:T(8,128)S(1)} %shard_map.64), channel_id=1, replica_groups=mesh['y'=8,'zl'=2,'core'=2,'zh'=4,'x'=4] {'y','core'}, dimensions={0} | all-to-all | bytes 131072 | tf_op jit(solution)/shard_map/all_to_all | solution.py:268
  111.5 1.0 shard_map.65
  112.5 12.8 %all_to_all.50.parts_ref = bf16[32,16,128]{2,1,0:T(8,128)(2,1)S(1)} all-to-all(bf16[32,16,128]{2,1,0:T(8,128)(2,1)S(1)} %get-tuple-element.31), channel_id=1, replica_groups=mesh['y'=8,'zl'=2,'core'=2,'zh'=4,'x'=4] {'x','zl','zh'}, dimensions={0} | all-to-all | bytes 262144 | tf_op jit(solution)/shard_map/all_to_all | solution.py:268
  125.3 1.8 %shard_map.66 = (f32[520,256]{1,0:T(8,128)S(1)}, f32[8,128]{1,0:T(8,128)}, f32[16,128]{1,0:T(8,128)S(1)}) custom-call(bf16[32,16,128]{2,1,0:T(8,128)(2,1)S(1)} %all_to_all.50.parts_ref, f32[8,128]{1,0:T(8,128)S(1)} %get-tuple-element.27.w_ref, f32[8,128]{1,0:T(8,128)S(1)} %collective-permute-done.1.other_w_ref, f32[16,128]{1,0:T(8,128)S(1)} %get-tuple-element.32.f_ref, ...), custom_call_target="tpu_custom_call" | custom-call | flops 536870912 | bytes 1048576 | tf_op jit(solution)/shard_map/pallas_call | solution.py:330
  127.1 3.6 %collective-permute-start.2 = (f32[520,256]{1,0:T(8,128)S(1)}, f32[520,256]{1,0:T(8,128)S(1)}, u32[]{:S(2)}, u32[]{:S(2)}) collective-permute-start(f32[520,256]{1,0:T(8,128)S(1)} %get-tuple-element.36), channel_id=1, source_target_pairs={{0,16},{16,0},{1,17},{17,1},{2,18},{18,2},{3,19},{19,3},{4,20},{20... | collective-permute-start | bytes 1597448 | tf_op jit(solution)/shard_map/ppermute | solution.py:337
  130.8 1.4 shard_map.67.own_ref
  132.2 0.1 collective-permute-done.2.other_ref
  132.3 0.1 shard_map.68
  132.4 15.0 %all_to_all.51.parts_ref = bf16[8,16,1152]{2,1,0:T(8,128)(2,1)S(1)} all-to-all(bf16[8,16,1152]{2,1,0:T(8,128)(2,1)S(1)} %shard_map.68), channel_id=1, replica_groups=mesh['y'=8,'zl'=2,'core'=2,'zh'=4,'x'=4] {'y'}, dimensions={0} | all-to-all | bytes 589824 | tf_op jit(solution)/shard_map/all_to_all | solution.py:268
  147.4 0.2 shard_map.69
  147.6 18.3 %all_to_all.52 = bf16[16,64,256]{2,1,0:T(8,128)(2,1)S(1)} all-to-all(bf16[16,64,256]{2,1,0:T(8,128)(2,1)S(1)} %shard_map.69), channel_id=1, replica_groups=mesh['y'=8,'zl'=2,'core'=2,'zh'=4,'x'=4] {'y','zl'}, dimensions={0} | all-to-all | bytes 1048576 | tf_op jit(solution)/shard_map/all_to_all | solution.py:268
  165.9 4.4 %collective-permute-start.3 = (bf16[1024,256]{1,0:T(8,128)(2,1)S(1)}, bf16[1024,256]{1,0:T(8,128)(2,1)S(1)}, u32[]{:S(2)}, u32[]{:S(2)}) collective-permute-start(bf16[1024,256]{1,0:T(8,128)(2,1)S(1)} %bitcast.3), channel_id=1, source_target_pairs={{0,16},{16,0},{1,17},{17,1},{2,18},{18,2},{3,19},{19,3},{4,20},{20... | collective-permute-start | bytes 1572872 | tf_op jit(solution)/shard_map/ppermute | solution.py:343
  170.3 0.8 shard_map.70._
  171.1 0.7 collective-permute-done.3.x_ref
  171.8 0.8 shard_map.71
Async XLA Ops:
  0.6 29.3 %collective-permute-start = (bf16[1024,256]{1,0:T(8,128)(2,1)}, bf16[1024,256]{1,0:T(8,128)(2,1)S(1)}, u32[]{:S(2)}, u32[]{:S(2)}) collective-permute-start(bf16[1024,256]{1,0:T(8,128)(2,1)} %docs_hbm.1), channel_id=1, source_target_pairs={{0,32},{32,0},{1,33},{33,1},{2,34},{34,2},{3,35},{35,3},{4,36},{36... | collective-permute-start | bytes 1572872 | tf_op jit(solution)/shard_map/ppermute | solution.py:285
  52.0 3.2 %copy-start = (f32[1024,2048]{1,0:T(8,128)}, f32[1024,2048]{1,0:T(8,128)S(1)}, u32[]{:S(2)}) copy-start(f32[1024,2048]{1,0:T(8,128)S(1)} %get-tuple-element.25.tile_ref) | copy-start | bytes 25165828
  55.2 12.8 %all-to-all-start.2 = ((bf16[32,16,128]{2,1,0:T(8,128)(2,1)}), bf16[32,16,128]{2,1,0:T(8,128)(2,1)S(1)}, u32[]{:S(2)}, u32[]{:S(2)}) async-start(bf16[32,16,128]{2,1,0:T(8,128)(2,1)} %get-tuple-element.26), calls=%async_computation.2 | async-start | bytes 262144 | tf_op jit(solution)/shard_map/all_to_all | solution.py:268
  59.1 4.8 %collective-permute-start.1 = (f32[8,128]{1,0:T(8,128)S(1)}, f32[8,128]{1,0:T(8,128)S(1)}, u32[]{:S(2)}, u32[]{:S(2)}) collective-permute-start(f32[8,128]{1,0:T(8,128)S(1)} %get-tuple-element.27.w_ref), channel_id=1, source_target_pairs={{0,32},{32,0},{1,33},{33,1},{2,34},{34,2},{3,35},{35,3},{4,36},{36... | collective-permute-start | bytes 12296 | tf_op jit(solution)/shard_map/ppermute | solution.py:299
  68.0 3.4 %copy-start.1 = (f32[1024,2048]{1,0:T(8,128)S(1)}, f32[1024,2048]{1,0:T(8,128)}, u32[]{:S(2)}) copy-start(f32[1024,2048]{1,0:T(8,128)} %copy-done) | copy-start | bytes 25165828
  71.4 13.0 %copy-start.2 = (f32[1024,2048]{1,0:T(8,128)S(1)}, f32[1024,2048]{1,0:T(8,128)}, u32[]{:S(2)}) copy-start(f32[1024,2048]{1,0:T(8,128)} %copy-done) | copy-start | bytes 25165828
  127.1 5.2 %collective-permute-start.2 = (f32[520,256]{1,0:T(8,128)S(1)}, f32[520,256]{1,0:T(8,128)S(1)}, u32[]{:S(2)}, u32[]{:S(2)}) collective-permute-start(f32[520,256]{1,0:T(8,128)S(1)} %get-tuple-element.36), channel_id=1, source_target_pairs={{0,16},{16,0},{1,17},{17,1},{2,18},{18,2},{3,19},{19,3},{4,20},{20... | collective-permute-start | bytes 1597448 | tf_op jit(solution)/shard_map/ppermute | solution.py:337
  165.9 5.9 %collective-permute-start.3 = (bf16[1024,256]{1,0:T(8,128)(2,1)S(1)}, bf16[1024,256]{1,0:T(8,128)(2,1)S(1)}, u32[]{:S(2)}, u32[]{:S(2)}) collective-permute-start(bf16[1024,256]{1,0:T(8,128)(2,1)S(1)} %bitcast.3), channel_id=1, source_target_pairs={{0,16},{16,0},{1,17},{17,1},{2,18},{18,2},{3,19},{19,3},{4,20},{20... | collective-permute-start | bytes 1572872 | tf_op jit(solution)/shard_map/ppermute | solution.py:343

commit v8 on v6

--- a/solution.py
+++ b/solution.py
@@ -61,24 +61,21 @@
 ):
     n_doc, n_cent = docs_hbm.shape[0], cents_hbm.shape[0]
     block = 512
-    steps = n_cent // block
-    copies = [pltpu.make_async_copy(docs_hbm, docs_ref, sems.at[steps])]
-    for q in range(steps):
-        rows = pl.ds(q * block, block)
-        copies.append(pltpu.make_async_copy(cents_hbm.at[rows, :], cents_ref.at[rows, :], sems.at[q]))
-    copies.append(pltpu.make_async_copy(mass_hbm, mass_ref, sems.at[steps + 1]))
-    copies.append(pltpu.make_async_copy(ids_hbm, ids_ref, sems.at[steps + 2]))
-    for copy in copies[-2:] + copies[:-2]:
+    copies = [
+        pltpu.make_async_copy(src, dst, sems.at[k])
+        for k, (src, dst) in enumerate(((mass_hbm, mass_ref), (ids_hbm, ids_ref), (docs_hbm, docs_ref), (cents_hbm, cents_ref)))
+    ]
+    for copy in copies:
         copy.start()
-    copies[steps + 1].wait()
-    copies[steps + 2].wait()
+    copies[0].wait()
+    copies[1].wait()
     w_ref[...] = weights_of(ids_ref[...], mass_ref)
-    copies[0].wait()
+    copies[2].wait()
+    copies[3].wait()
     groups = n_doc // 256
     tops = [jnp.full((8, 256), -jnp.inf, F32)] * groups
     totals = [jnp.zeros((8, 256), F32)] * groups
-    for q in range(steps):
-        copies[q + 1].wait()
+    for q in range(n_cent // block):
         cents = cents_ref[q * block : (q + 1) * block, :]
         for g in range(groups):
             s = nt_dot(cents, docs_ref[g * 256 : (g + 1) * 256, :]).reshape(block // 8, 8, 256)
@@ -294,7 +291,7 @@
         ),
         4,
         in_specs=[hbm] * 4,
-        scratch=[pltpu.SMEM(shard_mass.shape, jnp.int32), pltpu.VMEM((doc_rows // 2, LANES), jnp.int32), pltpu.SemaphoreType.DMA((7,))],
+        scratch=[pltpu.SMEM(shard_mass.shape, jnp.int32), pltpu.VMEM((doc_rows // 2, LANES), jnp.int32), pltpu.SemaphoreType.DMA((4,))],
         flops=2 * docs.shape[0] * cents.shape[0] * 256,
     )(*[pltpu.with_memory_space_constraint(x, pltpu.HBM) for x in (shard_mass, shard_ids.reshape(-1, LANES), docs, cents)])
     other_w = lax.ppermute(own_w, "zl", swap)
@@ -321,7 +318,7 @@
     parts, c = call(functools.partial(rows_after_first, log_target), rows_out, 3, flops=2 * n_doc * n_cent)(parts, top, tile)
     for turn in range(2):
         parts = exchange(parts, ROWS)
-        parts = call(columns_after, shape((col_peers, cent_rows, LANES), F32), 4, flops=2 * n_doc * n_cent)(parts, w, c, tile)
+        parts = call(columns_after, shape((col_peers, cent_rows, LANES), BF16), 4, flops=2 * n_doc * n_cent)(parts, w, c, tile)
         parts = exchange(parts, COLS)
         parts, c = call(functools.partial(rows_after, target), rows_out, 3, flops=2 * n_doc * n_cent)(parts, c, tile)
     parts = exchange(parts, ROWS)

time: 168 us -> 167 us (level)
  no operation moved by 1% of the time
where the time goes in v8:
time: 167 us; the launch traced here: 166 us
  blocking collectives  113 us (68%)
  starting transfers between devices  28.8 us (17%)
  Pallas kernels  17.3 us (10%)
  waiting for transfers between devices  6.57 us (4%)
    all_to_all x8, blocking collectives, exchange(): return lax.all_to_all(x, axes, 0, 0)  113 us
    all_to_all x1, starting transfers between devices, exchange(): return lax.all_to_all(x, axes, 0, 0)  12 us
    ppermute x1, starting transfers between devices, per_device(): other = lax.ppermute(own, 'core', swap)  5.19 us
    ppermute x1, starting transfers between devices, per_device(): other_docs = lax.ppermute(docs, 'zl', swap)  4.83 us
    pallas_call x1, Pallas kernels, per_device(): call(functools.partial(first_rows, scale), (shape((row_peers, doc_rows //...  4.55 us
    all_to_all x1, waiting for transfers between devices, exchange(): return lax.all_to_all(x, axes, 0, 0)  4.46 us
    ppermute x1, starting transfers between devices, per_device(): from_other = lax.ppermute(for_other, 'core', swap)  3.68 us
  transfers between devices with their start and end apart: 5, of which 4 were waited for; matrix products, arithmetic and copies ran while one was open for 0% of the time, Pallas kernels for 4%

profile of v8, /device:TPU:1, one launch (start us, length us, event | category | flops | bytes accessed | tf_op | source)
XLA Modules:
  0.0 166.5 jit_solution(13304641316804962620)
XLA Ops:
  0.6 4.8 %collective-permute-start.1 = (bf16[1024,256]{1,0:T(8,128)(2,1)}, bf16[1024,256]{1,0:T(8,128)(2,1)S(1)}, u32[]{:S(2)}, u32[]{:S(2)}) collective-permute-start(bf16[1024,256]{1,0:T(8,128)(2,1)} %docs_hbm.1), channel_id=1, source_target_pairs={{0,32},{32,0},{1,33},{33,1},{2,34},{34,2},{3,35},{35,3},{4,36},{36... | collective-permute-start | bytes 1572872 | tf_op jit(solution)/shard_map/ppermute | solution.py:283
  5.5 4.6 %shard_map.59 = (f32[32,8,128]{2,1,0:T(8,128)}, bf16[1024,256]{1,0:T(8,128)(2,1)S(1)}, bf16[2048,256]{1,0:T(8,128)(2,1)S(1)}, f32[8,128]{1,0:T(8,128)S(1)}) custom-call(s32[64]{0:T(128)} %mass_hbm.1, s32[8,128]{1,0:T(8,128)} %bitcast.5, bf16[1024,256]{1,0:T(8,128)(2,1)} %docs_hbm.1, bf16[2048,256]{1,0:T(8,128)(2,1)} %cents_hbm.1), custom_call_target="tpu_custom_call" | custom-call | flops 1073741824 | bytes 1048576 | tf_op jit(solution)/shard_map/pallas_call | solution.py:284
  10.0 12.0 %all-to-all-start = ((f32[32,8,128]{2,1,0:T(8,128)}), f32[32,8,128]{2,1,0:T(8,128)S(1)}, u32[]{:S(2)}, u32[]{:S(2)}) async-start(f32[32,8,128]{2,1,0:T(8,128)} %get-tuple-element.21), calls=%async_computation | async-start | bytes 262144 | tf_op jit(solution)/shard_map/all_to_all | solution.py:266
  22.0 3.1 %collective-permute-start = (f32[8,128]{1,0:T(8,128)S(1)}, f32[8,128]{1,0:T(8,128)S(1)}, u32[]{:S(2)}, u32[]{:S(2)}) collective-permute-start(f32[8,128]{1,0:T(8,128)S(1)} %get-tuple-element.22.own_w_ref), channel_id=1, source_target_pairs={{0,32},{32,0},{1,33},{33,1},{2,34},{34,2},{3,35},{35,3},{4,36},{36... | collective-permute-start | bytes 12296 | tf_op jit(solution)/shard_map/ppermute | solution.py:297
  25.2 1.3 collective-permute-done.other_w_ref
  26.5 4.5 %all-to-all-done.parts_ref = f32[32,8,128]{2,1,0:T(8,128)S(1)} async-done(((f32[32,8,128]{2,1,0:T(8,128)}), f32[32,8,128]{2,1,0:T(8,128)S(1)}, u32[]{:S(2)}, u32[]{:S(2)}) %all-to-all-start) | async-done | bytes 131104 | tf_op jit(solution)/shard_map/all_to_all | solution.py:266
  30.9 0.0 collective-permute-done.1.other_ref
  30.9 3.3 %shard_map.60 = (f32[16,8,128]{2,1,0:T(8,128)S(1)}, f32[1024,2048]{1,0:T(8,128)S(1)}, f32[8,128]{1,0:T(8,128)S(1)}, f32[16,128]{1,0:T(8,128)S(1)}, f32[16,128]{1,0:T(8,128)S(1)}, /*index=5*/bf16[2048,256]{1,0:T(8,128)(2,1)S(1)}) custom-call(f32[32,8,128]{2,1,0:T(8,128)S(1)} %all-to-all-done.parts_ref, f32[8,128]{1,0:T(8,128)S(1)} %get-tuple-element.22.own_w_ref, ...), custom_call_target="tpu_custom_call" | custom-call | flops 1073741824 | bytes 1048576 | tf_op jit(solution)/shard_map/pallas_call | solution.py:300
  34.2 17.0 %all_to_all.45.parts_ref = f32[16,8,128]{2,1,0:T(8,128)S(1)} all-to-all(f32[16,8,128]{2,1,0:T(8,128)S(1)} %get-tuple-element.25), channel_id=1, replica_groups=mesh['y'=8,'zl'=2,'core'=2,'zh'=4,'x'=4] {'y','core'}, dimensions={0} | all-to-all | bytes 131072 | tf_op jit(solution)/shard_map/all_to_all | solution.py:266
  51.3 1.0 shard_map.61
  52.3 13.7 %all_to_all.46.parts_ref = bf16[32,16,128]{2,1,0:T(8,128)(2,1)S(1)} all-to-all(bf16[32,16,128]{2,1,0:T(8,128)(2,1)S(1)} %get-tuple-element.28), channel_id=1, replica_groups=mesh['y'=8,'zl'=2,'core'=2,'zh'=4,'x'=4] {'x','zl','zh'}, dimensions={0} | all-to-all | bytes 262144 | tf_op jit(solution)/shard_map/all_to_all | solution.py:266
  66.0 0.7 shard_map.62
  66.7 11.6 %all_to_all.47.parts_ref = bf16[16,8,128]{2,1,0:T(8,128)(2,1)S(1)} all-to-all(bf16[16,8,128]{2,1,0:T(8,128)(2,1)S(1)} %shard_map.62), channel_id=1, replica_groups=mesh['y'=8,'zl'=2,'core'=2,'zh'=4,'x'=4] {'y','core'}, dimensions={0} | all-to-all | bytes 65536 | tf_op jit(solution)/shard_map/all_to_all | solution.py:266
  78.3 1.0 shard_map.63
  79.3 12.9 %all_to_all.48.parts_ref = bf16[32,16,128]{2,1,0:T(8,128)(2,1)S(1)} all-to-all(bf16[32,16,128]{2,1,0:T(8,128)(2,1)S(1)} %get-tuple-element.31), channel_id=1, replica_groups=mesh['y'=8,'zl'=2,'core'=2,'zh'=4,'x'=4] {'x','zl','zh'}, dimensions={0} | all-to-all | bytes 262144 | tf_op jit(solution)/shard_map/all_to_all | solution.py:266
  92.2 0.7 shard_map.64
  92.9 11.7 %all_to_all.49.parts_ref = bf16[16,8,128]{2,1,0:T(8,128)(2,1)S(1)} all-to-all(bf16[16,8,128]{2,1,0:T(8,128)(2,1)S(1)} %shard_map.64), channel_id=1, replica_groups=mesh['y'=8,'zl'=2,'core'=2,'zh'=4,'x'=4] {'y','core'}, dimensions={0} | all-to-all | bytes 65536 | tf_op jit(solution)/shard_map/all_to_all | solution.py:266
  104.5 1.0 shard_map.65
  105.6 12.7 %all_to_all.50.parts_ref = bf16[32,16,128]{2,1,0:T(8,128)(2,1)S(1)} all-to-all(bf16[32,16,128]{2,1,0:T(8,128)(2,1)S(1)} %get-tuple-element.33), channel_id=1, replica_groups=mesh['y'=8,'zl'=2,'core'=2,'zh'=4,'x'=4] {'x','zl','zh'}, dimensions={0} | all-to-all | bytes 262144 | tf_op jit(solution)/shard_map/all_to_all | solution.py:266
  118.3 1.9 %shard_map.66 = (f32[520,256]{1,0:T(8,128)S(1)}, f32[8,128]{1,0:T(8,128)}, f32[16,128]{1,0:T(8,128)S(1)}) custom-call(bf16[32,16,128]{2,1,0:T(8,128)(2,1)S(1)} %all_to_all.50.parts_ref, f32[16,128]{1,0:T(8,128)S(1)} %get-tuple-element.29.w_ref, f32[16,128]{1,0:T(8,128)S(1)} %get-tuple-element.34.f_ref, f32[8,128]{1,0:T(8,128)S(1)} %get-tuple-element.35.c_ref, ...), custom_call_target="tpu_custom_call" | custom-call | flops 536870912 | bytes 1048576 | tf_op jit(solution)/shard_map/pallas_call | solution.py:329
  120.1 3.7 %collective-permute-start.2 = (f32[520,256]{1,0:T(8,128)S(1)}, f32[520,256]{1,0:T(8,128)S(1)}, u32[]{:S(2)}, u32[]{:S(2)}) collective-permute-start(f32[520,256]{1,0:T(8,128)S(1)} %get-tuple-element.38), channel_id=1, source_target_pairs={{0,16},{16,0},{1,17},{17,1},{2,18},{18,2},{3,19},{19,3},{4,20},{20... | collective-permute-start | bytes 1597448 | tf_op jit(solution)/shard_map/ppermute | solution.py:336
  123.8 1.4 shard_map.67.own_ref
  125.2 0.1 collective-permute-done.2.other_ref
  125.4 0.1 shard_map.68
  125.4 15.0 %all_to_all.51.parts_ref = bf16[8,16,1152]{2,1,0:T(8,128)(2,1)S(1)} all-to-all(bf16[8,16,1152]{2,1,0:T(8,128)(2,1)S(1)} %shard_map.68), channel_id=1, replica_groups=mesh['y'=8,'zl'=2,'core'=2,'zh'=4,'x'=4] {'y'}, dimensions={0} | all-to-all | bytes 589824 | tf_op jit(solution)/shard_map/all_to_all | solution.py:266
  140.5 0.2 shard_map.69
  140.6 18.2 %all_to_all.52 = bf16[16,64,256]{2,1,0:T(8,128)(2,1)S(1)} all-to-all(bf16[16,64,256]{2,1,0:T(8,128)(2,1)S(1)} %shard_map.69), channel_id=1, replica_groups=mesh['y'=8,'zl'=2,'core'=2,'zh'=4,'x'=4] {'y','zl'}, dimensions={0} | all-to-all | bytes 1048576 | tf_op jit(solution)/shard_map/all_to_all | solution.py:266
  158.8 5.2 %collective-permute-start.3 = (bf16[1024,256]{1,0:T(8,128)(2,1)S(1)}, bf16[1024,256]{1,0:T(8,128)(2,1)S(1)}, u32[]{:S(2)}, u32[]{:S(2)}) collective-permute-start(bf16[1024,256]{1,0:T(8,128)(2,1)S(1)} %bitcast.3), channel_id=1, source_target_pairs={{0,16},{16,0},{1,17},{17,1},{2,18},{18,2},{3,19},{19,3},{4,20},{20... | collective-permute-start | bytes 1572872 | tf_op jit(solution)/shard_map/ppermute | solution.py:342
  164.0 0.8 shard_map.70._
  164.8 0.7 collective-permute-done.3.x_ref
  165.5 0.8 shard_map.71
Async XLA Ops:
  0.6 30.3 %collective-permute-start.1 = (bf16[1024,256]{1,0:T(8,128)(2,1)}, bf16[1024,256]{1,0:T(8,128)(2,1)S(1)}, u32[]{:S(2)}, u32[]{:S(2)}) collective-permute-start(bf16[1024,256]{1,0:T(8,128)(2,1)} %docs_hbm.1), channel_id=1, source_target_pairs={{0,32},{32,0},{1,33},{33,1},{2,34},{34,2},{3,35},{35,3},{4,36},{36... | collective-permute-start | bytes 1572872 | tf_op jit(solution)/shard_map/ppermute | solution.py:283
  10.0 20.9 %all-to-all-start = ((f32[32,8,128]{2,1,0:T(8,128)}), f32[32,8,128]{2,1,0:T(8,128)S(1)}, u32[]{:S(2)}, u32[]{:S(2)}) async-start(f32[32,8,128]{2,1,0:T(8,128)} %get-tuple-element.21), calls=%async_computation | async-start | bytes 262144 | tf_op jit(solution)/shard_map/all_to_all | solution.py:266
  22.0 4.4 %collective-permute-start = (f32[8,128]{1,0:T(8,128)S(1)}, f32[8,128]{1,0:T(8,128)S(1)}, u32[]{:S(2)}, u32[]{:S(2)}) collective-permute-start(f32[8,128]{1,0:T(8,128)S(1)} %get-tuple-element.22.own_w_ref), channel_id=1, source_target_pairs={{0,32},{32,0},{1,33},{33,1},{2,34},{34,2},{3,35},{35,3},{4,36},{36... | collective-permute-start | bytes 12296 | tf_op jit(solution)/shard_map/ppermute | solution.py:297
  120.1 5.2 %collective-permute-start.2 = (f32[520,256]{1,0:T(8,128)S(1)}, f32[520,256]{1,0:T(8,128)S(1)}, u32[]{:S(2)}, u32[]{:S(2)}) collective-permute-start(f32[520,256]{1,0:T(8,128)S(1)} %get-tuple-element.38), channel_id=1, source_target_pairs={{0,16},{16,0},{1,17},{17,1},{2,18},{18,2},{3,19},{19,3},{4,20},{20... | collective-permute-start | bytes 1597448 | tf_op jit(solution)/shard_map/ppermute | solution.py:336
  158.8 6.7 %collective-permute-start.3 = (bf16[1024,256]{1,0:T(8,128)(2,1)S(1)}, bf16[1024,256]{1,0:T(8,128)(2,1)S(1)}, u32[]{:S(2)}, u32[]{:S(2)}) collective-permute-start(bf16[1024,256]{1,0:T(8,128)(2,1)S(1)} %bitcast.3), channel_id=1, source_target_pairs={{0,16},{16,0},{1,17},{17,1},{2,18},{18,2},{3,19},{19,3},{4,20},{20... | collective-permute-start | bytes 1572872 | tf_op jit(solution)/shard_map/ppermute | solution.py:342

commit v9 on v7

--- a/solution.py
+++ b/solution.py
@@ -145,16 +145,19 @@
             p = tile_ref[r * LANES : (r + 1) * LANES, g * LANES : (g + 1) * LANES] * col
             totals[g] = totals[g] + jnp.sum(p.reshape(LANES // 8, 8, LANES), axis=0)
     rows = jnp.concatenate([jnp.sum(t, axis=0, keepdims=True) for t in totals], axis=0)
-    out_ref[...] = jnp.broadcast_to(rows[None], out_ref.shape).astype(out_ref.dtype)
-
-
-def rows_after_first(log_target, parts_ref, top_ref, tile_ref, out_ref, c_ref):
+    out_ref[:, 0:groups, :] = jnp.broadcast_to(rows[None], (out_ref.shape[0], groups, LANES)).astype(out_ref.dtype)
+
+
+def rows_after_first(log_target, parts_ref, top_ref, w_ref, tile_ref, out_ref, c_ref):
     parts = parts_ref[...]
     top = jnp.max(parts, axis=0)
     lse = top + jnp.log2(jnp.sum(jnp.exp2(parts - top[None]), axis=0))
     c = jnp.exp2(top_ref[...] + (log_target - lse))
     c_ref[...] = c
     weigh_columns(c, tile_ref, out_ref)
+    w = w_ref[...]
+    groups = out_ref.shape[1] - w.shape[0]
+    out_ref[:, groups:, :] = jnp.broadcast_to(w[None], (out_ref.shape[0], *w.shape)).astype(out_ref.dtype)
 
 
 def rows_after(target, parts_ref, last_ref, tile_ref, out_ref, c_ref):
@@ -163,14 +166,19 @@
     weigh_columns(c, tile_ref, out_ref)
 
 
-def in_order(own, other):
-    first = lax.axis_index("zl") == 0
-    return jnp.concatenate([jnp.where(first, own, other), jnp.where(first, other, own)], axis=0)
-
-
-def columns_after(parts_ref, w_ref, other_w_ref, c_ref, tile_ref, out_ref):
+def columns_after_first(n_zh, parts_ref, c_ref, tile_ref, out_ref, w_ref):
+    groups = w_ref.shape[0]
+    w = jnp.concatenate([parts_ref[z * n_zh, groups:, :].astype(F32) for z in range(2)], axis=0)
+    w_ref[...] = w
+    weigh_rows(w / jnp.sum(parts_ref[:, 0:groups, :].astype(F32), axis=0), c_ref, tile_ref, out_ref)
+
+
+def columns_after(parts_ref, w_ref, c_ref, tile_ref, out_ref):
+    weigh_rows(w_ref[...] / jnp.sum(parts_ref[...].astype(F32), axis=0), c_ref, tile_ref, out_ref)
+
+
+def weigh_rows(u, c_ref, tile_ref, out_ref):
     groups = tile_ref.shape[1] // LANES
-    u = in_order(w_ref[...], other_w_ref[...]) / jnp.sum(parts_ref[...].astype(F32), axis=0)
     lane = lane_iota()
     sums = jnp.zeros((LANES, LANES), F32)
     for r in range(tile_ref.shape[0] // LANES):
@@ -207,8 +215,8 @@
         out_ref[rows, :] = jnp.dot(p_ref[rows, :], docs_ref[...], preferred_element_type=F32)
 
 
-def final_other(parts_ref, w_ref, other_w_ref, f_ref, c_ref, tile_ref, docs_ref, out_ref, pot_ref, u_ref, p_ref):
-    u = in_order(w_ref[...], other_w_ref[...]) / jnp.sum(parts_ref[...].astype(F32), axis=0)
+def final_other(parts_ref, w_ref, f_ref, c_ref, tile_ref, docs_ref, out_ref, pot_ref, u_ref, p_ref):
+    u = w_ref[...] / jnp.sum(parts_ref[...].astype(F32), axis=0)
     u_ref[...] = u
     pot = (f_ref[...] + jnp.log2(u)) * LN2
     pot_ref[...] = jnp.where(lax.axis_index("zl") == 0, pot[0:8, :], pot[8:16, :])
@@ -250,11 +258,14 @@
         out_ref[:, i * 16 : (i + 1) * 16, :] = jnp.broadcast_to(new[None], (out_ref.shape[0], 16, 256))
 
 
-def place_own(x_ref, out_ref, sem):
+def place_own(x_ref, pot_ref, out_ref, pot_out_ref, sems):
     rows = x_ref.shape[0]
-    copy = pltpu.make_async_copy(x_ref, out_ref.at[pl.ds(pl.multiple_of(lax.axis_index("core") * rows, rows), rows), :], sem)
-    copy.start()
-    copy.wait()
+    place = pl.ds(pl.multiple_of(lax.axis_index("core") * rows, rows), rows)
+    copies = [pltpu.make_async_copy(x_ref, out_ref.at[place, :], sems.at[0]), pltpu.make_async_copy(pot_ref, pot_out_ref, sems.at[1])]
+    for copy in copies:
+        copy.start()
+    for copy in copies:
+        copy.wait()
 
 
 def place_other(x_ref, _, out_ref, sem):
@@ -296,7 +307,6 @@
         scratch=[pltpu.SMEM(shard_mass.shape, jnp.int32), pltpu.VMEM((doc_rows // 2, LANES), jnp.int32), pltpu.SemaphoreType.DMA((4,))],
         flops=2 * docs.shape[0] * cents.shape[0] * 256,
     )(*[pltpu.with_memory_space_constraint(x, pltpu.HBM) for x in (shard_mass, shard_ids.reshape(-1, LANES), docs, cents)])
-    other_w = lax.ppermute(own_w, "zl", swap)
     parts = exchange(parts, ROWS)
     chunk = n_cent // col_peers
     parts, tile, top, f, docs_all = call(
@@ -316,10 +326,16 @@
     rows_out = (shape((row_peers, doc_rows, LANES), BF16), small)
     parts = exchange(parts, COLS)
     log_target = math.log2(target)
-    parts, c = call(functools.partial(rows_after_first, log_target), rows_out, 3, flops=2 * n_doc * n_cent)(parts, top, tile)
+    first_out = (shape((row_peers, doc_rows + doc_rows // 2, LANES), BF16), small)
+    parts, c = call(functools.partial(rows_after_first, log_target), first_out, 4, flops=2 * n_doc * n_cent)(parts, top, own_w, tile)
+    col_out = shape((col_peers, cent_rows, LANES), BF16)
     for turn in range(2):
         parts = exchange(parts, ROWS)
-        parts = call(columns_after, shape((col_peers, cent_rows, LANES), F32), 5, flops=2 * n_doc * n_cent)(parts, own_w, other_w, c, tile)
+        if turn == 0:
+            out = (col_out, shape((doc_rows, LANES), F32))
+            parts, w = call(functools.partial(columns_after_first, n_zh), out, 3, flops=2 * n_doc * n_cent)(parts, c, tile)
+        else:
+            parts = call(columns_after, col_out, 4, flops=2 * n_doc * n_cent)(parts, w, c, tile)
         parts = exchange(parts, COLS)
         parts, c = call(functools.partial(rows_after, target), rows_out, 3, flops=2 * n_doc * n_cent)(parts, c, tile)
     parts = exchange(parts, ROWS)
@@ -329,11 +345,11 @@
     p_scratch = [pltpu.VMEM((n_half, n_doc), BF16)]
     for_other, pot, u = call(
         final_other,
-        (part_shape, shape((doc_rows // 2, LANES), F32), shape((doc_rows, LANES), F32)),
-        7,
+        (part_shape, pltpu.VMEM((doc_rows // 2, LANES), F32), shape((doc_rows, LANES), F32)),
+        6,
         scratch=p_scratch,
         flops=half_flops,
-    )(parts, own_w, other_w, f, c, tile, docs_all)
+    )(parts, w, f, c, tile, docs_all)
     from_other = lax.ppermute(for_other, "core", swap)
     for_own = call(final_own, part_shape, 4, scratch=p_scratch, flops=half_flops)(u, c, tile, docs_all)
     sums = call(final_join, shape((n_y, 16, 2 * LANES * (chunk // 16) + LANES), BF16), 2)(for_own, from_other)
@@ -342,7 +358,14 @@
     own = exchange(new, ("y", "zl")).reshape(n_y * n_zl * chunk, 256)
     other = lax.ppermute(own, "core", swap)
     placed = shape((cents.shape[0], 256), BF16)
-    new = call(place_own, placed, 1, in_specs=[any_space], out_specs=any_space, scratch=[pltpu.SemaphoreType.DMA])(own)
+    new, pot = call(
+        place_own,
+        (placed, shape((doc_rows // 2, LANES), F32)),
+        2,
+        in_specs=[any_space, pl.BlockSpec(memory_space=pltpu.VMEM)],
+        out_specs=(any_space, any_space),
+        scratch=[pltpu.SemaphoreType.DMA((2,))],
+    )(own, pot)
     new = call(
         place_other, placed, 2, in_specs=[any_space, any_space], out_specs=any_space, scratch=[pltpu.SemaphoreType.DMA], alias={1: 0}
     )(other, new)

time: 173 us -> 166 us (0.960)
  blocking collectives: 122 us -> 134 us
  local copies, waits for them, and re-layouts: 6.61 us -> 0 us
  starting transfers between devices: 19.8 us -> 13.7 us
  waiting for transfers between devices: 6.67 us -> 0.8 us
    all_to_all x8 -> x9, blocking collectives: 122 us -> 134 us  [exchange(): return lax.all_to_all(x, axes, 0, 0)]
    unnamed x6 -> x0, local copies, waits for them, and re-layouts: 6.61 us -> none
    all_to_all x1 -> x0, waiting for transfers between devices: 4.12 us -> none  [exchange(): return lax.all_to_all(x, axes, 0, 0)]
    all_to_all x1 -> x0, starting transfers between devices: 3.86 us -> none  [exchange(): return lax.all_to_all(x, axes, 0, 0)]
    ppermute x1 -> x0, starting transfers between devices: 3.06 us -> none  [per_device(): other_w = lax.ppermute(own_w, 'zl', swap)]
    ppermute x1 -> x0, waiting for transfers between devices: 1.73 us -> none  [per_device(): other_w = lax.ppermute(own_w, 'zl', swap)]
  transfers between devices with their start and end apart: 5 -> 3, of which waited for: 4 -> 2; matrix products, arithmetic and copies ran while one was open for 0% -> 0% of each run, Pallas kernels for 3% -> 4%
where the time goes in v9:
time: 166 us; the launch traced here: 165 us
  blocking collectives  134 us (81%)
  Pallas kernels  16.1 us (10%)
  starting transfers between devices  13.7 us (8%)
    all_to_all x9, blocking collectives, exchange(): return lax.all_to_all(x, axes, 0, 0)  134 us
    ppermute x1, starting transfers between devices, per_device(): other = lax.ppermute(own, 'core', swap)  5.17 us
    ppermute x1, starting transfers between devices, per_device(): other_docs = lax.ppermute(docs, 'zl', swap)  4.83 us
    pallas_call x1, Pallas kernels, per_device(): call(functools.partial(first_rows, scale), (shape((row_peers, doc_rows //...  3.83 us
    ppermute x1, starting transfers between devices, per_device(): from_other = lax.ppermute(for_other, 'core', swap)  3.69 us
  transfers between devices with their start and end apart: 3, of which 2 were waited for; matrix products, arithmetic and copies ran while one was open for 0% of the time, Pallas kernels for 4%

profile of v9, /device:TPU:1, one launch (start us, length us, event | category | flops | bytes accessed | tf_op | source)
XLA Modules:
  0.0 165.2 jit_solution(8962455552450041097)
XLA Ops:
  0.6 4.8 %collective-permute-start = (bf16[1024,256]{1,0:T(8,128)(2,1)}, bf16[1024,256]{1,0:T(8,128)(2,1)S(1)}, u32[]{:S(2)}, u32[]{:S(2)}) collective-permute-start(bf16[1024,256]{1,0:T(8,128)(2,1)} %docs_hbm.1), channel_id=1, source_target_pairs={{0,32},{32,0},{1,33},{33,1},{2,34},{34,2},{3,35},{35,3},{4,36},{36... | collective-permute-start | bytes 1572872 | tf_op jit(solution)/shard_map/ppermute | solution.py:296
  5.5 3.8 %shard_map.59 = (f32[32,8,128]{2,1,0:T(8,128)S(1)}, bf16[1024,256]{1,0:T(8,128)(2,1)S(1)}, bf16[2048,256]{1,0:T(8,128)(2,1)S(1)}, f32[8,128]{1,0:T(8,128)S(1)}) custom-call(s32[64]{0:T(128)} %mass_hbm.1, s32[8,128]{1,0:T(8,128)} %bitcast.5, bf16[1024,256]{1,0:T(8,128)(2,1)} %docs_hbm.1, bf16[2048,256]{1,0:T(8,128)(2,1)} %cents_hbm.1), custom_call_target="tpu_custom_call" | custom-call | flops 1073741824 | bytes 1048576 | tf_op jit(solution)/shard_map/pallas_call | solution.py:297
  9.3 20.7 %all_to_all.45.parts_ref = f32[32,8,128]{2,1,0:T(8,128)S(1)} all-to-all(f32[32,8,128]{2,1,0:T(8,128)S(1)} %get-tuple-element.24), channel_id=1, replica_groups=mesh['y'=8,'zl'=2,'core'=2,'zh'=4,'x'=4] {'x','zl','zh'}, dimensions={0} | all-to-all | bytes 262144 | tf_op jit(solution)/shard_map/all_to_all | solution.py:279
  30.0 0.0 collective-permute-done.other_ref
  30.0 3.2 %shard_map.60 = (f32[16,8,128]{2,1,0:T(8,128)S(1)}, f32[1024,2048]{1,0:T(8,128)S(1)}, f32[8,128]{1,0:T(8,128)S(1)}, f32[16,128]{1,0:T(8,128)S(1)}, bf16[2048,256]{1,0:T(8,128)(2,1)S(1)}) custom-call(f32[32,8,128]{2,1,0:T(8,128)S(1)} %all_to_all.45.parts_ref, bf16[1024,256]{1,0:T(8,128)(2,1)S(1)} %get-tuple-element.25.docs_ref, ...), custom_call_target="tpu_custom_call" | custom-call | flops 1073741824 | bytes 1048576 | tf_op jit(solution)/shard_map/pallas_call | solution.py:312
  33.2 17.1 %all_to_all.46.parts_ref = f32[16,8,128]{2,1,0:T(8,128)S(1)} all-to-all(f32[16,8,128]{2,1,0:T(8,128)S(1)} %get-tuple-element.27), channel_id=1, replica_groups=mesh['y'=8,'zl'=2,'core'=2,'zh'=4,'x'=4] {'y','core'}, dimensions={0} | all-to-all | bytes 131072 | tf_op jit(solution)/shard_map/all_to_all | solution.py:279
  50.3 1.0 shard_map.61
  51.3 12.6 %all_to_all.47.parts_ref = bf16[32,24,128]{2,1,0:T(8,128)(2,1)S(1)} all-to-all(bf16[32,24,128]{2,1,0:T(8,128)(2,1)S(1)} %get-tuple-element.31), channel_id=1, replica_groups=mesh['y'=8,'zl'=2,'core'=2,'zh'=4,'x'=4] {'x','zl','zh'}, dimensions={0} | all-to-all | bytes 393216 | tf_op jit(solution)/shard_map/all_to_all | solution.py:279
  63.9 0.7 shard_map.62
  64.6 11.9 %all_to_all.48.parts_ref = bf16[16,8,128]{2,1,0:T(8,128)(2,1)S(1)} all-to-all(bf16[16,8,128]{2,1,0:T(8,128)(2,1)S(1)} %get-tuple-element.33), channel_id=1, replica_groups=mesh['y'=8,'zl'=2,'core'=2,'zh'=4,'x'=4] {'y','core'}, dimensions={0} | all-to-all | bytes 65536 | tf_op jit(solution)/shard_map/all_to_all | solution.py:279
  76.5 1.0 shard_map.63
  77.5 13.9 %all_to_all.49.parts_ref = bf16[32,16,128]{2,1,0:T(8,128)(2,1)S(1)} all-to-all(bf16[32,16,128]{2,1,0:T(8,128)(2,1)S(1)} %get-tuple-element.34), channel_id=1, replica_groups=mesh['y'=8,'zl'=2,'core'=2,'zh'=4,'x'=4] {'x','zl','zh'}, dimensions={0} | all-to-all | bytes 262144 | tf_op jit(solution)/shard_map/all_to_all | solution.py:279
  91.4 0.7 shard_map.64
  92.1 11.7 %all_to_all.50.parts_ref = bf16[16,8,128]{2,1,0:T(8,128)(2,1)S(1)} all-to-all(bf16[16,8,128]{2,1,0:T(8,128)(2,1)S(1)} %shard_map.64), channel_id=1, replica_groups=mesh['y'=8,'zl'=2,'core'=2,'zh'=4,'x'=4] {'y','core'}, dimensions={0} | all-to-all | bytes 65536 | tf_op jit(solution)/shard_map/all_to_all | solution.py:279
  103.7 1.0 shard_map.65
  104.8 12.7 %all_to_all.51.parts_ref = bf16[32,16,128]{2,1,0:T(8,128)(2,1)S(1)} all-to-all(bf16[32,16,128]{2,1,0:T(8,128)(2,1)S(1)} %get-tuple-element.37), channel_id=1, replica_groups=mesh['y'=8,'zl'=2,'core'=2,'zh'=4,'x'=4] {'x','zl','zh'}, dimensions={0} | all-to-all | bytes 262144 | tf_op jit(solution)/shard_map/all_to_all | solution.py:279
  117.5 1.4 shard_map.66
  118.9 3.7 %collective-permute-start.1 = (f32[520,256]{1,0:T(8,128)S(1)}, f32[520,256]{1,0:T(8,128)S(1)}, u32[]{:S(2)}, u32[]{:S(2)}) collective-permute-start(f32[520,256]{1,0:T(8,128)S(1)} %get-tuple-element.42), channel_id=1, source_target_pairs={{0,16},{16,0},{1,17},{17,1},{2,18},{18,2},{3,19},{19,3},{4,20},{20... | collective-permute-start | bytes 1597448 | tf_op jit(solution)/shard_map/ppermute | solution.py:353
  122.6 1.4 shard_map.67.own_ref
  124.0 0.1 collective-permute-done.1.other_ref
  124.1 0.1 shard_map.68
  124.2 15.0 %all_to_all.52.parts_ref = bf16[8,16,1152]{2,1,0:T(8,128)(2,1)S(1)} all-to-all(bf16[8,16,1152]{2,1,0:T(8,128)(2,1)S(1)} %shard_map.68), channel_id=1, replica_groups=mesh['y'=8,'zl'=2,'core'=2,'zh'=4,'x'=4] {'y'}, dimensions={0} | all-to-all | bytes 589824 | tf_op jit(solution)/shard_map/all_to_all | solution.py:279
  139.2 0.2 shard_map.69
  139.4 18.2 %all_to_all.53 = bf16[16,64,256]{2,1,0:T(8,128)(2,1)S(1)} all-to-all(bf16[16,64,256]{2,1,0:T(8,128)(2,1)S(1)} %shard_map.69), channel_id=1, replica_groups=mesh['y'=8,'zl'=2,'core'=2,'zh'=4,'x'=4] {'y','zl'}, dimensions={0} | all-to-all | bytes 1048576 | tf_op jit(solution)/shard_map/all_to_all | solution.py:279
  157.6 5.2 %collective-permute-start.2 = (bf16[1024,256]{1,0:T(8,128)(2,1)S(1)}, bf16[1024,256]{1,0:T(8,128)(2,1)S(1)}, u32[]{:S(2)}, u32[]{:S(2)}) collective-permute-start(bf16[1024,256]{1,0:T(8,128)(2,1)S(1)} %bitcast.3), channel_id=1, source_target_pairs={{0,16},{16,0},{1,17},{17,1},{2,18},{18,2},{3,19},{19,3},{4,20},{20... | collective-permute-start | bytes 1572872 | tf_op jit(solution)/shard_map/ppermute | solution.py:359
  162.8 0.8 shard_map.70
  163.6 0.7 collective-permute-done.2.x_ref
  164.3 0.8 shard_map.71
Async XLA Ops:
  0.6 29.3 %collective-permute-start = (bf16[1024,256]{1,0:T(8,128)(2,1)}, bf16[1024,256]{1,0:T(8,128)(2,1)S(1)}, u32[]{:S(2)}, u32[]{:S(2)}) collective-permute-start(bf16[1024,256]{1,0:T(8,128)(2,1)} %docs_hbm.1), channel_id=1, source_target_pairs={{0,32},{32,0},{1,33},{33,1},{2,34},{34,2},{3,35},{35,3},{4,36},{36... | collective-permute-start | bytes 1572872 | tf_op jit(solution)/shard_map/ppermute | solution.py:296
  118.9 5.2 %collective-permute-start.1 = (f32[520,256]{1,0:T(8,128)S(1)}, f32[520,256]{1,0:T(8,128)S(1)}, u32[]{:S(2)}, u32[]{:S(2)}) collective-permute-start(f32[520,256]{1,0:T(8,128)S(1)} %get-tuple-element.42), channel_id=1, source_target_pairs={{0,16},{16,0},{1,17},{17,1},{2,18},{18,2},{3,19},{19,3},{4,20},{20... | collective-permute-start | bytes 1597448 | tf_op jit(solution)/shard_map/ppermute | solution.py:353
  157.6 6.7 %collective-permute-start.2 = (bf16[1024,256]{1,0:T(8,128)(2,1)S(1)}, bf16[1024,256]{1,0:T(8,128)(2,1)S(1)}, u32[]{:S(2)}, u32[]{:S(2)}) collective-permute-start(bf16[1024,256]{1,0:T(8,128)(2,1)S(1)} %bitcast.3), channel_id=1, source_target_pairs={{0,16},{16,0},{1,17},{17,1},{2,18},{18,2},{3,19},{19,3},{4,20},{20... | collective-permute-start | bytes 1572872 | tf_op jit(solution)/shard_map/ppermute | solution.py:359

commit v10 on v9

--- a/solution.py
+++ b/solution.py
@@ -137,10 +137,9 @@
 
 def weigh_columns(c, tile_ref, out_ref):
     groups = tile_ref.shape[1] // LANES
-    cols = to_columns(c)
     totals = [jnp.zeros((8, LANES), F32) for _ in range(groups)]
     for r in range(tile_ref.shape[0] // LANES):
-        col = jnp.broadcast_to(cols[:, r : r + 1], (LANES, LANES))
+        col = jnp.broadcast_to(c[r : r + 1, :], (LANES, LANES)).T
         for g in range(groups):
             p = tile_ref[r * LANES : (r + 1) * LANES, g * LANES : (g + 1) * LANES] * col
             totals[g] = totals[g] + jnp.sum(p.reshape(LANES // 8, 8, LANES), axis=0)

time: 166 us -> 165 us (level)
  no operation moved by 1% of the time
where the time goes in v10:
time: 165 us; the launch traced here: 164 us
  blocking collectives  134 us (81%)
  Pallas kernels  15.1 us (9%)
  starting transfers between devices  13.7 us (8%)
    all_to_all x9, blocking collectives, exchange(): return lax.all_to_all(x, axes, 0, 0)  134 us
    ppermute x1, starting transfers between devices, per_device(): other = lax.ppermute(own, 'core', swap)  5.19 us
    ppermute x1, starting transfers between devices, per_device(): other_docs = lax.ppermute(docs, 'zl', swap)  4.83 us
    pallas_call x1, Pallas kernels, per_device(): call(functools.partial(first_rows, scale), (shape((row_peers, doc_rows //...  3.83 us
    ppermute x1, starting transfers between devices, per_device(): from_other = lax.ppermute(for_other, 'core', swap)  3.69 us
  transfers between devices with their start and end apart: 3, of which 2 were waited for; matrix products, arithmetic and copies ran while one was open for 0% of the time, Pallas kernels for 4%

profile of v10, /device:TPU:1, one launch (start us, length us, event | category | flops | bytes accessed | tf_op | source)
XLA Modules:
  0.0 164.2 jit_solution(406380952565985140)
XLA Ops:
  0.6 4.8 %collective-permute-start = (bf16[1024,256]{1,0:T(8,128)(2,1)}, bf16[1024,256]{1,0:T(8,128)(2,1)S(1)}, u32[]{:S(2)}, u32[]{:S(2)}) collective-permute-start(bf16[1024,256]{1,0:T(8,128)(2,1)} %docs_hbm.1), channel_id=1, source_target_pairs={{0,32},{32,0},{1,33},{33,1},{2,34},{34,2},{3,35},{35,3},{4,36},{36... | collective-permute-start | bytes 1572872 | tf_op jit(solution)/shard_map/ppermute | solution.py:295
  5.5 3.8 %shard_map.59 = (f32[32,8,128]{2,1,0:T(8,128)S(1)}, bf16[1024,256]{1,0:T(8,128)(2,1)S(1)}, bf16[2048,256]{1,0:T(8,128)(2,1)S(1)}, f32[8,128]{1,0:T(8,128)S(1)}) custom-call(s32[64]{0:T(128)} %mass_hbm.1, s32[8,128]{1,0:T(8,128)} %bitcast.5, bf16[1024,256]{1,0:T(8,128)(2,1)} %docs_hbm.1, bf16[2048,256]{1,0:T(8,128)(2,1)} %cents_hbm.1), custom_call_target="tpu_custom_call" | custom-call | flops 1073741824 | bytes 1048576 | tf_op jit(solution)/shard_map/pallas_call | solution.py:296
  9.3 20.7 %all_to_all.45.parts_ref = f32[32,8,128]{2,1,0:T(8,128)S(1)} all-to-all(f32[32,8,128]{2,1,0:T(8,128)S(1)} %get-tuple-element.24), channel_id=1, replica_groups=mesh['y'=8,'zl'=2,'core'=2,'zh'=4,'x'=4] {'x','zl','zh'}, dimensions={0} | all-to-all | bytes 262144 | tf_op jit(solution)/shard_map/all_to_all | solution.py:278
  30.0 0.0 collective-permute-done.other_ref
  30.0 3.2 %shard_map.60 = (f32[16,8,128]{2,1,0:T(8,128)S(1)}, f32[1024,2048]{1,0:T(8,128)S(1)}, f32[8,128]{1,0:T(8,128)S(1)}, f32[16,128]{1,0:T(8,128)S(1)}, bf16[2048,256]{1,0:T(8,128)(2,1)S(1)}) custom-call(f32[32,8,128]{2,1,0:T(8,128)S(1)} %all_to_all.45.parts_ref, bf16[1024,256]{1,0:T(8,128)(2,1)S(1)} %get-tuple-element.25.docs_ref, ...), custom_call_target="tpu_custom_call" | custom-call | flops 1073741824 | bytes 1048576 | tf_op jit(solution)/shard_map/pallas_call | solution.py:311
  33.2 17.1 %all_to_all.46.parts_ref = f32[16,8,128]{2,1,0:T(8,128)S(1)} all-to-all(f32[16,8,128]{2,1,0:T(8,128)S(1)} %get-tuple-element.27), channel_id=1, replica_groups=mesh['y'=8,'zl'=2,'core'=2,'zh'=4,'x'=4] {'y','core'}, dimensions={0} | all-to-all | bytes 131072 | tf_op jit(solution)/shard_map/all_to_all | solution.py:278
  50.3 0.7 shard_map.61
  51.0 12.6 %all_to_all.47.parts_ref = bf16[32,24,128]{2,1,0:T(8,128)(2,1)S(1)} all-to-all(bf16[32,24,128]{2,1,0:T(8,128)(2,1)S(1)} %get-tuple-element.31), channel_id=1, replica_groups=mesh['y'=8,'zl'=2,'core'=2,'zh'=4,'x'=4] {'x','zl','zh'}, dimensions={0} | all-to-all | bytes 393216 | tf_op jit(solution)/shard_map/all_to_all | solution.py:278
  63.6 0.7 shard_map.62
  64.3 11.9 %all_to_all.48.parts_ref = bf16[16,8,128]{2,1,0:T(8,128)(2,1)S(1)} all-to-all(bf16[16,8,128]{2,1,0:T(8,128)(2,1)S(1)} %get-tuple-element.33), channel_id=1, replica_groups=mesh['y'=8,'zl'=2,'core'=2,'zh'=4,'x'=4] {'y','core'}, dimensions={0} | all-to-all | bytes 65536 | tf_op jit(solution)/shard_map/all_to_all | solution.py:278
  76.2 0.7 shard_map.63
  76.9 13.9 %all_to_all.49.parts_ref = bf16[32,16,128]{2,1,0:T(8,128)(2,1)S(1)} all-to-all(bf16[32,16,128]{2,1,0:T(8,128)(2,1)S(1)} %get-tuple-element.34), channel_id=1, replica_groups=mesh['y'=8,'zl'=2,'core'=2,'zh'=4,'x'=4] {'x','zl','zh'}, dimensions={0} | all-to-all | bytes 262144 | tf_op jit(solution)/shard_map/all_to_all | solution.py:278
  90.7 0.7 shard_map.64
  91.4 11.7 %all_to_all.50.parts_ref = bf16[16,8,128]{2,1,0:T(8,128)(2,1)S(1)} all-to-all(bf16[16,8,128]{2,1,0:T(8,128)(2,1)S(1)} %shard_map.64), channel_id=1, replica_groups=mesh['y'=8,'zl'=2,'core'=2,'zh'=4,'x'=4] {'y','core'}, dimensions={0} | all-to-all | bytes 65536 | tf_op jit(solution)/shard_map/all_to_all | solution.py:278
  103.1 0.7 shard_map.65
  103.8 12.7 %all_to_all.51.parts_ref = bf16[32,16,128]{2,1,0:T(8,128)(2,1)S(1)} all-to-all(bf16[32,16,128]{2,1,0:T(8,128)(2,1)S(1)} %get-tuple-element.37), channel_id=1, replica_groups=mesh['y'=8,'zl'=2,'core'=2,'zh'=4,'x'=4] {'x','zl','zh'}, dimensions={0} | all-to-all | bytes 262144 | tf_op jit(solution)/shard_map/all_to_all | solution.py:278
  116.5 1.4 shard_map.66
  117.9 3.7 %collective-permute-start.1 = (f32[520,256]{1,0:T(8,128)S(1)}, f32[520,256]{1,0:T(8,128)S(1)}, u32[]{:S(2)}, u32[]{:S(2)}) collective-permute-start(f32[520,256]{1,0:T(8,128)S(1)} %get-tuple-element.42), channel_id=1, source_target_pairs={{0,16},{16,0},{1,17},{17,1},{2,18},{18,2},{3,19},{19,3},{4,20},{20... | collective-permute-start | bytes 1597448 | tf_op jit(solution)/shard_map/ppermute | solution.py:352
  121.6 1.4 shard_map.67.own_ref
  123.0 0.1 collective-permute-done.1.other_ref
  123.1 0.1 shard_map.68
  123.2 15.0 %all_to_all.52.parts_ref = bf16[8,16,1152]{2,1,0:T(8,128)(2,1)S(1)} all-to-all(bf16[8,16,1152]{2,1,0:T(8,128)(2,1)S(1)} %shard_map.68), channel_id=1, replica_groups=mesh['y'=8,'zl'=2,'core'=2,'zh'=4,'x'=4] {'y'}, dimensions={0} | all-to-all | bytes 589824 | tf_op jit(solution)/shard_map/all_to_all | solution.py:278
  138.2 0.2 shard_map.69
  138.4 18.2 %all_to_all.53 = bf16[16,64,256]{2,1,0:T(8,128)(2,1)S(1)} all-to-all(bf16[16,64,256]{2,1,0:T(8,128)(2,1)S(1)} %shard_map.69), channel_id=1, replica_groups=mesh['y'=8,'zl'=2,'core'=2,'zh'=4,'x'=4] {'y','zl'}, dimensions={0} | all-to-all | bytes 1048576 | tf_op jit(solution)/shard_map/all_to_all | solution.py:278
  156.6 5.2 %collective-permute-start.2 = (bf16[1024,256]{1,0:T(8,128)(2,1)S(1)}, bf16[1024,256]{1,0:T(8,128)(2,1)S(1)}, u32[]{:S(2)}, u32[]{:S(2)}) collective-permute-start(bf16[1024,256]{1,0:T(8,128)(2,1)S(1)} %bitcast.3), channel_id=1, source_target_pairs={{0,16},{16,0},{1,17},{17,1},{2,18},{18,2},{3,19},{19,3},{4,20},{20... | collective-permute-start | bytes 1572872 | tf_op jit(solution)/shard_map/ppermute | solution.py:358
  161.8 0.8 shard_map.70
  162.6 0.7 collective-permute-done.2.x_ref
  163.3 0.8 shard_map.71
Async XLA Ops:
  0.6 29.3 %collective-permute-start = (bf16[1024,256]{1,0:T(8,128)(2,1)}, bf16[1024,256]{1,0:T(8,128)(2,1)S(1)}, u32[]{:S(2)}, u32[]{:S(2)}) collective-permute-start(bf16[1024,256]{1,0:T(8,128)(2,1)} %docs_hbm.1), channel_id=1, source_target_pairs={{0,32},{32,0},{1,33},{33,1},{2,34},{34,2},{3,35},{35,3},{4,36},{36... | collective-permute-start | bytes 1572872 | tf_op jit(solution)/shard_map/ppermute | solution.py:295
  117.9 5.2 %collective-permute-start.1 = (f32[520,256]{1,0:T(8,128)S(1)}, f32[520,256]{1,0:T(8,128)S(1)}, u32[]{:S(2)}, u32[]{:S(2)}) collective-permute-start(f32[520,256]{1,0:T(8,128)S(1)} %get-tuple-element.42), channel_id=1, source_target_pairs={{0,16},{16,0},{1,17},{17,1},{2,18},{18,2},{3,19},{19,3},{4,20},{20... | collective-permute-start | bytes 1597448 | tf_op jit(solution)/shard_map/ppermute | solution.py:352
  156.6 6.7 %collective-permute-start.2 = (bf16[1024,256]{1,0:T(8,128)(2,1)S(1)}, bf16[1024,256]{1,0:T(8,128)(2,1)S(1)}, u32[]{:S(2)}, u32[]{:S(2)}) collective-permute-start(bf16[1024,256]{1,0:T(8,128)(2,1)S(1)} %bitcast.3), channel_id=1, source_target_pairs={{0,16},{16,0},{1,17},{17,1},{2,18},{18,2},{3,19},{19,3},{4,20},{20... | collective-permute-start | bytes 1572872 | tf_op jit(solution)/shard_map/ppermute | solution.py:358

commit v11 on v10

--- a/solution.py
+++ b/solution.py
@@ -92,7 +92,7 @@
 
 
 def first_columns(
-    scale, n_x, chunk, parts_ref, docs_ref, other_ref, cents_ref,
+    scale, n_x, parts_ref, docs_ref, other_ref, cents_ref,
     out_ref, tile_ref, top_ref, f_ref, docs_all_ref, half_ref,
 ):
     zl = lax.axis_index("zl")
@@ -100,9 +100,10 @@
     groups = 2 * n_doc // LANES
     docs_all_ref[pl.ds(pl.multiple_of(zl * n_doc, n_doc), n_doc), :] = docs_ref[...]
     docs_all_ref[pl.ds(pl.multiple_of((1 - zl) * n_doc, n_doc), n_doc), :] = other_ref[...]
-    for q in range(n_cent // chunk):
-        rows = pl.ds(pl.multiple_of(q * 2 * chunk + zl * chunk, chunk), chunk)
-        half_ref[q * chunk : (q + 1) * chunk, :] = cents_ref[rows, :]
+    run = n_cent // 2
+    for q in range(2):
+        rows = pl.ds(pl.multiple_of(q * n_cent + zl * run, run), run)
+        half_ref[q * run : (q + 1) * run, :] = cents_ref[rows, :]
     by_zl = parts_ref[...].reshape(n_x, 2, parts_ref.shape[0] // (2 * n_x), 8, LANES)
     for z in range(2):
         parts = by_zl[:, z].reshape(parts_ref.shape[0] // 2, 8, LANES)
@@ -309,7 +310,7 @@
     parts = exchange(parts, ROWS)
     chunk = n_cent // col_peers
     parts, tile, top, f, docs_all = call(
-        functools.partial(first_columns, scale, n_x, chunk),
+        functools.partial(first_columns, scale, n_x),
         (
             shape((col_peers, cent_rows, LANES), F32),
             tile_shape,
@@ -354,7 +355,7 @@
     sums = call(final_join, shape((n_y, 16, 2 * LANES * (chunk // 16) + LANES), BF16), 2)(for_own, from_other)
     sums = exchange(sums, "y")
     new = call(divide, shape((n_y * n_zl, chunk, 256), BF16), 1, scratch=[pltpu.VMEM((LANES, LANES), F32)])(sums)
-    own = exchange(new, ("y", "zl")).reshape(n_y * n_zl * chunk, 256)
+    own = exchange(new, ("zl", "y")).reshape(n_y * n_zl * chunk, 256)
     other = lax.ppermute(own, "core", swap)
     placed = shape((cents.shape[0], 256), BF16)
     new, pot = call(

time: 165 us -> 163 us (0.988)
  blocking collectives: 134 us -> 132 us
    all_to_all x9, blocking collectives: 134 us -> 132 us  [exchange(): return lax.all_to_all(x, axes, 0, 0)]
where the time goes in v11:
time: 163 us; the launch traced here: 162 us
  blocking collectives  132 us (81%)
  Pallas kernels  15.1 us (9%)
  starting transfers between devices  13.3 us (8%)
    all_to_all x9, blocking collectives, exchange(): return lax.all_to_all(x, axes, 0, 0)  132 us
    ppermute x1, starting transfers between devices, per_device(): other_docs = lax.ppermute(docs, 'zl', swap)  4.83 us
    ppermute x1, starting transfers between devices, per_device(): other = lax.ppermute(own, 'core', swap)  4.73 us
    pallas_call x1, Pallas kernels, per_device(): call(functools.partial(first_rows, scale), (shape((row_peers, doc_rows //...  3.83 us
    ppermute x1, starting transfers between devices, per_device(): from_other = lax.ppermute(for_other, 'core', swap)  3.69 us
  transfers between devices with their start and end apart: 3, of which 2 were waited for; matrix products, arithmetic and copies ran while one was open for 0% of the time, Pallas kernels for 4%

profile of v11, /device:TPU:1, one launch (start us, length us, event | category | flops | bytes accessed | tf_op | source)
XLA Modules:
  0.0 162.1 jit_solution(3016665036635110421)
XLA Ops:
  0.6 4.8 %collective-permute-start = (bf16[1024,256]{1,0:T(8,128)(2,1)}, bf16[1024,256]{1,0:T(8,128)(2,1)S(1)}, u32[]{:S(2)}, u32[]{:S(2)}) collective-permute-start(bf16[1024,256]{1,0:T(8,128)(2,1)} %docs_hbm.1), channel_id=1, source_target_pairs={{0,32},{32,0},{1,33},{33,1},{2,34},{34,2},{3,35},{35,3},{4,36},{36... | collective-permute-start | bytes 1572872 | tf_op jit(solution)/shard_map/ppermute | solution.py:296
  5.5 3.8 %shard_map.59 = (f32[32,8,128]{2,1,0:T(8,128)S(1)}, bf16[1024,256]{1,0:T(8,128)(2,1)S(1)}, bf16[2048,256]{1,0:T(8,128)(2,1)S(1)}, f32[8,128]{1,0:T(8,128)S(1)}) custom-call(s32[64]{0:T(128)} %mass_hbm.1, s32[8,128]{1,0:T(8,128)} %bitcast.5, bf16[1024,256]{1,0:T(8,128)(2,1)} %docs_hbm.1, bf16[2048,256]{1,0:T(8,128)(2,1)} %cents_hbm.1), custom_call_target="tpu_custom_call" | custom-call | flops 1073741824 | bytes 1048576 | tf_op jit(solution)/shard_map/pallas_call | solution.py:297
  9.3 20.7 %all_to_all.45.parts_ref = f32[32,8,128]{2,1,0:T(8,128)S(1)} all-to-all(f32[32,8,128]{2,1,0:T(8,128)S(1)} %get-tuple-element.24), channel_id=1, replica_groups=mesh['y'=8,'zl'=2,'core'=2,'zh'=4,'x'=4] {'x','zl','zh'}, dimensions={0} | all-to-all | bytes 262144 | tf_op jit(solution)/shard_map/all_to_all | solution.py:279
  30.0 0.0 collective-permute-done.other_ref
  30.0 3.2 %shard_map.60 = (f32[16,8,128]{2,1,0:T(8,128)S(1)}, f32[1024,2048]{1,0:T(8,128)S(1)}, f32[8,128]{1,0:T(8,128)S(1)}, f32[16,128]{1,0:T(8,128)S(1)}, bf16[2048,256]{1,0:T(8,128)(2,1)S(1)}) custom-call(f32[32,8,128]{2,1,0:T(8,128)S(1)} %all_to_all.45.parts_ref, bf16[1024,256]{1,0:T(8,128)(2,1)S(1)} %get-tuple-element.25.docs_ref, ...), custom_call_target="tpu_custom_call" | custom-call | flops 1073741824 | bytes 1048576 | tf_op jit(solution)/shard_map/pallas_call | solution.py:312
  33.2 17.1 %all_to_all.46.parts_ref = f32[16,8,128]{2,1,0:T(8,128)S(1)} all-to-all(f32[16,8,128]{2,1,0:T(8,128)S(1)} %get-tuple-element.27), channel_id=1, replica_groups=mesh['y'=8,'zl'=2,'core'=2,'zh'=4,'x'=4] {'y','core'}, dimensions={0} | all-to-all | bytes 131072 | tf_op jit(solution)/shard_map/all_to_all | solution.py:279
  50.3 0.7 shard_map.61
  51.0 12.6 %all_to_all.47.parts_ref = bf16[32,24,128]{2,1,0:T(8,128)(2,1)S(1)} all-to-all(bf16[32,24,128]{2,1,0:T(8,128)(2,1)S(1)} %get-tuple-element.31), channel_id=1, replica_groups=mesh['y'=8,'zl'=2,'core'=2,'zh'=4,'x'=4] {'x','zl','zh'}, dimensions={0} | all-to-all | bytes 393216 | tf_op jit(solution)/shard_map/all_to_all | solution.py:279
  63.6 0.7 shard_map.62
  64.3 11.9 %all_to_all.48.parts_ref = bf16[16,8,128]{2,1,0:T(8,128)(2,1)S(1)} all-to-all(bf16[16,8,128]{2,1,0:T(8,128)(2,1)S(1)} %get-tuple-element.33), channel_id=1, replica_groups=mesh['y'=8,'zl'=2,'core'=2,'zh'=4,'x'=4] {'y','core'}, dimensions={0} | all-to-all | bytes 65536 | tf_op jit(solution)/shard_map/all_to_all | solution.py:279
  76.2 0.7 shard_map.63
  76.9 13.9 %all_to_all.49.parts_ref = bf16[32,16,128]{2,1,0:T(8,128)(2,1)S(1)} all-to-all(bf16[32,16,128]{2,1,0:T(8,128)(2,1)S(1)} %get-tuple-element.34), channel_id=1, replica_groups=mesh['y'=8,'zl'=2,'core'=2,'zh'=4,'x'=4] {'x','zl','zh'}, dimensions={0} | all-to-all | bytes 262144 | tf_op jit(solution)/shard_map/all_to_all | solution.py:279
  90.7 0.7 shard_map.64
  91.4 11.7 %all_to_all.50.parts_ref = bf16[16,8,128]{2,1,0:T(8,128)(2,1)S(1)} all-to-all(bf16[16,8,128]{2,1,0:T(8,128)(2,1)S(1)} %shard_map.64), channel_id=1, replica_groups=mesh['y'=8,'zl'=2,'core'=2,'zh'=4,'x'=4] {'y','core'}, dimensions={0} | all-to-all | bytes 65536 | tf_op jit(solution)/shard_map/all_to_all | solution.py:279
  103.1 0.7 shard_map.65
  103.8 12.7 %all_to_all.51.parts_ref = bf16[32,16,128]{2,1,0:T(8,128)(2,1)S(1)} all-to-all(bf16[32,16,128]{2,1,0:T(8,128)(2,1)S(1)} %get-tuple-element.37), channel_id=1, replica_groups=mesh['y'=8,'zl'=2,'core'=2,'zh'=4,'x'=4] {'x','zl','zh'}, dimensions={0} | all-to-all | bytes 262144 | tf_op jit(solution)/shard_map/all_to_all | solution.py:279
  116.5 1.4 shard_map.66
  117.9 3.7 %collective-permute-start.1 = (f32[520,256]{1,0:T(8,128)S(1)}, f32[520,256]{1,0:T(8,128)S(1)}, u32[]{:S(2)}, u32[]{:S(2)}) collective-permute-start(f32[520,256]{1,0:T(8,128)S(1)} %get-tuple-element.42), channel_id=1, source_target_pairs={{0,16},{16,0},{1,17},{17,1},{2,18},{18,2},{3,19},{19,3},{4,20},{20... | collective-permute-start | bytes 1597448 | tf_op jit(solution)/shard_map/ppermute | solution.py:353
  121.6 1.4 shard_map.67.own_ref
  123.0 0.1 collective-permute-done.1.other_ref
  123.1 0.1 shard_map.68
  123.2 15.0 %all_to_all.52.parts_ref = bf16[8,16,1152]{2,1,0:T(8,128)(2,1)S(1)} all-to-all(bf16[8,16,1152]{2,1,0:T(8,128)(2,1)S(1)} %shard_map.68), channel_id=1, replica_groups=mesh['y'=8,'zl'=2,'core'=2,'zh'=4,'x'=4] {'y'}, dimensions={0} | all-to-all | bytes 589824 | tf_op jit(solution)/shard_map/all_to_all | solution.py:279
  138.2 0.2 shard_map.69
  138.4 16.5 %all_to_all.53 = bf16[16,64,256]{2,1,0:T(8,128)(2,1)S(1)} all-to-all(bf16[16,64,256]{2,1,0:T(8,128)(2,1)S(1)} %shard_map.69), channel_id=1, replica_groups=mesh['y'=8,'zl'=2,'core'=2,'zh'=4,'x'=4] {'zl','y'}, dimensions={0} | all-to-all | bytes 1048576 | tf_op jit(solution)/shard_map/all_to_all | solution.py:279
  154.9 4.7 %collective-permute-start.2 = (bf16[1024,256]{1,0:T(8,128)(2,1)S(1)}, bf16[1024,256]{1,0:T(8,128)(2,1)S(1)}, u32[]{:S(2)}, u32[]{:S(2)}) collective-permute-start(bf16[1024,256]{1,0:T(8,128)(2,1)S(1)} %bitcast.3), channel_id=1, source_target_pairs={{0,16},{16,0},{1,17},{17,1},{2,18},{18,2},{3,19},{19,3},{4,20},{20... | collective-permute-start | bytes 1572872 | tf_op jit(solution)/shard_map/ppermute | solution.py:359
  159.7 0.8 shard_map.70
  160.5 0.7 collective-permute-done.2.x_ref
  161.2 0.8 shard_map.71
Async XLA Ops:
  0.6 29.3 %collective-permute-start = (bf16[1024,256]{1,0:T(8,128)(2,1)}, bf16[1024,256]{1,0:T(8,128)(2,1)S(1)}, u32[]{:S(2)}, u32[]{:S(2)}) collective-permute-start(bf16[1024,256]{1,0:T(8,128)(2,1)} %docs_hbm.1), channel_id=1, source_target_pairs={{0,32},{32,0},{1,33},{33,1},{2,34},{34,2},{3,35},{35,3},{4,36},{36... | collective-permute-start | bytes 1572872 | tf_op jit(solution)/shard_map/ppermute | solution.py:296
  117.9 5.2 %collective-permute-start.1 = (f32[520,256]{1,0:T(8,128)S(1)}, f32[520,256]{1,0:T(8,128)S(1)}, u32[]{:S(2)}, u32[]{:S(2)}) collective-permute-start(f32[520,256]{1,0:T(8,128)S(1)} %get-tuple-element.42), channel_id=1, source_target_pairs={{0,16},{16,0},{1,17},{17,1},{2,18},{18,2},{3,19},{19,3},{4,20},{20... | collective-permute-start | bytes 1597448 | tf_op jit(solution)/shard_map/ppermute | solution.py:353
  154.9 6.3 %collective-permute-start.2 = (bf16[1024,256]{1,0:T(8,128)(2,1)S(1)}, bf16[1024,256]{1,0:T(8,128)(2,1)S(1)}, u32[]{:S(2)}, u32[]{:S(2)}) collective-permute-start(bf16[1024,256]{1,0:T(8,128)(2,1)S(1)} %bitcast.3), channel_id=1, source_target_pairs={{0,16},{16,0},{1,17},{17,1},{2,18},{18,2},{3,19},{19,3},{4,20},{20... | collective-permute-start | bytes 1572872 | tf_op jit(solution)/shard_map/ppermute | solution.py:359

commit v12 on v11

--- a/solution.py
+++ b/solution.py
@@ -14,7 +14,8 @@
 LANES = 128
 VMEM_LIMIT = 32 * 1024 * 1024
 ROWS = ("x", "zl", "zh")
-COLS = ("y", "core")
+COLS = ("yc", "yb", "ya", "core")
+SUMS = ("yb", "ya", "yc")
 F32 = jnp.float32
 BF16 = jnp.bfloat16
 
@@ -251,7 +252,7 @@
     chunk = tiles * 8
     mass = total[0:8, tiles * LANES :] + total[8:16, tiles * LANES :]
     mass_ref[...] = to_columns(mass)
-    col = mass_ref[pl.ds(pl.multiple_of((lax.axis_index("y") & 1) * chunk, chunk), chunk), :]
+    col = mass_ref[pl.ds(pl.multiple_of((lax.axis_index("yc")) * chunk, chunk), chunk), :]
     for i in range(chunk // 16):
         pair = [total[:, (i * 2 + h) * LANES : (i * 2 + h + 1) * LANES] / col[i * 16 : (i + 1) * 16, :] for h in range(2)]
         new = jnp.concatenate(pair, axis=1).astype(BF16)
@@ -280,7 +281,8 @@
 
 
 def per_device(sizes, docs, cents, shard_ids, shard_mass):
-    n_y, n_zl, n_core, n_zh, n_x = sizes
+    *y_bits, n_zl, n_core, n_zh, n_x = sizes
+    n_y = math.prod(y_bits)
     row_peers, col_peers = n_zl * n_zh * n_x, n_y * n_core
     n_doc, n_cent = docs.shape[0] * 2, cents.shape[0] // 2
     doc_rows, cent_rows = n_doc // LANES, n_cent // LANES
@@ -353,9 +355,9 @@
     from_other = lax.ppermute(for_other, "core", swap)
     for_own = call(final_own, part_shape, 4, scratch=p_scratch, flops=half_flops)(u, c, tile, docs_all)
     sums = call(final_join, shape((n_y, 16, 2 * LANES * (chunk // 16) + LANES), BF16), 2)(for_own, from_other)
-    sums = exchange(sums, "y")
+    sums = exchange(sums, SUMS)
     new = call(divide, shape((n_y * n_zl, chunk, 256), BF16), 1, scratch=[pltpu.VMEM((LANES, LANES), F32)])(sums)
-    own = exchange(new, ("zl", "y")).reshape(n_y * n_zl * chunk, 256)
+    own = exchange(new, ("zl", *SUMS)).reshape(n_y * n_zl * chunk, 256)
     other = lax.ppermute(own, "core", swap)
     placed = shape((cents.shape[0], 256), BF16)
     new, pot = call(
@@ -372,12 +374,12 @@
     return new, pot.reshape(-1)
 
 
-SIZES = (8, 2, 2, 4, 4)
+SIZES = (2, 2, 2, 2, 2, 4, 4)
 
 
 def solution(mesh, sizes=SIZES):
-    fine = Mesh(mesh.devices.reshape(sizes), ("y", "zl", "core", "zh", "x"))
-    docs, cents = ("y", "zl", "core"), ("zh", "x")
+    fine = Mesh(mesh.devices.reshape(sizes), ("ya", "yb", "yc", "zl", "core", "zh", "x"))
+    docs, cents = ("ya", "yb", "yc", "zl", "core"), ("zh", "x")
     return jax.shard_map(
         functools.partial(per_device, sizes),
         mesh=fine,

time: 163 us -> 162 us (level)
  no operation moved by 1% of the time
where the time goes in v12:
time: 162 us; the launch traced here: 161 us
  blocking collectives  131 us (81%)
  Pallas kernels  15.1 us (9%)
  starting transfers between devices  13.2 us (8%)
    all_to_all x9, blocking collectives, exchange(): return lax.all_to_all(x, axes, 0, 0)  131 us
    ppermute x1, starting transfers between devices, per_device(): other_docs = lax.ppermute(docs, 'zl', swap)  4.83 us
    ppermute x1, starting transfers between devices, per_device(): other = lax.ppermute(own, 'core', swap)  4.65 us
    pallas_call x1, Pallas kernels, per_device(): call(functools.partial(first_rows, scale), (shape((row_peers, doc_rows //...  3.83 us
    ppermute x1, starting transfers between devices, per_device(): from_other = lax.ppermute(for_other, 'core', swap)  3.69 us
    pallas_call x1, Pallas kernels, per_device(): call(functools.partial(first_columns, scale, n_x), (shape((col_peers, cen...  3.24 us
  transfers between devices with their start and end apart: 3, of which 2 were waited for; matrix products, arithmetic and copies ran while one was open for 0% of the time, Pallas kernels for 4%

profile of v12, /device:TPU:1, one launch (start us, length us, event | category | flops | bytes accessed | tf_op | source)
XLA Modules:
  0.0 161.5 jit_solution(13705034006616615717)
XLA Ops:
  0.6 4.8 %collective-permute-start = (bf16[1024,256]{1,0:T(8,128)(2,1)}, bf16[1024,256]{1,0:T(8,128)(2,1)S(1)}, u32[]{:S(2)}, u32[]{:S(2)}) collective-permute-start(bf16[1024,256]{1,0:T(8,128)(2,1)} %docs_hbm.1), channel_id=1, source_target_pairs={{0,32},{32,0},{1,33},{33,1},{2,34},{34,2},{3,35},{35,3},{4,36},{36... | collective-permute-start | bytes 1572872 | tf_op jit(solution)/shard_map/ppermute | solution.py:298
  5.5 3.8 %shard_map.59 = (f32[32,8,128]{2,1,0:T(8,128)S(1)}, bf16[1024,256]{1,0:T(8,128)(2,1)S(1)}, bf16[2048,256]{1,0:T(8,128)(2,1)S(1)}, f32[8,128]{1,0:T(8,128)S(1)}) custom-call(s32[64]{0:T(128)} %mass_hbm.1, s32[8,128]{1,0:T(8,128)} %bitcast.5, bf16[1024,256]{1,0:T(8,128)(2,1)} %docs_hbm.1, bf16[2048,256]{1,0:T(8,128)(2,1)} %cents_hbm.1), custom_call_target="tpu_custom_call" | custom-call | flops 1073741824 | bytes 1048576 | tf_op jit(solution)/shard_map/pallas_call | solution.py:299
  9.3 20.7 %all_to_all.45.parts_ref = f32[32,8,128]{2,1,0:T(8,128)S(1)} all-to-all(f32[32,8,128]{2,1,0:T(8,128)S(1)} %get-tuple-element.24), channel_id=1, replica_groups=mesh['ya'=2,'yb'=2,'yc'=2,'zl'=2,'core'=2,'zh'=4,'x'=4] {'x','zl','zh'}, dimensions={0} | all-to-all | bytes 262144 | tf_op jit(solution)/shard_map/all_to_all | solution.py:280
  30.0 0.0 collective-permute-done.other_ref
  30.0 3.2 %shard_map.60 = (f32[16,8,128]{2,1,0:T(8,128)S(1)}, f32[1024,2048]{1,0:T(8,128)S(1)}, f32[8,128]{1,0:T(8,128)S(1)}, f32[16,128]{1,0:T(8,128)S(1)}, bf16[2048,256]{1,0:T(8,128)(2,1)S(1)}) custom-call(f32[32,8,128]{2,1,0:T(8,128)S(1)} %all_to_all.45.parts_ref, bf16[1024,256]{1,0:T(8,128)(2,1)S(1)} %get-tuple-element.25.docs_ref, ...), custom_call_target="tpu_custom_call" | custom-call | flops 1073741824 | bytes 1048576 | tf_op jit(solution)/shard_map/pallas_call | solution.py:314
  33.2 17.1 %all_to_all.46.parts_ref = f32[16,8,128]{2,1,0:T(8,128)S(1)} all-to-all(f32[16,8,128]{2,1,0:T(8,128)S(1)} %get-tuple-element.27), channel_id=1, replica_groups=mesh['ya'=2,'yb'=2,'yc'=2,'zl'=2,'core'=2,'zh'=4,'x'=4] {'yc','yb','ya',..., dimensions={0} | all-to-all | bytes 131072 | tf_op jit(solution)/shard_map/all_to_all | solution.py:280
  50.3 0.7 shard_map.61
  51.0 12.6 %all_to_all.47.parts_ref = bf16[32,24,128]{2,1,0:T(8,128)(2,1)S(1)} all-to-all(bf16[32,24,128]{2,1,0:T(8,128)(2,1)S(1)} %get-tuple-element.31), channel_id=1, replica_groups=mesh['ya'=2,'yb'=2,'yc'=2,'zl'=2,'core'=2,'zh'=4,'x'=4] {'x','zl','zh'}, dimensions={0} | all-to-all | bytes 393216 | tf_op jit(solution)/shard_map/all_to_all | solution.py:280
  63.6 0.7 shard_map.62
  64.3 11.9 %all_to_all.48.parts_ref = bf16[16,8,128]{2,1,0:T(8,128)(2,1)S(1)} all-to-all(bf16[16,8,128]{2,1,0:T(8,128)(2,1)S(1)} %get-tuple-element.33), channel_id=1, replica_groups=mesh['ya'=2,'yb'=2,'yc'=2,'zl'=2,'core'=2,'zh'=4,'x'=4] {'yc','yb','ya',..., dimensions={0} | all-to-all | bytes 65536 | tf_op jit(solution)/shard_map/all_to_all | solution.py:280
  76.2 0.7 shard_map.63
  76.9 13.8 %all_to_all.49.parts_ref = bf16[32,16,128]{2,1,0:T(8,128)(2,1)S(1)} all-to-all(bf16[32,16,128]{2,1,0:T(8,128)(2,1)S(1)} %get-tuple-element.34), channel_id=1, replica_groups=mesh['ya'=2,'yb'=2,'yc'=2,'zl'=2,'core'=2,'zh'=4,'x'=4] {'x','zl','zh'}, dimensions={0} | all-to-all | bytes 262144 | tf_op jit(solution)/shard_map/all_to_all | solution.py:280
  90.7 0.7 shard_map.64
  91.4 11.6 %all_to_all.50.parts_ref = bf16[16,8,128]{2,1,0:T(8,128)(2,1)S(1)} all-to-all(bf16[16,8,128]{2,1,0:T(8,128)(2,1)S(1)} %shard_map.64), channel_id=1, replica_groups=mesh['ya'=2,'yb'=2,'yc'=2,'zl'=2,'core'=2,'zh'=4,'x'=4] {'yc','yb','ya',..., dimensions={0} | all-to-all | bytes 65536 | tf_op jit(solution)/shard_map/all_to_all | solution.py:280
  102.9 0.7 shard_map.65
  103.6 12.7 %all_to_all.51.parts_ref = bf16[32,16,128]{2,1,0:T(8,128)(2,1)S(1)} all-to-all(bf16[32,16,128]{2,1,0:T(8,128)(2,1)S(1)} %get-tuple-element.37), channel_id=1, replica_groups=mesh['ya'=2,'yb'=2,'yc'=2,'zl'=2,'core'=2,'zh'=4,'x'=4] {'x','zl','zh'}, dimensions={0} | all-to-all | bytes 262144 | tf_op jit(solution)/shard_map/all_to_all | solution.py:280
  116.4 1.4 shard_map.66
  117.8 3.7 %collective-permute-start.1 = (f32[520,256]{1,0:T(8,128)S(1)}, f32[520,256]{1,0:T(8,128)S(1)}, u32[]{:S(2)}, u32[]{:S(2)}) collective-permute-start(f32[520,256]{1,0:T(8,128)S(1)} %get-tuple-element.42), channel_id=1, source_target_pairs={{0,16},{16,0},{1,17},{17,1},{2,18},{18,2},{3,19},{19,3},{4,20},{20... | collective-permute-start | bytes 1597448 | tf_op jit(solution)/shard_map/ppermute | solution.py:355
  121.5 1.4 shard_map.67.own_ref
  122.9 0.1 collective-permute-done.1.other_ref
  123.0 0.1 shard_map.68
  123.0 13.7 %all_to_all.52.parts_ref = bf16[8,16,1152]{2,1,0:T(8,128)(2,1)S(1)} all-to-all(bf16[8,16,1152]{2,1,0:T(8,128)(2,1)S(1)} %shard_map.68), channel_id=1, replica_groups=mesh['ya'=2,'yb'=2,'yc'=2,'zl'=2,'core'=2,'zh'=4,'x'=4] {'yb','ya','yc'}, dimensions={0} | all-to-all | bytes 589824 | tf_op jit(solution)/shard_map/all_to_all | solution.py:280
  136.7 0.2 shard_map.69
  136.9 17.4 %all_to_all.53 = bf16[16,64,256]{2,1,0:T(8,128)(2,1)S(1)} all-to-all(bf16[16,64,256]{2,1,0:T(8,128)(2,1)S(1)} %shard_map.69), channel_id=1, replica_groups=mesh['ya'=2,'yb'=2,'yc'=2,'zl'=2,'core'=2,'zh'=4,'x'=4] {'zl','yb','ya',..., dimensions={0} | all-to-all | bytes 1048576 | tf_op jit(solution)/shard_map/all_to_all | solution.py:280
  154.3 4.6 %collective-permute-start.2 = (bf16[1024,256]{1,0:T(8,128)(2,1)S(1)}, bf16[1024,256]{1,0:T(8,128)(2,1)S(1)}, u32[]{:S(2)}, u32[]{:S(2)}) collective-permute-start(bf16[1024,256]{1,0:T(8,128)(2,1)S(1)} %bitcast.3), channel_id=1, source_target_pairs={{0,16},{16,0},{1,17},{17,1},{2,18},{18,2},{3,19},{19,3},{4,20},{20... | collective-permute-start | bytes 1572872 | tf_op jit(solution)/shard_map/ppermute | solution.py:361
  159.0 0.8 shard_map.70
  159.8 0.7 collective-permute-done.2.x_ref
  160.5 0.8 shard_map.71
Async XLA Ops:
  0.6 29.3 %collective-permute-start = (bf16[1024,256]{1,0:T(8,128)(2,1)}, bf16[1024,256]{1,0:T(8,128)(2,1)S(1)}, u32[]{:S(2)}, u32[]{:S(2)}) collective-permute-start(bf16[1024,256]{1,0:T(8,128)(2,1)} %docs_hbm.1), channel_id=1, source_target_pairs={{0,32},{32,0},{1,33},{33,1},{2,34},{34,2},{3,35},{35,3},{4,36},{36... | collective-permute-start | bytes 1572872 | tf_op jit(solution)/shard_map/ppermute | solution.py:298
  117.8 5.2 %collective-permute-start.1 = (f32[520,256]{1,0:T(8,128)S(1)}, f32[520,256]{1,0:T(8,128)S(1)}, u32[]{:S(2)}, u32[]{:S(2)}) collective-permute-start(f32[520,256]{1,0:T(8,128)S(1)} %get-tuple-element.42), channel_id=1, source_target_pairs={{0,16},{16,0},{1,17},{17,1},{2,18},{18,2},{3,19},{19,3},{4,20},{20... | collective-permute-start | bytes 1597448 | tf_op jit(solution)/shard_map/ppermute | solution.py:355
  154.3 6.2 %collective-permute-start.2 = (bf16[1024,256]{1,0:T(8,128)(2,1)S(1)}, bf16[1024,256]{1,0:T(8,128)(2,1)S(1)}, u32[]{:S(2)}, u32[]{:S(2)}) collective-permute-start(bf16[1024,256]{1,0:T(8,128)(2,1)S(1)} %bitcast.3), channel_id=1, source_target_pairs={{0,16},{16,0},{1,17},{17,1},{2,18},{18,2},{3,19},{19,3},{4,20},{20... | collective-permute-start | bytes 1572872 | tf_op jit(solution)/shard_map/ppermute | solution.py:361

commit v13 on v12

--- a/solution.py
+++ b/solution.py
@@ -13,7 +13,7 @@
 LN2 = 0.6931471805599453
 LANES = 128
 VMEM_LIMIT = 32 * 1024 * 1024
-ROWS = ("x", "zl", "zh")
+ROWS = ("zb", "za", "zl", "xb", "xa")
 COLS = ("yc", "yb", "ya", "core")
 SUMS = ("yb", "ya", "yc")
 F32 = jnp.float32
@@ -93,7 +93,7 @@
 
 
 def first_columns(
-    scale, n_x, parts_ref, docs_ref, other_ref, cents_ref,
+    scale, n_zh, parts_ref, docs_ref, other_ref, cents_ref,
     out_ref, tile_ref, top_ref, f_ref, docs_all_ref, half_ref,
 ):
     zl = lax.axis_index("zl")
@@ -105,7 +105,7 @@
     for q in range(2):
         rows = pl.ds(pl.multiple_of(q * n_cent + zl * run, run), run)
         half_ref[q * run : (q + 1) * run, :] = cents_ref[rows, :]
-    by_zl = parts_ref[...].reshape(n_x, 2, parts_ref.shape[0] // (2 * n_x), 8, LANES)
+    by_zl = parts_ref[...].reshape(n_zh, 2, parts_ref.shape[0] // (2 * n_zh), 8, LANES)
     for z in range(2):
         parts = by_zl[:, z].reshape(parts_ref.shape[0] // 2, 8, LANES)
         top = jnp.max(parts, axis=0)
@@ -167,9 +167,9 @@
     weigh_columns(c, tile_ref, out_ref)
 
 
-def columns_after_first(n_zh, parts_ref, c_ref, tile_ref, out_ref, w_ref):
+def columns_after_first(n_x, parts_ref, c_ref, tile_ref, out_ref, w_ref):
     groups = w_ref.shape[0]
-    w = jnp.concatenate([parts_ref[z * n_zh, groups:, :].astype(F32) for z in range(2)], axis=0)
+    w = jnp.concatenate([parts_ref[z * n_x, groups:, :].astype(F32) for z in range(2)], axis=0)
     w_ref[...] = w
     weigh_rows(w / jnp.sum(parts_ref[:, 0:groups, :].astype(F32), axis=0), c_ref, tile_ref, out_ref)
 
@@ -281,8 +281,8 @@
 
 
 def per_device(sizes, docs, cents, shard_ids, shard_mass):
-    *y_bits, n_zl, n_core, n_zh, n_x = sizes
-    n_y = math.prod(y_bits)
+    n_y, n_zl, n_core = math.prod(sizes[0:3]), sizes[3], sizes[4]
+    n_zh, n_x = math.prod(sizes[5:7]), math.prod(sizes[7:9])
     row_peers, col_peers = n_zl * n_zh * n_x, n_y * n_core
     n_doc, n_cent = docs.shape[0] * 2, cents.shape[0] // 2
     doc_rows, cent_rows = n_doc // LANES, n_cent // LANES
@@ -312,7 +312,7 @@
     parts = exchange(parts, ROWS)
     chunk = n_cent // col_peers
     parts, tile, top, f, docs_all = call(
-        functools.partial(first_columns, scale, n_x),
+        functools.partial(first_columns, scale, n_zh),
         (
             shape((col_peers, cent_rows, LANES), F32),
             tile_shape,
@@ -335,7 +335,7 @@
         parts = exchange(parts, ROWS)
         if turn == 0:
             out = (col_out, shape((doc_rows, LANES), F32))
-            parts, w = call(functools.partial(columns_after_first, n_zh), out, 3, flops=2 * n_doc * n_cent)(parts, c, tile)
+            parts, w = call(functools.partial(columns_after_first, n_x), out, 3, flops=2 * n_doc * n_cent)(parts, c, tile)
         else:
             parts = call(columns_after, col_out, 4, flops=2 * n_doc * n_cent)(parts, w, c, tile)
         parts = exchange(parts, COLS)
@@ -374,12 +374,12 @@
     return new, pot.reshape(-1)
 
 
-SIZES = (2, 2, 2, 2, 2, 4, 4)
+SIZES = (2, 2, 2, 2, 2, 2, 2, 2, 2)
 
 
 def solution(mesh, sizes=SIZES):
-    fine = Mesh(mesh.devices.reshape(sizes), ("ya", "yb", "yc", "zl", "core", "zh", "x"))
-    docs, cents = ("ya", "yb", "yc", "zl", "core"), ("zh", "x")
+    fine = Mesh(mesh.devices.reshape(sizes), ("ya", "yb", "yc", "zl", "core", "za", "zb", "xa", "xb"))
+    docs, cents = ("ya", "yb", "yc", "zl", "core"), ("za", "zb", "xa", "xb")
     return jax.shard_map(
         functools.partial(per_device, sizes),
         mesh=fine,

time: 162 us -> 162 us (level)
  no operation moved by 1% of the time
where the time goes in v13:
time: 162 us; the launch traced here: 161 us
  blocking collectives  131 us (81%)
  Pallas kernels  15.1 us (9%)
  starting transfers between devices  13.4 us (8%)
    all_to_all x9, blocking collectives, exchange(): return lax.all_to_all(x, axes, 0, 0)  131 us
    ppermute x1, starting transfers between devices, per_device(): other_docs = lax.ppermute(docs, 'zl', swap)  4.83 us
    ppermute x1, starting transfers between devices, per_device(): other = lax.ppermute(own, 'core', swap)  4.79 us
    pallas_call x1, Pallas kernels, per_device(): call(functools.partial(first_rows, scale), (shape((row_peers, doc_rows //...  3.83 us
    ppermute x1, starting transfers between devices, per_device(): from_other = lax.ppermute(for_other, 'core', swap)  3.83 us
    pallas_call x1, Pallas kernels, per_device(): call(functools.partial(first_columns, scale, n_zh), (shape((col_peers, ce...  3.25 us
  transfers between devices with their start and end apart: 3, of which 2 were waited for; matrix products, arithmetic and copies ran while one was open for 0% of the time, Pallas kernels for 4%

profile of v13, /device:TPU:1, one launch (start us, length us, event | category | flops | bytes accessed | tf_op | source)
XLA Modules:
  0.0 161.4 jit_solution(962518790612264780)
XLA Ops:
  0.6 4.8 %collective-permute-start = (bf16[1024,256]{1,0:T(8,128)(2,1)}, bf16[1024,256]{1,0:T(8,128)(2,1)S(1)}, u32[]{:S(2)}, u32[]{:S(2)}) collective-permute-start(bf16[1024,256]{1,0:T(8,128)(2,1)} %docs_hbm.1), channel_id=1, source_target_pairs={{0,32},{32,0},{1,33},{33,1},{2,34},{34,2},{3,35},{35,3},{4,36},{36... | collective-permute-start | bytes 1572872 | tf_op jit(solution)/shard_map/ppermute | solution.py:298
  5.5 3.8 %shard_map.59 = (f32[32,8,128]{2,1,0:T(8,128)S(1)}, bf16[1024,256]{1,0:T(8,128)(2,1)S(1)}, bf16[2048,256]{1,0:T(8,128)(2,1)S(1)}, f32[8,128]{1,0:T(8,128)S(1)}) custom-call(s32[64]{0:T(128)} %mass_hbm.1, s32[8,128]{1,0:T(8,128)} %bitcast.5, bf16[1024,256]{1,0:T(8,128)(2,1)} %docs_hbm.1, bf16[2048,256]{1,0:T(8,128)(2,1)} %cents_hbm.1), custom_call_target="tpu_custom_call" | custom-call | flops 1073741824 | bytes 1048576 | tf_op jit(solution)/shard_map/pallas_call | solution.py:299
  9.3 21.1 %all_to_all.45.parts_ref = f32[32,8,128]{2,1,0:T(8,128)S(1)} all-to-all(f32[32,8,128]{2,1,0:T(8,128)S(1)} %get-tuple-element.24), channel_id=1, replica_groups=mesh['ya'=2,'yb'=2,'yc'=2,'zl'=2,'core'=2,'za'=2,'zb'=2,'xa'=2,'xb'=2] {..., dimensions={0} | all-to-all | bytes 262144 | tf_op jit(solution)/shard_map/all_to_all | solution.py:280
  30.5 0.0 collective-permute-done.other_ref
  30.5 3.2 %shard_map.60 = (f32[16,8,128]{2,1,0:T(8,128)S(1)}, f32[1024,2048]{1,0:T(8,128)S(1)}, f32[8,128]{1,0:T(8,128)S(1)}, f32[16,128]{1,0:T(8,128)S(1)}, bf16[2048,256]{1,0:T(8,128)(2,1)S(1)}) custom-call(f32[32,8,128]{2,1,0:T(8,128)S(1)} %all_to_all.45.parts_ref, bf16[1024,256]{1,0:T(8,128)(2,1)S(1)} %get-tuple-element.25.docs_ref, ...), custom_call_target="tpu_custom_call" | custom-call | flops 1073741824 | bytes 1048576 | tf_op jit(solution)/shard_map/pallas_call | solution.py:314
  33.7 17.2 %all_to_all.46.parts_ref = f32[16,8,128]{2,1,0:T(8,128)S(1)} all-to-all(f32[16,8,128]{2,1,0:T(8,128)S(1)} %get-tuple-element.27), channel_id=1, replica_groups=mesh['ya'=2,'yb'=2,'yc'=2,'zl'=2,'core'=2,'za'=2,'zb'=2,'xa'=2,'xb'=2] {..., dimensions={0} | all-to-all | bytes 131072 | tf_op jit(solution)/shard_map/all_to_all | solution.py:280
  50.9 0.7 shard_map.61
  51.6 13.6 %all_to_all.47.parts_ref = bf16[32,24,128]{2,1,0:T(8,128)(2,1)S(1)} all-to-all(bf16[32,24,128]{2,1,0:T(8,128)(2,1)S(1)} %get-tuple-element.31), channel_id=1, replica_groups=mesh['ya'=2,'yb'=2,'yc'=2,'zl'=2,'core'=2,'za'=2,'zb'=2,'xa'=2,'xb'=2] {..., dimensions={0} | all-to-all | bytes 393216 | tf_op jit(solution)/shard_map/all_to_all | solution.py:280
  65.2 0.7 shard_map.62
  65.9 11.8 %all_to_all.48.parts_ref = bf16[16,8,128]{2,1,0:T(8,128)(2,1)S(1)} all-to-all(bf16[16,8,128]{2,1,0:T(8,128)(2,1)S(1)} %get-tuple-element.33), channel_id=1, replica_groups=mesh['ya'=2,'yb'=2,'yc'=2,'zl'=2,'core'=2,'za'=2,'zb'=2,'xa'=2,'xb'=2] {..., dimensions={0} | all-to-all | bytes 65536 | tf_op jit(solution)/shard_map/all_to_all | solution.py:280
  77.8 0.7 shard_map.63
  78.5 12.5 %all_to_all.49.parts_ref = bf16[32,16,128]{2,1,0:T(8,128)(2,1)S(1)} all-to-all(bf16[32,16,128]{2,1,0:T(8,128)(2,1)S(1)} %get-tuple-element.34), channel_id=1, replica_groups=mesh['ya'=2,'yb'=2,'yc'=2,'zl'=2,'core'=2,'za'=2,'zb'=2,'xa'=2,'xb'=2] {..., dimensions={0} | all-to-all | bytes 262144 | tf_op jit(solution)/shard_map/all_to_all | solution.py:280
  90.9 0.7 shard_map.64
  91.6 11.7 %all_to_all.50.parts_ref = bf16[16,8,128]{2,1,0:T(8,128)(2,1)S(1)} all-to-all(bf16[16,8,128]{2,1,0:T(8,128)(2,1)S(1)} %shard_map.64), channel_id=1, replica_groups=mesh['ya'=2,'yb'=2,'yc'=2,'zl'=2,'core'=2,'za'=2,'zb'=2,'xa'=2,'xb'=2] {..., dimensions={0} | all-to-all | bytes 65536 | tf_op jit(solution)/shard_map/all_to_all | solution.py:280
  103.3 0.7 shard_map.65
  104.0 12.4 %all_to_all.51.parts_ref = bf16[32,16,128]{2,1,0:T(8,128)(2,1)S(1)} all-to-all(bf16[32,16,128]{2,1,0:T(8,128)(2,1)S(1)} %get-tuple-element.37), channel_id=1, replica_groups=mesh['ya'=2,'yb'=2,'yc'=2,'zl'=2,'core'=2,'za'=2,'zb'=2,'xa'=2,'xb'=2] {..., dimensions={0} | all-to-all | bytes 262144 | tf_op jit(solution)/shard_map/all_to_all | solution.py:280
  116.4 1.4 shard_map.66
  117.8 3.8 %collective-permute-start.1 = (f32[520,256]{1,0:T(8,128)S(1)}, f32[520,256]{1,0:T(8,128)S(1)}, u32[]{:S(2)}, u32[]{:S(2)}) collective-permute-start(f32[520,256]{1,0:T(8,128)S(1)} %get-tuple-element.42), channel_id=1, source_target_pairs={{0,16},{16,0},{1,17},{17,1},{2,18},{18,2},{3,19},{19,3},{4,20},{20... | collective-permute-start | bytes 1597448 | tf_op jit(solution)/shard_map/ppermute | solution.py:355
  121.7 1.4 shard_map.67.own_ref
  123.1 0.1 collective-permute-done.1.other_ref
  123.2 0.1 shard_map.68
  123.3 13.7 %all_to_all.52.parts_ref = bf16[8,16,1152]{2,1,0:T(8,128)(2,1)S(1)} all-to-all(bf16[8,16,1152]{2,1,0:T(8,128)(2,1)S(1)} %shard_map.68), channel_id=1, replica_groups=mesh['ya'=2,'yb'=2,'yc'=2,'zl'=2,'core'=2,'za'=2,'zb'=2,'xa'=2,'xb'=2] {..., dimensions={0} | all-to-all | bytes 589824 | tf_op jit(solution)/shard_map/all_to_all | solution.py:280
  136.9 0.2 shard_map.69
  137.1 17.0 %all_to_all.53 = bf16[16,64,256]{2,1,0:T(8,128)(2,1)S(1)} all-to-all(bf16[16,64,256]{2,1,0:T(8,128)(2,1)S(1)} %shard_map.69), channel_id=1, replica_groups=mesh['ya'=2,'yb'=2,'yc'=2,'zl'=2,'core'=2,'za'=2,'zb'=2,'xa'=2,'xb'=2] {..., dimensions={0} | all-to-all | bytes 1048576 | tf_op jit(solution)/shard_map/all_to_all | solution.py:280
  154.1 4.8 %collective-permute-start.2 = (bf16[1024,256]{1,0:T(8,128)(2,1)S(1)}, bf16[1024,256]{1,0:T(8,128)(2,1)S(1)}, u32[]{:S(2)}, u32[]{:S(2)}) collective-permute-start(bf16[1024,256]{1,0:T(8,128)(2,1)S(1)} %bitcast.3), channel_id=1, source_target_pairs={{0,16},{16,0},{1,17},{17,1},{2,18},{18,2},{3,19},{19,3},{4,20},{20... | collective-permute-start | bytes 1572872 | tf_op jit(solution)/shard_map/ppermute | solution.py:361
  158.9 0.8 shard_map.70
  159.8 0.7 collective-permute-done.2.x_ref
  160.4 0.8 shard_map.71
Async XLA Ops:
  0.6 29.8 %collective-permute-start = (bf16[1024,256]{1,0:T(8,128)(2,1)}, bf16[1024,256]{1,0:T(8,128)(2,1)S(1)}, u32[]{:S(2)}, u32[]{:S(2)}) collective-permute-start(bf16[1024,256]{1,0:T(8,128)(2,1)} %docs_hbm.1), channel_id=1, source_target_pairs={{0,32},{32,0},{1,33},{33,1},{2,34},{34,2},{3,35},{35,3},{4,36},{36... | collective-permute-start | bytes 1572872 | tf_op jit(solution)/shard_map/ppermute | solution.py:298
  117.8 5.4 %collective-permute-start.1 = (f32[520,256]{1,0:T(8,128)S(1)}, f32[520,256]{1,0:T(8,128)S(1)}, u32[]{:S(2)}, u32[]{:S(2)}) collective-permute-start(f32[520,256]{1,0:T(8,128)S(1)} %get-tuple-element.42), channel_id=1, source_target_pairs={{0,16},{16,0},{1,17},{17,1},{2,18},{18,2},{3,19},{19,3},{4,20},{20... | collective-permute-start | bytes 1597448 | tf_op jit(solution)/shard_map/ppermute | solution.py:355
  154.1 6.3 %collective-permute-start.2 = (bf16[1024,256]{1,0:T(8,128)(2,1)S(1)}, bf16[1024,256]{1,0:T(8,128)(2,1)S(1)}, u32[]{:S(2)}, u32[]{:S(2)}) collective-permute-start(bf16[1024,256]{1,0:T(8,128)(2,1)S(1)} %bitcast.3), channel_id=1, source_target_pairs={{0,16},{16,0},{1,17},{17,1},{2,18},{18,2},{3,19},{19,3},{4,20},{20... | collective-permute-start | bytes 1572872 | tf_op jit(solution)/shard_map/ppermute | solution.py:361

commit v14 on v13

--- a/solution.py
+++ b/solution.py
@@ -94,38 +94,38 @@
 
 def first_columns(
     scale, n_zh, parts_ref, docs_ref, other_ref, cents_ref,
-    out_ref, tile_ref, top_ref, f_ref, docs_all_ref, half_ref,
+    out_ref, tile_ref, top_ref, f_ref, docs_all_ref,
 ):
     zl = lax.axis_index("zl")
     n_doc, n_cent = docs_ref.shape[0], cents_ref.shape[0] // 2
     groups = 2 * n_doc // LANES
     docs_all_ref[pl.ds(pl.multiple_of(zl * n_doc, n_doc), n_doc), :] = docs_ref[...]
     docs_all_ref[pl.ds(pl.multiple_of((1 - zl) * n_doc, n_doc), n_doc), :] = other_ref[...]
-    run = n_cent // 2
-    for q in range(2):
-        rows = pl.ds(pl.multiple_of(q * n_cent + zl * run, run), run)
-        half_ref[q * run : (q + 1) * run, :] = cents_ref[rows, :]
     by_zl = parts_ref[...].reshape(n_zh, 2, parts_ref.shape[0] // (2 * n_zh), 8, LANES)
     for z in range(2):
         parts = by_zl[:, z].reshape(parts_ref.shape[0] // 2, 8, LANES)
         top = jnp.max(parts, axis=0)
         f_ref[z * 8 : (z + 1) * 8, :] = -(top + jnp.log2(jnp.sum(jnp.exp2(parts - top[None]), axis=0)))
 
-    for g in range(groups // 2):
-        f = jnp.concatenate([f_ref[2 * g : 2 * g + 1, :], f_ref[2 * g + 1 : 2 * g + 2, :]], axis=1)
-        docs = docs_all_ref[g * 256 : (g + 1) * 256, :]
-        for q in range(n_cent // 256):
-            cents = half_ref[q * 256 : (q + 1) * 256, :]
-            tile_ref[q * 256 : (q + 1) * 256, g * 256 : (g + 1) * 256] = nt_dot(cents, docs) * scale + f
+    run = n_cent // 2
+    maxima = []
+    for q in range(n_cent // 256):
+        start = (q * 256 // run) * n_cent + q * 256 % run
+        cents = cents_ref[pl.ds(pl.multiple_of(start + zl * run, 256), 256), :]
+        top = None
+        for g in range(groups // 2):
+            f = jnp.concatenate([f_ref[2 * g : 2 * g + 1, :], f_ref[2 * g + 1 : 2 * g + 2, :]], axis=1)
+            s = nt_dot(cents, docs_all_ref[g * 256 : (g + 1) * 256, :]) * scale + f
+            tile_ref[q * 256 : (q + 1) * 256, g * 256 : (g + 1) * 256] = s
+            larger = jnp.maximum(s[:, 0:LANES], s[:, LANES:256])
+            top = larger if top is None else jnp.maximum(top, larger)
+        maxima += [top[0:LANES], top[LANES:256]]
     lane = lane_iota()
     tops = jnp.zeros((LANES, LANES), F32)
     lses = jnp.zeros((LANES, LANES), F32)
     for r in range(n_cent // LANES):
         rows = slice(r * LANES, (r + 1) * LANES)
-        top = tile_ref[rows, 0:LANES]
-        for g in range(1, groups):
-            top = jnp.maximum(top, tile_ref[rows, g * LANES : (g + 1) * LANES])
-        top = jnp.broadcast_to(jnp.max(top, axis=1, keepdims=True), (LANES, LANES))
+        top = jnp.broadcast_to(jnp.max(maxima[r], axis=1, keepdims=True), (LANES, LANES))
         total = jnp.zeros((LANES, LANES), F32)
         for g in range(groups):
             e = jnp.exp2(tile_ref[rows, g * LANES : (g + 1) * LANES] - top)
@@ -321,7 +321,6 @@
             pltpu.VMEM((n_doc, 256), BF16),
         ),
         4,
-        scratch=[pltpu.VMEM((n_cent, 256), BF16)],
         flops=2 * n_doc * n_cent * 256,
     )(parts, docs, other_docs, cents)
 

time: 162 us -> 161 us (level)
  no operation moved by 1% of the time
where the time goes in v14:
time: 161 us
  blocking collectives  131 us (81%)
  Pallas kernels  14.8 us (9%)
  starting transfers between devices  13.4 us (8%)
    all_to_all x9, blocking collectives, exchange(): return lax.all_to_all(x, axes, 0, 0)  131 us
    ppermute x1, starting transfers between devices, per_device(): other_docs = lax.ppermute(docs, 'zl', swap)  4.83 us
    ppermute x1, starting transfers between devices, per_device(): other = lax.ppermute(own, 'core', swap)  4.79 us
    pallas_call x1, Pallas kernels, per_device(): call(functools.partial(first_rows, scale), (shape((row_peers, doc_rows //...  3.83 us
    ppermute x1, starting transfers between devices, per_device(): from_other = lax.ppermute(for_other, 'core', swap)  3.82 us
  transfers between devices with their start and end apart: 3, of which 2 were waited for; matrix products, arithmetic and copies ran while one was open for 0% of the time, Pallas kernels for 4%

profile of v14, /device:TPU:1, one launch (start us, length us, event | category | flops | bytes accessed | tf_op | source)
XLA Modules:
  0.0 160.8 jit_solution(3614547798240774195)
XLA Ops:
  0.6 4.8 %collective-permute-start = (bf16[1024,256]{1,0:T(8,128)(2,1)}, bf16[1024,256]{1,0:T(8,128)(2,1)S(1)}, u32[]{:S(2)}, u32[]{:S(2)}) collective-permute-start(bf16[1024,256]{1,0:T(8,128)(2,1)} %docs_hbm.1), channel_id=1, source_target_pairs={{0,32},{32,0},{1,33},{33,1},{2,34},{34,2},{3,35},{35,3},{4,36},{36... | collective-permute-start | bytes 1572872 | tf_op jit(solution)/shard_map/ppermute | solution.py:298
  5.5 3.8 %shard_map.59 = (f32[32,8,128]{2,1,0:T(8,128)S(1)}, bf16[1024,256]{1,0:T(8,128)(2,1)S(1)}, bf16[2048,256]{1,0:T(8,128)(2,1)S(1)}, f32[8,128]{1,0:T(8,128)S(1)}) custom-call(s32[64]{0:T(128)} %mass_hbm.1, s32[8,128]{1,0:T(8,128)} %bitcast.5, bf16[1024,256]{1,0:T(8,128)(2,1)} %docs_hbm.1, bf16[2048,256]{1,0:T(8,128)(2,1)} %cents_hbm.1), custom_call_target="tpu_custom_call" | custom-call | flops 1073741824 | bytes 1048576 | tf_op jit(solution)/shard_map/pallas_call | solution.py:299
  9.3 21.2 %all_to_all.45.parts_ref = f32[32,8,128]{2,1,0:T(8,128)S(1)} all-to-all(f32[32,8,128]{2,1,0:T(8,128)S(1)} %get-tuple-element.24), channel_id=1, replica_groups=mesh['ya'=2,'yb'=2,'yc'=2,'zl'=2,'core'=2,'za'=2,'zb'=2,'xa'=2,'xb'=2] {..., dimensions={0} | all-to-all | bytes 262144 | tf_op jit(solution)/shard_map/all_to_all | solution.py:280
  30.5 0.0 collective-permute-done.other_ref
  30.5 2.9 %shard_map.60 = (f32[16,8,128]{2,1,0:T(8,128)S(1)}, f32[1024,2048]{1,0:T(8,128)S(1)}, f32[8,128]{1,0:T(8,128)S(1)}, f32[16,128]{1,0:T(8,128)S(1)}, bf16[2048,256]{1,0:T(8,128)(2,1)S(1)}) custom-call(f32[32,8,128]{2,1,0:T(8,128)S(1)} %all_to_all.45.parts_ref, bf16[1024,256]{1,0:T(8,128)(2,1)S(1)} %get-tuple-element.25.docs_ref, ...), custom_call_target="tpu_custom_call" | custom-call | flops 1073741824 | bytes 1048576 | tf_op jit(solution)/shard_map/pallas_call | solution.py:314
  33.3 17.2 %all_to_all.46.parts_ref = f32[16,8,128]{2,1,0:T(8,128)S(1)} all-to-all(f32[16,8,128]{2,1,0:T(8,128)S(1)} %get-tuple-element.27), channel_id=1, replica_groups=mesh['ya'=2,'yb'=2,'yc'=2,'zl'=2,'core'=2,'za'=2,'zb'=2,'xa'=2,'xb'=2] {..., dimensions={0} | all-to-all | bytes 131072 | tf_op jit(solution)/shard_map/all_to_all | solution.py:280
  50.5 0.7 shard_map.61
  51.2 13.6 %all_to_all.47.parts_ref = bf16[32,24,128]{2,1,0:T(8,128)(2,1)S(1)} all-to-all(bf16[32,24,128]{2,1,0:T(8,128)(2,1)S(1)} %get-tuple-element.31), channel_id=1, replica_groups=mesh['ya'=2,'yb'=2,'yc'=2,'zl'=2,'core'=2,'za'=2,'zb'=2,'xa'=2,'xb'=2] {..., dimensions={0} | all-to-all | bytes 393216 | tf_op jit(solution)/shard_map/all_to_all | solution.py:280
  64.8 0.7 shard_map.62
  65.5 11.8 %all_to_all.48.parts_ref = bf16[16,8,128]{2,1,0:T(8,128)(2,1)S(1)} all-to-all(bf16[16,8,128]{2,1,0:T(8,128)(2,1)S(1)} %get-tuple-element.33), channel_id=1, replica_groups=mesh['ya'=2,'yb'=2,'yc'=2,'zl'=2,'core'=2,'za'=2,'zb'=2,'xa'=2,'xb'=2] {..., dimensions={0} | all-to-all | bytes 65536 | tf_op jit(solution)/shard_map/all_to_all | solution.py:280
  77.4 0.7 shard_map.63
  78.1 12.5 %all_to_all.49.parts_ref = bf16[32,16,128]{2,1,0:T(8,128)(2,1)S(1)} all-to-all(bf16[32,16,128]{2,1,0:T(8,128)(2,1)S(1)} %get-tuple-element.34), channel_id=1, replica_groups=mesh['ya'=2,'yb'=2,'yc'=2,'zl'=2,'core'=2,'za'=2,'zb'=2,'xa'=2,'xb'=2] {..., dimensions={0} | all-to-all | bytes 262144 | tf_op jit(solution)/shard_map/all_to_all | solution.py:280
  90.6 0.7 shard_map.64
  91.2 11.7 %all_to_all.50.parts_ref = bf16[16,8,128]{2,1,0:T(8,128)(2,1)S(1)} all-to-all(bf16[16,8,128]{2,1,0:T(8,128)(2,1)S(1)} %shard_map.64), channel_id=1, replica_groups=mesh['ya'=2,'yb'=2,'yc'=2,'zl'=2,'core'=2,'za'=2,'zb'=2,'xa'=2,'xb'=2] {..., dimensions={0} | all-to-all | bytes 65536 | tf_op jit(solution)/shard_map/all_to_all | solution.py:280
  102.9 0.7 shard_map.65
  103.6 12.4 %all_to_all.51.parts_ref = bf16[32,16,128]{2,1,0:T(8,128)(2,1)S(1)} all-to-all(bf16[32,16,128]{2,1,0:T(8,128)(2,1)S(1)} %get-tuple-element.37), channel_id=1, replica_groups=mesh['ya'=2,'yb'=2,'yc'=2,'zl'=2,'core'=2,'za'=2,'zb'=2,'xa'=2,'xb'=2] {..., dimensions={0} | all-to-all | bytes 262144 | tf_op jit(solution)/shard_map/all_to_all | solution.py:280
  116.0 1.4 shard_map.66
  117.4 3.8 %collective-permute-start.1 = (f32[520,256]{1,0:T(8,128)S(1)}, f32[520,256]{1,0:T(8,128)S(1)}, u32[]{:S(2)}, u32[]{:S(2)}) collective-permute-start(f32[520,256]{1,0:T(8,128)S(1)} %get-tuple-element.42), channel_id=1, source_target_pairs={{0,16},{16,0},{1,17},{17,1},{2,18},{18,2},{3,19},{19,3},{4,20},{20... | collective-permute-start | bytes 1597448 | tf_op jit(solution)/shard_map/ppermute | solution.py:354
  121.3 1.4 shard_map.67.own_ref
  122.7 0.1 collective-permute-done.1.other_ref
  122.8 0.1 shard_map.68
  122.9 13.7 %all_to_all.52.parts_ref = bf16[8,16,1152]{2,1,0:T(8,128)(2,1)S(1)} all-to-all(bf16[8,16,1152]{2,1,0:T(8,128)(2,1)S(1)} %shard_map.68), channel_id=1, replica_groups=mesh['ya'=2,'yb'=2,'yc'=2,'zl'=2,'core'=2,'za'=2,'zb'=2,'xa'=2,'xb'=2] {..., dimensions={0} | all-to-all | bytes 589824 | tf_op jit(solution)/shard_map/all_to_all | solution.py:280
  136.5 0.2 shard_map.69
  136.7 17.0 %all_to_all.53 = bf16[16,64,256]{2,1,0:T(8,128)(2,1)S(1)} all-to-all(bf16[16,64,256]{2,1,0:T(8,128)(2,1)S(1)} %shard_map.69), channel_id=1, replica_groups=mesh['ya'=2,'yb'=2,'yc'=2,'zl'=2,'core'=2,'za'=2,'zb'=2,'xa'=2,'xb'=2] {..., dimensions={0} | all-to-all | bytes 1048576 | tf_op jit(solution)/shard_map/all_to_all | solution.py:280
  153.7 4.8 %collective-permute-start.2 = (bf16[1024,256]{1,0:T(8,128)(2,1)S(1)}, bf16[1024,256]{1,0:T(8,128)(2,1)S(1)}, u32[]{:S(2)}, u32[]{:S(2)}) collective-permute-start(bf16[1024,256]{1,0:T(8,128)(2,1)S(1)} %bitcast.3), channel_id=1, source_target_pairs={{0,16},{16,0},{1,17},{17,1},{2,18},{18,2},{3,19},{19,3},{4,20},{20... | collective-permute-start | bytes 1572872 | tf_op jit(solution)/shard_map/ppermute | solution.py:360
  158.5 0.8 shard_map.70
  159.4 0.7 collective-permute-done.2.x_ref
  160.0 0.8 shard_map.71
Async XLA Ops:
  0.6 29.8 %collective-permute-start = (bf16[1024,256]{1,0:T(8,128)(2,1)}, bf16[1024,256]{1,0:T(8,128)(2,1)S(1)}, u32[]{:S(2)}, u32[]{:S(2)}) collective-permute-start(bf16[1024,256]{1,0:T(8,128)(2,1)} %docs_hbm.1), channel_id=1, source_target_pairs={{0,32},{32,0},{1,33},{33,1},{2,34},{34,2},{3,35},{35,3},{4,36},{36... | collective-permute-start | bytes 1572872 | tf_op jit(solution)/shard_map/ppermute | solution.py:298
  117.4 5.4 %collective-permute-start.1 = (f32[520,256]{1,0:T(8,128)S(1)}, f32[520,256]{1,0:T(8,128)S(1)}, u32[]{:S(2)}, u32[]{:S(2)}) collective-permute-start(f32[520,256]{1,0:T(8,128)S(1)} %get-tuple-element.42), channel_id=1, source_target_pairs={{0,16},{16,0},{1,17},{17,1},{2,18},{18,2},{3,19},{19,3},{4,20},{20... | collective-permute-start | bytes 1597448 | tf_op jit(solution)/shard_map/ppermute | solution.py:354
  153.7 6.3 %collective-permute-start.2 = (bf16[1024,256]{1,0:T(8,128)(2,1)S(1)}, bf16[1024,256]{1,0:T(8,128)(2,1)S(1)}, u32[]{:S(2)}, u32[]{:S(2)}) collective-permute-start(bf16[1024,256]{1,0:T(8,128)(2,1)S(1)} %bitcast.3), channel_id=1, source_target_pairs={{0,16},{16,0},{1,17},{17,1},{2,18},{18,2},{3,19},{19,3},{4,20},{20... | collective-permute-start | bytes 1572872 | tf_op jit(solution)/shard_map/ppermute | solution.py:360

commit v15 on v14

--- a/solution.py
+++ b/solution.py
@@ -195,13 +195,13 @@
     n_half, n_doc = p_ref.shape
     groups = n_doc // LANES
     blocks = n_half // LANES
-    cols = to_columns(c_ref[pl.ds(side * blocks, blocks), :])
+    c = c_ref[pl.ds(side * blocks, blocks), :]
     base = pl.multiple_of(side * n_half, n_half)
     lane = lane_iota()
     masses = jnp.zeros((LANES, LANES), F32)
     for r in range(blocks):
         rows = pl.ds(pl.multiple_of(base + r * LANES, LANES), LANES)
-        col = jnp.broadcast_to(cols[:, r : r + 1], (LANES, LANES))
+        col = jnp.broadcast_to(c[r : r + 1, :], (LANES, LANES)).T
         total = jnp.zeros((LANES, LANES), F32)
         for g in range(groups):
             lanes = slice(g * LANES, (g + 1) * LANES)

time: 161 us -> 161 us (level)
  no operation moved by 1% of the time
where the time goes in v15:
time: 161 us
  blocking collectives  131 us (81%)
  Pallas kernels  14.6 us (9%)
  starting transfers between devices  13.4 us (8%)
    all_to_all x9, blocking collectives, exchange(): return lax.all_to_all(x, axes, 0, 0)  131 us
    ppermute x1, starting transfers between devices, per_device(): other_docs = lax.ppermute(docs, 'zl', swap)  4.83 us
    ppermute x1, starting transfers between devices, per_device(): other = lax.ppermute(own, 'core', swap)  4.79 us
    pallas_call x1, Pallas kernels, per_device(): call(functools.partial(first_rows, scale), (shape((row_peers, doc_rows //...  3.83 us
    ppermute x1, starting transfers between devices, per_device(): from_other = lax.ppermute(for_other, 'core', swap)  3.82 us
  transfers between devices with their start and end apart: 3, of which 2 were waited for; matrix products, arithmetic and copies ran while one was open for 0% of the time, Pallas kernels for 4%

profile of v15, /device:TPU:1, one launch (start us, length us, event | category | flops | bytes accessed | tf_op | source)
XLA Modules:
  0.0 160.8 jit_solution(726162831264148033)
XLA Ops:
  0.6 4.8 %collective-permute-start = (bf16[1024,256]{1,0:T(8,128)(2,1)}, bf16[1024,256]{1,0:T(8,128)(2,1)S(1)}, u32[]{:S(2)}, u32[]{:S(2)}) collective-permute-start(bf16[1024,256]{1,0:T(8,128)(2,1)} %docs_hbm.1), channel_id=1, source_target_pairs={{0,32},{32,0},{1,33},{33,1},{2,34},{34,2},{3,35},{35,3},{4,36},{36... | collective-permute-start | bytes 1572872 | tf_op jit(solution)/shard_map/ppermute | solution.py:298
  5.5 3.8 %shard_map.59 = (f32[32,8,128]{2,1,0:T(8,128)S(1)}, bf16[1024,256]{1,0:T(8,128)(2,1)S(1)}, bf16[2048,256]{1,0:T(8,128)(2,1)S(1)}, f32[8,128]{1,0:T(8,128)S(1)}) custom-call(s32[64]{0:T(128)} %mass_hbm.1, s32[8,128]{1,0:T(8,128)} %bitcast.5, bf16[1024,256]{1,0:T(8,128)(2,1)} %docs_hbm.1, bf16[2048,256]{1,0:T(8,128)(2,1)} %cents_hbm.1), custom_call_target="tpu_custom_call" | custom-call | flops 1073741824 | bytes 1048576 | tf_op jit(solution)/shard_map/pallas_call | solution.py:299
  9.3 21.2 %all_to_all.45.parts_ref = f32[32,8,128]{2,1,0:T(8,128)S(1)} all-to-all(f32[32,8,128]{2,1,0:T(8,128)S(1)} %get-tuple-element.24), channel_id=1, replica_groups=mesh['ya'=2,'yb'=2,'yc'=2,'zl'=2,'core'=2,'za'=2,'zb'=2,'xa'=2,'xb'=2] {..., dimensions={0} | all-to-all | bytes 262144 | tf_op jit(solution)/shard_map/all_to_all | solution.py:280
  30.5 0.0 collective-permute-done.other_ref
  30.5 2.9 %shard_map.60 = (f32[16,8,128]{2,1,0:T(8,128)S(1)}, f32[1024,2048]{1,0:T(8,128)S(1)}, f32[8,128]{1,0:T(8,128)S(1)}, f32[16,128]{1,0:T(8,128)S(1)}, bf16[2048,256]{1,0:T(8,128)(2,1)S(1)}) custom-call(f32[32,8,128]{2,1,0:T(8,128)S(1)} %all_to_all.45.parts_ref, bf16[1024,256]{1,0:T(8,128)(2,1)S(1)} %get-tuple-element.25.docs_ref, ...), custom_call_target="tpu_custom_call" | custom-call | flops 1073741824 | bytes 1048576 | tf_op jit(solution)/shard_map/pallas_call | solution.py:314
  33.3 17.2 %all_to_all.46.parts_ref = f32[16,8,128]{2,1,0:T(8,128)S(1)} all-to-all(f32[16,8,128]{2,1,0:T(8,128)S(1)} %get-tuple-element.27), channel_id=1, replica_groups=mesh['ya'=2,'yb'=2,'yc'=2,'zl'=2,'core'=2,'za'=2,'zb'=2,'xa'=2,'xb'=2] {..., dimensions={0} | all-to-all | bytes 131072 | tf_op jit(solution)/shard_map/all_to_all | solution.py:280
  50.5 0.7 shard_map.61
  51.2 13.6 %all_to_all.47.parts_ref = bf16[32,24,128]{2,1,0:T(8,128)(2,1)S(1)} all-to-all(bf16[32,24,128]{2,1,0:T(8,128)(2,1)S(1)} %get-tuple-element.31), channel_id=1, replica_groups=mesh['ya'=2,'yb'=2,'yc'=2,'zl'=2,'core'=2,'za'=2,'zb'=2,'xa'=2,'xb'=2] {..., dimensions={0} | all-to-all | bytes 393216 | tf_op jit(solution)/shard_map/all_to_all | solution.py:280
  64.8 0.7 shard_map.62
  65.5 11.8 %all_to_all.48.parts_ref = bf16[16,8,128]{2,1,0:T(8,128)(2,1)S(1)} all-to-all(bf16[16,8,128]{2,1,0:T(8,128)(2,1)S(1)} %get-tuple-element.33), channel_id=1, replica_groups=mesh['ya'=2,'yb'=2,'yc'=2,'zl'=2,'core'=2,'za'=2,'zb'=2,'xa'=2,'xb'=2] {..., dimensions={0} | all-to-all | bytes 65536 | tf_op jit(solution)/shard_map/all_to_all | solution.py:280
  77.4 0.7 shard_map.63
  78.1 12.5 %all_to_all.49.parts_ref = bf16[32,16,128]{2,1,0:T(8,128)(2,1)S(1)} all-to-all(bf16[32,16,128]{2,1,0:T(8,128)(2,1)S(1)} %get-tuple-element.34), channel_id=1, replica_groups=mesh['ya'=2,'yb'=2,'yc'=2,'zl'=2,'core'=2,'za'=2,'zb'=2,'xa'=2,'xb'=2] {..., dimensions={0} | all-to-all | bytes 262144 | tf_op jit(solution)/shard_map/all_to_all | solution.py:280
  90.6 0.7 shard_map.64
  91.2 11.7 %all_to_all.50.parts_ref = bf16[16,8,128]{2,1,0:T(8,128)(2,1)S(1)} all-to-all(bf16[16,8,128]{2,1,0:T(8,128)(2,1)S(1)} %shard_map.64), channel_id=1, replica_groups=mesh['ya'=2,'yb'=2,'yc'=2,'zl'=2,'core'=2,'za'=2,'zb'=2,'xa'=2,'xb'=2] {..., dimensions={0} | all-to-all | bytes 65536 | tf_op jit(solution)/shard_map/all_to_all | solution.py:280
  102.9 0.7 shard_map.65
  103.6 12.4 %all_to_all.51.parts_ref = bf16[32,16,128]{2,1,0:T(8,128)(2,1)S(1)} all-to-all(bf16[32,16,128]{2,1,0:T(8,128)(2,1)S(1)} %get-tuple-element.37), channel_id=1, replica_groups=mesh['ya'=2,'yb'=2,'yc'=2,'zl'=2,'core'=2,'za'=2,'zb'=2,'xa'=2,'xb'=2] {..., dimensions={0} | all-to-all | bytes 262144 | tf_op jit(solution)/shard_map/all_to_all | solution.py:280
  116.0 1.3 shard_map.66
  117.4 3.8 %collective-permute-start.1 = (f32[520,256]{1,0:T(8,128)S(1)}, f32[520,256]{1,0:T(8,128)S(1)}, u32[]{:S(2)}, u32[]{:S(2)}) collective-permute-start(f32[520,256]{1,0:T(8,128)S(1)} %get-tuple-element.42), channel_id=1, source_target_pairs={{0,16},{16,0},{1,17},{17,1},{2,18},{18,2},{3,19},{19,3},{4,20},{20... | collective-permute-start | bytes 1597448 | tf_op jit(solution)/shard_map/ppermute | solution.py:354
  121.2 1.3 shard_map.67.own_ref
  122.5 0.2 collective-permute-done.1.other_ref
  122.7 0.1 shard_map.68
  122.8 13.7 %all_to_all.52.parts_ref = bf16[8,16,1152]{2,1,0:T(8,128)(2,1)S(1)} all-to-all(bf16[8,16,1152]{2,1,0:T(8,128)(2,1)S(1)} %shard_map.68), channel_id=1, replica_groups=mesh['ya'=2,'yb'=2,'yc'=2,'zl'=2,'core'=2,'za'=2,'zb'=2,'xa'=2,'xb'=2] {..., dimensions={0} | all-to-all | bytes 589824 | tf_op jit(solution)/shard_map/all_to_all | solution.py:280
  136.5 0.2 shard_map.69
  136.6 17.0 %all_to_all.53 = bf16[16,64,256]{2,1,0:T(8,128)(2,1)S(1)} all-to-all(bf16[16,64,256]{2,1,0:T(8,128)(2,1)S(1)} %shard_map.69), channel_id=1, replica_groups=mesh['ya'=2,'yb'=2,'yc'=2,'zl'=2,'core'=2,'za'=2,'zb'=2,'xa'=2,'xb'=2] {..., dimensions={0} | all-to-all | bytes 1048576 | tf_op jit(solution)/shard_map/all_to_all | solution.py:280
  153.7 4.8 %collective-permute-start.2 = (bf16[1024,256]{1,0:T(8,128)(2,1)S(1)}, bf16[1024,256]{1,0:T(8,128)(2,1)S(1)}, u32[]{:S(2)}, u32[]{:S(2)}) collective-permute-start(bf16[1024,256]{1,0:T(8,128)(2,1)S(1)} %bitcast.3), channel_id=1, source_target_pairs={{0,16},{16,0},{1,17},{17,1},{2,18},{18,2},{3,19},{19,3},{4,20},{20... | collective-permute-start | bytes 1572872 | tf_op jit(solution)/shard_map/ppermute | solution.py:360
  158.5 0.8 shard_map.70
  159.3 0.7 collective-permute-done.2.x_ref
  160.0 0.8 shard_map.71
Async XLA Ops:
  0.6 29.8 %collective-permute-start = (bf16[1024,256]{1,0:T(8,128)(2,1)}, bf16[1024,256]{1,0:T(8,128)(2,1)S(1)}, u32[]{:S(2)}, u32[]{:S(2)}) collective-permute-start(bf16[1024,256]{1,0:T(8,128)(2,1)} %docs_hbm.1), channel_id=1, source_target_pairs={{0,32},{32,0},{1,33},{33,1},{2,34},{34,2},{3,35},{35,3},{4,36},{36... | collective-permute-start | bytes 1572872 | tf_op jit(solution)/shard_map/ppermute | solution.py:298
  117.4 5.4 %collective-permute-start.1 = (f32[520,256]{1,0:T(8,128)S(1)}, f32[520,256]{1,0:T(8,128)S(1)}, u32[]{:S(2)}, u32[]{:S(2)}) collective-permute-start(f32[520,256]{1,0:T(8,128)S(1)} %get-tuple-element.42), channel_id=1, source_target_pairs={{0,16},{16,0},{1,17},{17,1},{2,18},{18,2},{3,19},{19,3},{4,20},{20... | collective-permute-start | bytes 1597448 | tf_op jit(solution)/shard_map/ppermute | solution.py:354
  153.7 6.3 %collective-permute-start.2 = (bf16[1024,256]{1,0:T(8,128)(2,1)S(1)}, bf16[1024,256]{1,0:T(8,128)(2,1)S(1)}, u32[]{:S(2)}, u32[]{:S(2)}) collective-permute-start(bf16[1024,256]{1,0:T(8,128)(2,1)S(1)} %bitcast.3), channel_id=1, source_target_pairs={{0,16},{16,0},{1,17},{17,1},{2,18},{18,2},{3,19},{19,3},{4,20},{20... | collective-permute-start | bytes 1572872 | tf_op jit(solution)/shard_map/ppermute | solution.py:360
